TPU v7x, 256 devices: a whole 4x4x8 slice. The times are simulated.
256 devices in a mesh: mod: 8 (over x_lo, y), blk: 32 (over z, x_hi, core).
Axes of the slice: x: 4 (x_hi: 2, x_lo: 2; x = x_hi * 2 + x_lo), y: 4, z: 8, core: 2. Of those that a mesh axis runs over, the one named last changes fastest.
Arguments:
- train_grads: float32 [8, 20480, 4096], P('mod', 'blk'), may hold values from -6 to 6
- left_factor: float32 [8, 64, 64], P('mod'), may hold values from -0.75 to 0.75
- right_factor: float32 [8, 64, 64], P('mod'), may hold values from -0.75 to 0.75
- queries: float32 [8, 1024, 4096], P('mod', 'blk'), may hold values from -0.03125 to 0.03125
- owners: int32 [32], replicated, may hold values from 0 to 31, each once
- range_start: int32 [32], replicated, may hold values from 0 to 10240
Outputs:
- scores: float32 [1024, 20480], P('mod', 'blk')
Inputs may be any that keep to these rules, and one draw needn't show every extreme that they name: owners is a permutation of the 32 block numbers.
All inputs are finite; a program needn't handle non-finite values.
Results may differ from a plain program's by a relative error of at most 0.0001.
Values sent between devices are 32-bit elements; how exact they have to be, the bound alone decides.
No kernel may reach another device: no remote copies, remote signals or barrier semaphores. Data moves between devices by JAX's collectives and lax.ppermute only.
A program may use at most 128 MiB of HBM per device.

v0:
```python
import functools

import jax
import jax.numpy as jnp
from jax import lax
from jax.experimental import pallas as pl
from jax.experimental.pallas import tpu as pltpu
from jax.sharding import PartitionSpec as P

NZ = 8
NY = 4
FEAT_STEP = 1024
VMEM_LIMIT = 16 * 1024 * 1024


def blk_pairs(move):
    return [
        (z * 4 + h * 2 + c, move(z, h, c))
        for z in range(NZ)
        for h in range(2)
        for c in range(2)
    ]


Z_UP = blk_pairs(lambda z, h, c: (z + 1) % NZ * 4 + h * 2 + c)
Z_DOWN = blk_pairs(lambda z, h, c: (z - 1) % NZ * 4 + h * 2 + c)
X_FAR = blk_pairs(lambda z, h, c: z * 4 + (1 - h) * 2 + c)
CORE = blk_pairs(lambda z, h, c: z * 4 + h * 2 + 1 - c)
Y_GROUPS = [[x * 4 + y for y in range(NY)] for x in range(2)]


def up(block):
    return lax.ppermute(block, "blk", Z_UP)


def down(block):
    return lax.ppermute(block, "blk", Z_DOWN)


def far(block):
    return lax.ppermute(block, "blk", X_FAR)


def other(block):
    return lax.ppermute(block, "blk", CORE)


def split(value):
    high = value.astype(jnp.bfloat16)
    low = (value - high.astype(jnp.float32)).astype(jnp.bfloat16)
    return high, low


def nt(a, b):
    return lax.dot_general(a, b, (((1,), (1,)), ((), ())), preferred_element_type=jnp.float32)


def split_kernel(g_ref, hi_ref, lo_ref, sq_ref):
    rows = g_ref.shape[0]
    here = pl.ds(pl.multiple_of(pl.program_id(0) * rows, rows), rows)
    g = g_ref[...]
    hi_ref[here, :], lo_ref[here, :] = split(g)
    sq_ref[here, :] = jnp.broadcast_to(jnp.sum(g * g, axis=1, keepdims=True), (rows, 128))


def split_grads(grads):
    rows, feat = grads.shape
    whole = pl.BlockSpec(memory_space=pltpu.VMEM)
    return pl.pallas_call(
        split_kernel,
        grid=(rows // 128,),
        in_specs=[pl.BlockSpec((128, feat), lambda i: (i, 0))],
        out_specs=[whole, whole, whole],
        out_shape=[
            pltpu.VMEM((rows, feat), jnp.bfloat16),
            pltpu.VMEM((rows, feat), jnp.bfloat16),
            pltpu.VMEM((rows, 128), jnp.float32),
        ],
        compiler_params=pltpu.CompilerParams(vmem_limit_bytes=VMEM_LIMIT),
    )(pltpu.with_memory_space_constraint(grads, pltpu.HBM))


def score_kernel(spans, squares, hi_ref, lo_ref, *refs):
    if squares:
        sq_ref, *refs = refs
    pieces = refs[: len(spans)]
    out_ref, acc = refs[len(spans) :]
    rows, feat = hi_ref.shape
    for start in range(0, feat, FEAT_STEP):
        part = slice(start, start + FEAT_STEP)
        q = jnp.concatenate([p[a:b, part] for p, (a, b) in zip(pieces, spans)], axis=0)
        qhi, qlo = split(q)
        ghi, glo = hi_ref[:, part], lo_ref[:, part]
        value = nt(ghi, qhi) + (nt(ghi, qlo) + nt(glo, qhi))
        if start == 0:
            acc[...] = value
        else:
            acc[...] += value
    count = rows // NY
    for k in range(NY):
        here = slice(k * count, (k + 1) * count)
        out_ref[k, 0:count, :] = acc[here, :]
        if squares:
            out_ref[k, count:, :] = jnp.zeros((8, out_ref.shape[2]), jnp.float32)
            out_ref[k, count:, 0:count] = jnp.transpose(sq_ref[here, 0:8])


def scores_of(grads, pieces, squares=None):
    hi, lo = (pltpu.with_memory_space_constraint(g, pltpu.VMEM) for g in grads)
    rows = hi.shape[0]
    spans = [(first, first + count) for _, first, count in pieces]
    width = sum(count for _, _, count in pieces)
    slice_rows = rows // NY + (0 if squares is None else 8)
    whole = pl.BlockSpec(memory_space=pltpu.VMEM)
    extra = [] if squares is None else [squares]
    flops = 6 * rows * width * hi.shape[1]
    return pl.pallas_call(
        functools.partial(score_kernel, spans, squares is not None),
        in_specs=[whole] * (2 + len(extra) + len(pieces)),
        out_specs=whole,
        out_shape=jax.ShapeDtypeStruct((NY, slice_rows, width), jnp.float32),
        scratch_shapes=[pltpu.VMEM((rows, width), jnp.float32)],
        compiler_params=pltpu.CompilerParams(vmem_limit_bytes=VMEM_LIMIT),
        cost_estimate=pl.CostEstimate(flops=flops, bytes_accessed=4 * 1024 * 1024, transcendentals=0),
    )(hi, lo, *extra, *[p[0] for p in pieces])


def over_y(slices):
    return lax.all_to_all(slices, "mod", 0, 0, axis_index_groups=Y_GROUPS)


def pack_kernel(plans, *refs):
    blocks, outs = refs[: -len(plans)], refs[-len(plans) :]
    for out, plan in zip(outs, plans):
        at = 0
        for which, first, count in plan:
            out[at : at + count, :] = blocks[which][first : first + count, :]
            at += count


def pack(blocks, *plans):
    whole = pl.BlockSpec(memory_space=pltpu.VMEM)
    return pl.pallas_call(
        functools.partial(pack_kernel, plans),
        in_specs=[whole] * len(blocks),
        out_specs=[whole] * len(plans),
        out_shape=[
            jax.ShapeDtypeStruct((sum(p[2] for p in plan), blocks[0].shape[1]), jnp.float32)
            for plan in plans
        ],
        compiler_params=pltpu.CompilerParams(vmem_limit_bytes=VMEM_LIMIT),
    )(*blocks)


def place_kernel(dest_ref, *refs):
    *parts, out_ref = refs
    sums = [p[0] + p[1] + (p[2] + p[3]) for p in parts]
    count = parts[-1].shape[1]
    total = jnp.concatenate([v[:count] for v in sums], axis=1)
    high = total.astype(jnp.bfloat16)
    rest = total - high.astype(jnp.float32)
    mid = rest.astype(jnp.bfloat16)
    low = (rest - mid.astype(jnp.float32)).astype(jnp.bfloat16)
    stacked = jnp.concatenate([high, mid, low], axis=0)
    squares = sums[0][count:, :]
    row = lax.broadcasted_iota(jnp.int32, (8, 128), 0)
    tail = jnp.where(row == 0, squares[:, 0:128], squares[:, 128:256])
    nq = dest_ref.shape[0]
    lane = lax.broadcasted_iota(jnp.int32, (nq, 256), 1)
    for first in range(0, nq, 256):
        pick = jnp.where(dest_ref[...] == lane + first, 1.0, 0.0).astype(jnp.bfloat16)
        moved = jnp.dot(stacked, pick, preferred_element_type=jnp.float32)
        moved = moved[:count] + (moved[count : 2 * count] + moved[2 * count :])
        for k in range(2):
            out_ref[first // 128 + k, 0:count, :] = moved[:, k * 128 : (k + 1) * 128]
            out_ref[first // 128 + k, count:, :] = tail


def place(dest, parts):
    whole = pl.BlockSpec(memory_space=pltpu.VMEM)
    nq = dest.shape[0]
    return pl.pallas_call(
        place_kernel,
        in_specs=[whole] * (1 + len(parts)),
        out_specs=whole,
        out_shape=jax.ShapeDtypeStruct((nq // 128, parts[0].shape[1], 128), jnp.float32),
        compiler_params=pltpu.CompilerParams(vmem_limit_bytes=VMEM_LIMIT),
    )(dest[:, None], *parts)


def finish_kernel(window, terms, base_ref, first_ref, got_ref, out_ref):
    rows = got_ref.shape[1] - 8
    both = [got_ref[k] + got_ref[NY + k] for k in range(NY)]
    values = jnp.transpose(jnp.concatenate([v[:rows] for v in both], axis=0))
    squares = jnp.concatenate(
        [w for v in both for w in (v[rows : rows + 1, :], v[rows + 1 : rows + 2, : rows - 128])],
        axis=1,
    )
    scale = lax.rsqrt(squares / terms + 1e-06)
    ids = base_ref[0] + lax.broadcasted_iota(jnp.int32, values.shape, 1)
    first = first_ref[...]
    inside = (ids >= first) & (ids < first + window)
    out_ref[...] = jnp.where(inside, values * scale, 0.0)


def finish(base, first, got, window, terms):
    whole = pl.BlockSpec(memory_space=pltpu.VMEM)
    return pl.pallas_call(
        functools.partial(finish_kernel, window, terms),
        in_specs=[pl.BlockSpec(memory_space=pltpu.SMEM), whole, whole],
        out_specs=whole,
        out_shape=jax.ShapeDtypeStruct((got.shape[2], NY * (got.shape[1] - 8)), jnp.float32),
        compiler_params=pltpu.CompilerParams(vmem_limit_bytes=VMEM_LIMIT),
    )(base, first[:, None], got)


def fence(*arrays):
    return lax.optimization_barrier(arrays)


def shards(train_grads, left_factor, right_factor, queries, owners, range_start):
    highest = lax.Precision.HIGHEST
    nmods = lax.axis_size("mod")
    nblk = lax.axis_size("blk")
    rows_dev = train_grads.shape[1]
    feat = train_grads.shape[2]
    side = left_factor.shape[1]
    qblock = queries.shape[1]
    half = qblock // 2
    window = rows_dev * nblk // 2
    grads = train_grads[0]
    m = lax.axis_index("mod")
    b = lax.axis_index("blk")
    z, h, c = b // 4, (b // 2) % 2, b % 2

    mats = queries[0].reshape(qblock, side, side)
    mats = jnp.einsum("rad,cd->rac", mats, right_factor[0], precision=highest)
    mats = jnp.einsum("ba,rac->rbc", left_factor[0], mats, precision=highest)
    own = mats.reshape(qblock, feat)

    own, grads = fence(own, grads)
    halves = []

    def ids(*named):
        for flip in range(2):
            for d, col, *ps in named:
                where = (z + d) % NZ * 4 + (h + col) % 2 * 2 + (c + flip) % 2
                halves.extend(where * 2 + p for p in (ps or (0, 1)))

    size = qblock
    a1m, a1p, e0 = up(own), down(own), far(own)
    a1m, a1p = fence(a1m, a1p)
    a2m, a2p, e1p = up(a1m), down(a1p), far(a1p)
    hi, lo, squares = split_grads(grads)
    a2m, a2p, e0, hi, lo, squares = fence(a2m, a2p, e0, hi, lo, squares)
    a3m, a3p, e1m = up(a2m), down(a2p), far(a1m)
    (near,) = pack([own, a1m, a1p, e0, a2m, a2p], [(k, 0, size) for k in range(6)])
    near_c = other(near)
    ids((0, 0), (-1, 0), (1, 0), (0, 1), (-2, 0), (2, 0))
    part0 = scores_of((hi, lo), [(near, 0, 6 * size), (near_c, 0, 6 * size)], squares)
    a3m, a3p, e1m, e1p, part0 = fence(a3m, a3p, e1m, e1p, part0)
    for_up, for_down, for_far, three = pack(
        [a3m, a3p, e1m, e1p],
        [(0, 0, half), (2, 0, half)],
        [(1, half, half), (3, 0, half)],
        [(1, half, half), (0, half, half)],
        [(k, 0, size) for k in range(4)],
    )
    up4, down4, far4 = up(for_up), down(for_down), far(for_far)
    three_c, part0 = fence(other(three), part0)
    got0 = over_y(part0)
    ids((-3, 0), (3, 0), (-1, 1), (1, 1))
    part1 = scores_of((hi, lo), [(three, 0, 4 * size), (three_c, 0, 4 * size)])
    up4, down4, far4, part1 = fence(up4, down4, far4, part1)
    for_up, for_down, for_far, four = pack(
        [up4, down4, far4, e1m, e1p],
        [(3, half, half), (0, half, half)],
        [(4, half, half), (1, half, half)],
        [(0, 0, half), (1, 0, half)],
        [(k, 0, size) for k in range(3)],
    )
    up5, down5, far5 = up(for_up), down(for_down), far(for_far)
    four_c, part1 = fence(other(four), part1)
    got1 = over_y(part1)
    ids((4, 0, 0), (-2, 1, 0), (4, 0, 1), (2, 1, 0))
    part2 = scores_of((hi, lo), [(four, 0, 2 * size), (four_c, 0, 2 * size)])
    up5, down5, far5, part2, got0 = fence(up5, down5, far5, part2, got0)
    (five,) = pack([up5, down5, far5], [(k, 0, size) for k in range(3)])
    five_c = other(five)
    got2 = over_y(part2)
    ids((3, 1, 1), (-3, 1, 1), (-2, 1, 1), (-3, 1, 0), (2, 1, 1), (3, 1, 0), (4, 1, 0), (4, 1, 1))
    part3 = scores_of(
        (hi, lo),
        [(four, 2 * size, size), (five, 0, 3 * size), (four_c, 2 * size, size), (five_c, 0, 3 * size)],
    )
    part3, got1 = fence(part3, got1)
    got3 = over_y(part3)

    source = jnp.stack(halves).astype(jnp.int32)
    blocks = jnp.arange(nblk, dtype=jnp.int32)
    target = jnp.sum(jnp.where((source // 2)[:, None] == blocks[None, :], owners[None, :], 0), axis=1)
    dest = ((target * 2 + source % 2) * half)[:, None] + jnp.arange(half, dtype=jnp.int32)[None, :]
    dest = dest.reshape(-1)
    placed = place(dest, [got0, got1, got2, got3])
    got = lax.all_to_all(placed, "mod", 0, 0)
    out_block = m * (nblk // nmods) + jnp.arange(placed.shape[2], dtype=jnp.int32) // qblock
    first = jnp.sum(jnp.where(out_block[:, None] == blocks[None, :], range_start[None, :], 0), axis=1)
    base = jnp.reshape(b * rows_dev, (1,)).astype(jnp.int32)
    return finish(base, first, got, window, nmods * feat)


def solution(mesh):
    in_specs = (
        P("mod", "blk", None),
        P("mod", None, None),
        P("mod", None, None),
        P("mod", "blk", None),
        P(),
        P(),
    )
    out_specs = P("mod", "blk")
    return jax.shard_map(shards, mesh=mesh, in_specs=in_specs, out_specs=out_specs, check_vma=False)
```

profile of v0, /device:TPU:2, one launch (start us, length us, event | category | flops | bytes accessed | tf_op | source)
XLA Modules:
  0.0 183.0 jit_solution(3238000668750785838)
XLA Ops:
  1.5 3.1 %fusion.1 = f32[32,64,64]{1,2,0:T(8,128)S(1)} fusion(f32[32,64,64]{2,1,0:T(8,128)S(1)} %reshape_squeeze.3, f32[1,64,64]{2,1,0:T(8,128)S(1)} %copy-done), kind=kOutput, calls=%fused_computation.2 | convolution fusion | flops 100663296 | bytes 1064960 | tf_op jit(solution)/shard_map/rad,cd->rac/dot_general | solution.py:237
  6.3 2.0 %collective-permute-start = (f32[32,4096]{1,0:T(8,128)S(1)}, f32[32,4096]{1,0:T(8,128)S(1)}, u32[]{:S(2)}, u32[]{:S(2)}) collective-permute-start(f32[32,4096]{1,0:T(8,128)S(1)} %reshape.3020.refs_0_), channel_id=1, source_target_pairs={{0,4},{1,5},{2,6},{3,7},{4,8},{5,9},{6,10},{7,11},{8,12},{9,13},{1... | collective-permute-start | bytes 1572872 | tf_op jit(solution)/shard_map/ppermute | solution.py:33
  8.3 4.0 %collective-permute-start.1 = (f32[32,4096]{1,0:T(8,128)S(1)}, f32[32,4096]{1,0:T(8,128)S(1)}, u32[]{:S(2)}, u32[]{:S(2)}) collective-permute-start(f32[32,4096]{1,0:T(8,128)S(1)} %reshape.3020.refs_0_), channel_id=1, source_target_pairs={{0,28},{1,29},{2,30},{3,31},{4,0},{5,1},{6,2},{7,3},{8,4},{9,5},{1... | collective-permute-start | bytes 1572872 | tf_op jit(solution)/shard_map/ppermute | solution.py:37
  12.3 2.1 %collective-permute-start.4 = (f32[32,4096]{1,0:T(8,128)S(1)}, f32[32,4096]{1,0:T(8,128)S(1)}, u32[]{:S(2)}, u32[]{:S(2)}) collective-permute-start(f32[32,4096]{1,0:T(8,128)S(1)} %reshape.3020.refs_0_), channel_id=1, source_target_pairs={{0,2},{1,3},{2,0},{3,1},{4,6},{5,7},{6,4},{7,5},{8,10},{9,11},{10,... | collective-permute-start | bytes 1572872 | tf_op jit(solution)/shard_map/ppermute | solution.py:41
  14.4 9.7 %collective-permute-done.refs_1_ = f32[32,4096]{1,0:T(8,128)S(1)} collective-permute-done((f32[32,4096]{1,0:T(8,128)S(1)}, f32[32,4096]{1,0:T(8,128)S(1)}, u32[]{:S(2)}, u32[]{:S(2)}) %collective-permute-start) | collective-permute-done | bytes 524320 | tf_op jit(solution)/shard_map/ppermute | solution.py:33
  24.1 3.2 %collective-permute-start.3 = (f32[32,4096]{1,0:T(8,128)S(1)}, f32[32,4096]{1,0:T(8,128)S(1)}, u32[]{:S(2)}, u32[]{:S(2)}) collective-permute-start(f32[32,4096]{1,0:T(8,128)S(1)} %collective-permute-done.1.refs_2_), channel_id=1, source_target_pairs={{0,28},{1,29},{2,30},{3,31},{4,0},{5,1},{6,2},{7,3},{8,4},{9,5},{1... | collective-permute-start | bytes 1572872 | tf_op jit(solution)/shard_map/ppermute | solution.py:37
  27.4 6.8 %shard_map.64 = (bf16[640,4096]{1,0:T(8,128)(2,1)S(1)}, bf16[640,4096]{1,0:T(8,128)(2,1)S(1)}, f32[640,128]{1,0:T(8,128)S(1)}) custom-call(f32[640,4096]{1,0:T(8,128)} %bitcast.79), custom_call_target="tpu_custom_call" | custom-call | tf_op jit(solution)/shard_map/pallas_call | solution.py:69
  34.3 4.2 %collective-permute-done.2.refs_4_ = f32[32,4096]{1,0:T(8,128)S(1)} collective-permute-done((f32[32,4096]{1,0:T(8,128)S(1)}, f32[32,4096]{1,0:T(8,128)S(1)}, u32[]{:S(2)}, u32[]{:S(2)}) %collective-permute-start.2) | collective-permute-done | bytes 524320 | tf_op jit(solution)/shard_map/ppermute | solution.py:33
  39.8 2.2 %collective-permute-start.7 = (f32[32,4096]{1,0:T(8,128)S(1)}, f32[32,4096]{1,0:T(8,128)S(1)}, u32[]{:S(2)}, u32[]{:S(2)}) collective-permute-start(f32[32,4096]{1,0:T(8,128)S(1)} %collective-permute-done.refs_1_), channel_id=1, source_target_pairs={{0,2},{1,3},{2,0},{3,1},{4,6},{5,7},{6,4},{7,5},{8,10},{9,11},{10,... | collective-permute-start | bytes 1572872 | tf_op jit(solution)/shard_map/ppermute | solution.py:41
  46.7 8.3 %shard_map.66 = f32[4,168,384]{2,1,0:T(8,128)S(1)} custom-call(bf16[640,4096]{1,0:T(8,128)(2,1)S(1)} %get-tuple-element.55.hi_ref, bf16[640,4096]{1,0:T(8,128)(2,1)S(1)} %get-tuple-element.56.lo_ref, f32[640,128]{1,0:T(8,128)S(1)} %get-tuple-element.57.refs_0_, f32[192,4096]{1,0:T(8,128)S(1)} %shard_map.65.refs_1_, ...), custom_call_target="tpu_custom_call" | custom-call | flops 6039797760 | bytes 4194304 | tf_op jit(solution)/shard_map/pallas_call | solution.py:117
  56.1 10.8 %collective-permute-done.8.refs_3_.refs_4_ = f32[32,4096]{1,0:T(8,128)S(1)} collective-permute-done((f32[32,4096]{1,0:T(8,128)S(1)}, f32[32,4096]{1,0:T(8,128)S(1)}, u32[]{:S(2)}, u32[]{:S(2)}) %collective-permute-start.8) | collective-permute-done | bytes 524320 | tf_op jit(solution)/shard_map/ppermute | solution.py:41
  70.6 2.1 %collective-permute-start.12 = (f32[32,4096]{1,0:T(8,128)S(1)}, f32[32,4096]{1,0:T(8,128)S(1)}, u32[]{:S(2)}, u32[]{:S(2)}) collective-permute-start(f32[32,4096]{1,0:T(8,128)S(1)} %get-tuple-element.65), channel_id=1, source_target_pairs={{0,2},{1,3},{2,0},{3,1},{4,6},{5,7},{6,4},{7,5},{8,10},{9,11},{10,... | collective-permute-start | bytes 1572872 | tf_op jit(solution)/shard_map/ppermute | solution.py:41
  72.7 4.3 %shard_map.68 = f32[4,160,256]{2,1,0:T(8,128)S(1)} custom-call(bf16[640,4096]{1,0:T(8,128)(2,1)S(1)} %get-tuple-element.55.hi_ref, bf16[640,4096]{1,0:T(8,128)(2,1)S(1)} %get-tuple-element.56.lo_ref, f32[128,4096]{1,0:T(8,128)S(1)} %get-tuple-element.66.refs_0_, f32[128,4096]{1,0:T(8,128)S(1)} %collective-permute-done.13.refs_1_), custom_call_target="tpu_custom_call" | custom-call | flops 4026531840 | bytes 4194304 | tf_op jit(solution)/shard_map/pallas_call | solution.py:117
  77.8 5.0 %collective-permute-done.10.refs_0_ = f32[32,4096]{1,0:T(8,128)S(1)} collective-permute-done((f32[32,4096]{1,0:T(8,128)S(1)}, f32[32,4096]{1,0:T(8,128)S(1)}, u32[]{:S(2)}, u32[]{:S(2)}) %collective-permute-start.10) | collective-permute-done | bytes 524320 | tf_op jit(solution)/shard_map/ppermute | solution.py:33
  83.1 2.6 %collective-permute-done.12.refs_2_ = f32[32,4096]{1,0:T(8,128)S(1)} collective-permute-done((f32[32,4096]{1,0:T(8,128)S(1)}, f32[32,4096]{1,0:T(8,128)S(1)}, u32[]{:S(2)}, u32[]{:S(2)}) %collective-permute-start.12) | collective-permute-done | bytes 524320 | tf_op jit(solution)/shard_map/ppermute | solution.py:41
  88.4 4.5 %all-to-all-start = ((f32[4,168,384]{2,1,0:T(8,128)}), f32[4,168,384]{2,1,0:T(8,128)}, u32[]{:S(2)}, u32[]{:S(2)}) async-start(f32[4,168,384]{2,1,0:T(8,128)} %copy-done.16), calls=%async_computation | async-start | bytes 2064384 | tf_op jit(solution)/shard_map/all_to_all | solution.py:129
  93.5 2.6 %collective-permute-start.15 = (f32[32,4096]{1,0:T(8,128)}, f32[32,4096]{1,0:T(8,128)S(1)}, u32[]{:S(2)}, u32[]{:S(2)}) collective-permute-start(f32[32,4096]{1,0:T(8,128)} %copy-done.24), channel_id=1, source_target_pairs={{0,28},{1,29},{2,30},{3,31},{4,0},{5,1},{6,2},{7,3},{8,4},{9,5},{1... | collective-permute-start | bytes 1572872 | tf_op jit(solution)/shard_map/ppermute | solution.py:37
  96.1 2.1 %collective-permute-start.16 = (f32[32,4096]{1,0:T(8,128)}, f32[32,4096]{1,0:T(8,128)S(1)}, u32[]{:S(2)}, u32[]{:S(2)}) collective-permute-start(f32[32,4096]{1,0:T(8,128)} %copy-done.23), channel_id=1, source_target_pairs={{0,2},{1,3},{2,0},{3,1},{4,6},{5,7},{6,4},{7,5},{8,10},{9,11},{10,... | collective-permute-start | bytes 1572872 | tf_op jit(solution)/shard_map/ppermute | solution.py:41
  98.2 2.5 %copy-done.2 = bf16[640,4096]{1,0:T(8,128)(2,1)S(1)} copy-done((bf16[640,4096]{1,0:T(8,128)(2,1)S(1)}, bf16[640,4096]{1,0:T(8,128)(2,1)}, u32[]{:S(2)}) %copy-start.2) | copy-done | bytes 5242904
  100.7 2.5 %copy-done.5 = bf16[640,4096]{1,0:T(8,128)(2,1)S(1)} copy-done((bf16[640,4096]{1,0:T(8,128)(2,1)S(1)}, bf16[640,4096]{1,0:T(8,128)(2,1)}, u32[]{:S(2)}) %copy-start.5) | copy-done | bytes 5242904
  103.2 4.9 %shard_map.70 = f32[4,160,128]{2,1,0:T(8,128)} custom-call(bf16[640,4096]{1,0:T(8,128)(2,1)S(1)} %copy-done.2, bf16[640,4096]{1,0:T(8,128)(2,1)S(1)} %copy-done.5, f32[96,4096]{1,0:T(8,128)S(1)} %get-tuple-element.75.refs_0_, f32[96,4096]{1,0:T(8,128)S(1)} %collective-permute-done.17.refs_1_.refs_2_), custom_call_target="tpu_custom_call" | custom-call | flops 2013265920 | bytes 4194304 | tf_op jit(solution)/shard_map/pallas_call | solution.py:117
  115.5 4.5 %all-to-all-start.1 = ((f32[4,160,256]{2,1,0:T(8,128)}), f32[4,160,256]{2,1,0:T(8,128)}, u32[]{:S(2)}, u32[]{:S(2)}) async-start(f32[4,160,256]{2,1,0:T(8,128)} %copy-done.12), calls=%async_computation.1 | async-start | bytes 1310720 | tf_op jit(solution)/shard_map/all_to_all | solution.py:129
  120.2 11.5 %all-to-all-done.1.refs_1_ = f32[4,160,256]{2,1,0:T(8,128)} async-done(((f32[4,160,256]{2,1,0:T(8,128)}), f32[4,160,256]{2,1,0:T(8,128)}, u32[]{:S(2)}, u32[]{:S(2)}) %all-to-all-start.1) | async-done | bytes 655392 | tf_op jit(solution)/shard_map/all_to_all | solution.py:129
  131.7 3.7 %all-to-all-start.2 = ((f32[4,160,128]{2,1,0:T(8,128)}), f32[4,160,128]{2,1,0:T(8,128)S(1)}, u32[]{:S(2)}, u32[]{:S(2)}) async-start(f32[4,160,128]{2,1,0:T(8,128)} %shard_map.70), calls=%async_computation.2 | async-start | bytes 655360 | tf_op jit(solution)/shard_map/all_to_all | solution.py:129
  135.4 2.5 %copy-done.3 = bf16[640,4096]{1,0:T(8,128)(2,1)S(1)} copy-done((bf16[640,4096]{1,0:T(8,128)(2,1)S(1)}, bf16[640,4096]{1,0:T(8,128)(2,1)}, u32[]{:S(2)}) %copy-start.3) | copy-done | bytes 5242904
  137.9 2.5 %copy-done.6 = bf16[640,4096]{1,0:T(8,128)(2,1)S(1)} copy-done((bf16[640,4096]{1,0:T(8,128)(2,1)S(1)}, bf16[640,4096]{1,0:T(8,128)(2,1)}, u32[]{:S(2)}) %copy-start.6) | copy-done | bytes 5242904
  141.8 5.7 %shard_map.72 = f32[4,160,256]{2,1,0:T(8,128)S(1)} custom-call(bf16[640,4096]{1,0:T(8,128)(2,1)S(1)} %copy-done.3, bf16[640,4096]{1,0:T(8,128)(2,1)S(1)} %copy-done.6, f32[96,4096]{1,0:T(8,128)S(1)} %get-tuple-element.75.refs_0_, f32[96,4096]{1,0:T(8,128)S(1)} %shard_map.71.refs_1_, f32[96,4096]{1,0:T(8,128)S(1)} %copy-done.8, ...), custom_call_target="tpu_custom_call" | custom-call | flops 4026531840 | bytes 4194304 | tf_op jit(solution)/shard_map/pallas_call | solution.py:117
  148.3 4.5 %all-to-all-start.3 = ((f32[4,160,256]{2,1,0:T(8,128)}), f32[4,160,256]{2,1,0:T(8,128)S(1)}, u32[]{:S(2)}, u32[]{:S(2)}) async-start(f32[4,160,256]{2,1,0:T(8,128)} %copy-done.9), calls=%async_computation.3 | async-start | bytes 1310720 | tf_op jit(solution)/shard_map/all_to_all | solution.py:129
  154.1 8.9 %all-to-all-done.3.refs_3_ = f32[4,160,256]{2,1,0:T(8,128)S(1)} async-done(((f32[4,160,256]{2,1,0:T(8,128)}), f32[4,160,256]{2,1,0:T(8,128)S(1)}, u32[]{:S(2)}, u32[]{:S(2)}) %all-to-all-start.3) | async-done | bytes 655392 | tf_op jit(solution)/shard_map/all_to_all | solution.py:129
  166.0 3.6 %shard_map.73 = f32[8,168,128]{2,1,0:T(8,128)} custom-call(s32[1024,1]{1,0:T(8,128)S(1)} %copy-done.15, f32[4,168,384]{2,1,0:T(8,128)} %all-to-all-done.refs_0_, f32[4,160,256]{2,1,0:T(8,128)} %all-to-all-done.1.refs_1_, f32[4,160,128]{2,1,0:T(8,128)S(1)} %all-to-all-done.2.refs_2_, f32[4,160,256]{2,1,0:T(8,128)S(1)} %copy-done.11), custom_call_target="tpu_custom_call" | custom-call | tf_op jit(solution)/shard_map/pallas_call | solution.py:182
  169.6 4.0 %all-to-all-start.4 = ((f32[8,168,128]{2,1,0:T(8,128)}), f32[8,168,128]{2,1,0:T(8,128)S(1)}, u32[]{:S(2)}, u32[]{:S(2)}) async-start(f32[8,168,128]{2,1,0:T(8,128)} %shard_map.73), calls=%async_computation.4 | async-start | bytes 1376256 | tf_op jit(solution)/shard_map/all_to_all | solution.py:305
  173.8 8.2 %all-to-all-done.4.got_ref = f32[8,168,128]{2,1,0:T(8,128)S(1)} async-done(((f32[8,168,128]{2,1,0:T(8,128)}), f32[8,168,128]{2,1,0:T(8,128)S(1)}, u32[]{:S(2)}, u32[]{:S(2)}) %all-to-all-start.4) | async-done | bytes 688160 | tf_op jit(solution)/shard_map/all_to_all | solution.py:305
  (99 shorter events, 33.6 us)
Async XLA Ops:
  0.0 4.6 %copy-start.26 = (f32[1,64,64]{2,1,0:T(8,128)S(1)}, f32[1,64,64]{2,1,0:T(8,128)}, u32[]{:S(2)}) copy-start(f32[1,64,64]{2,1,0:T(8,128)} %param.7) | copy-start | bytes 49156
  6.3 28.0 %copy-start.13 = (f32[32,4096]{1,0:T(8,128)}, f32[32,4096]{1,0:T(8,128)S(1)}, u32[]{:S(2)}) copy-start(f32[32,4096]{1,0:T(8,128)S(1)} %reshape.3020.refs_0_) | copy-start | bytes 1572868
  6.3 17.9 %collective-permute-start = (f32[32,4096]{1,0:T(8,128)S(1)}, f32[32,4096]{1,0:T(8,128)S(1)}, u32[]{:S(2)}, u32[]{:S(2)}) collective-permute-start(f32[32,4096]{1,0:T(8,128)S(1)} %reshape.3020.refs_0_), channel_id=1, source_target_pairs={{0,4},{1,5},{2,6},{3,7},{4,8},{5,9},{6,10},{7,11},{8,12},{9,13},{1... | collective-permute-start | bytes 1572872 | tf_op jit(solution)/shard_map/ppermute | solution.py:33
  8.3 15.9 %collective-permute-start.1 = (f32[32,4096]{1,0:T(8,128)S(1)}, f32[32,4096]{1,0:T(8,128)S(1)}, u32[]{:S(2)}, u32[]{:S(2)}) collective-permute-start(f32[32,4096]{1,0:T(8,128)S(1)} %reshape.3020.refs_0_), channel_id=1, source_target_pairs={{0,28},{1,29},{2,30},{3,31},{4,0},{5,1},{6,2},{7,3},{8,4},{9,5},{1... | collective-permute-start | bytes 1572872 | tf_op jit(solution)/shard_map/ppermute | solution.py:37
  12.3 21.9 %collective-permute-start.4 = (f32[32,4096]{1,0:T(8,128)S(1)}, f32[32,4096]{1,0:T(8,128)S(1)}, u32[]{:S(2)}, u32[]{:S(2)}) collective-permute-start(f32[32,4096]{1,0:T(8,128)S(1)} %reshape.3020.refs_0_), channel_id=1, source_target_pairs={{0,2},{1,3},{2,0},{3,1},{4,6},{5,7},{6,4},{7,5},{8,10},{9,11},{10,... | collective-permute-start | bytes 1572872 | tf_op jit(solution)/shard_map/ppermute | solution.py:41
  24.1 14.3 %collective-permute-start.2 = (f32[32,4096]{1,0:T(8,128)S(1)}, f32[32,4096]{1,0:T(8,128)S(1)}, u32[]{:S(2)}, u32[]{:S(2)}) collective-permute-start(f32[32,4096]{1,0:T(8,128)S(1)} %collective-permute-done.refs_1_), channel_id=1, source_target_pairs={{0,4},{1,5},{2,6},{3,7},{4,8},{5,9},{6,10},{7,11},{8,12},{9,13},{1... | collective-permute-start | bytes 1572872 | tf_op jit(solution)/shard_map/ppermute | solution.py:33
  24.1 14.3 %collective-permute-start.3 = (f32[32,4096]{1,0:T(8,128)S(1)}, f32[32,4096]{1,0:T(8,128)S(1)}, u32[]{:S(2)}, u32[]{:S(2)}) collective-permute-start(f32[32,4096]{1,0:T(8,128)S(1)} %collective-permute-done.1.refs_2_), channel_id=1, source_target_pairs={{0,28},{1,29},{2,30},{3,31},{4,0},{5,1},{6,2},{7,3},{8,4},{9,5},{1... | collective-permute-start | bytes 1572872 | tf_op jit(solution)/shard_map/ppermute | solution.py:37
  34.2 38.5 %copy-start.1 = (bf16[640,4096]{1,0:T(8,128)(2,1)}, bf16[640,4096]{1,0:T(8,128)(2,1)S(1)}, u32[]{:S(2)}) copy-start(bf16[640,4096]{1,0:T(8,128)(2,1)S(1)} %get-tuple-element.55.hi_ref) | copy-start | bytes 15728644
  34.2 38.5 %copy-start.4 = (bf16[640,4096]{1,0:T(8,128)(2,1)}, bf16[640,4096]{1,0:T(8,128)(2,1)S(1)}, u32[]{:S(2)}) copy-start(bf16[640,4096]{1,0:T(8,128)(2,1)S(1)} %get-tuple-element.56.lo_ref) | copy-start | bytes 15728644
  39.7 7.0 %collective-permute-start.9 = (f32[192,4096]{1,0:T(8,128)S(1)}, f32[192,4096]{1,0:T(8,128)S(1)}, u32[]{:S(2)}, u32[]{:S(2)}) collective-permute-start(f32[192,4096]{1,0:T(8,128)S(1)} %shard_map.65.refs_1_), channel_id=1, source_target_pairs={{0,1},{1,0},{2,3},{3,2},{4,5},{5,4},{6,7},{7,6},{8,9},{9,8},{10,11... | collective-permute-start | bytes 9437192 | tf_op jit(solution)/shard_map/ppermute | solution.py:45
  39.8 16.3 %collective-permute-start.7 = (f32[32,4096]{1,0:T(8,128)S(1)}, f32[32,4096]{1,0:T(8,128)S(1)}, u32[]{:S(2)}, u32[]{:S(2)}) collective-permute-start(f32[32,4096]{1,0:T(8,128)S(1)} %collective-permute-done.refs_1_), channel_id=1, source_target_pairs={{0,2},{1,3},{2,0},{3,1},{4,6},{5,7},{6,4},{7,5},{8,10},{9,11},{10,... | collective-permute-start | bytes 1572872 | tf_op jit(solution)/shard_map/ppermute | solution.py:41
  42.0 24.9 %collective-permute-start.8 = (f32[32,4096]{1,0:T(8,128)S(1)}, f32[32,4096]{1,0:T(8,128)S(1)}, u32[]{:S(2)}, u32[]{:S(2)}) collective-permute-start(f32[32,4096]{1,0:T(8,128)S(1)} %collective-permute-done.1.refs_2_), channel_id=1, source_target_pairs={{0,2},{1,3},{2,0},{3,1},{4,6},{5,7},{6,4},{7,5},{8,10},{9,11},{10,... | collective-permute-start | bytes 1572872 | tf_op jit(solution)/shard_map/ppermute | solution.py:41
  43.4 23.5 %collective-permute-start.5 = (f32[32,4096]{1,0:T(8,128)S(1)}, f32[32,4096]{1,0:T(8,128)S(1)}, u32[]{:S(2)}, u32[]{:S(2)}) collective-permute-start(f32[32,4096]{1,0:T(8,128)S(1)} %collective-permute-done.2.refs_4_), channel_id=1, source_target_pairs={{0,4},{1,5},{2,6},{3,7},{4,8},{5,9},{6,10},{7,11},{8,12},{9,13},{1... | collective-permute-start | bytes 1572872 | tf_op jit(solution)/shard_map/ppermute | solution.py:33
  45.2 21.6 %collective-permute-start.6 = (f32[32,4096]{1,0:T(8,128)S(1)}, f32[32,4096]{1,0:T(8,128)S(1)}, u32[]{:S(2)}, u32[]{:S(2)}) collective-permute-start(f32[32,4096]{1,0:T(8,128)S(1)} %collective-permute-done.3.refs_5_), channel_id=1, source_target_pairs={{0,28},{1,29},{2,30},{3,31},{4,0},{5,1},{6,2},{7,3},{8,4},{9,5},{1... | collective-permute-start | bytes 1572872 | tf_op jit(solution)/shard_map/ppermute | solution.py:37
  67.1 5.6 %collective-permute-start.13 = (f32[128,4096]{1,0:T(8,128)S(1)}, f32[128,4096]{1,0:T(8,128)S(1)}, u32[]{:S(2)}, u32[]{:S(2)}) collective-permute-start(f32[128,4096]{1,0:T(8,128)S(1)} %get-tuple-element.66.refs_0_), channel_id=1, source_target_pairs={{0,1},{1,0},{2,3},{3,2},{4,5},{5,4},{6,7},{7,6},{8,9},{9,8},{10,11... | collective-permute-start | bytes 6291464 | tf_op jit(solution)/shard_map/ppermute | solution.py:45
  67.2 15.6 %collective-permute-start.10 = (f32[32,4096]{1,0:T(8,128)S(1)}, f32[32,4096]{1,0:T(8,128)S(1)}, u32[]{:S(2)}, u32[]{:S(2)}) collective-permute-start(f32[32,4096]{1,0:T(8,128)S(1)} %get-tuple-element.63), channel_id=1, source_target_pairs={{0,4},{1,5},{2,6},{3,7},{4,8},{5,9},{6,10},{7,11},{8,12},{9,13},{1... | collective-permute-start | bytes 1572872 | tf_op jit(solution)/shard_map/ppermute | solution.py:33
  69.1 14.0 %collective-permute-start.11 = (f32[32,4096]{1,0:T(8,128)S(1)}, f32[32,4096]{1,0:T(8,128)S(1)}, u32[]{:S(2)}, u32[]{:S(2)}) collective-permute-start(f32[32,4096]{1,0:T(8,128)S(1)} %get-tuple-element.64), channel_id=1, source_target_pairs={{0,28},{1,29},{2,30},{3,31},{4,0},{5,1},{6,2},{7,3},{8,4},{9,5},{1... | collective-permute-start | bytes 1572872 | tf_op jit(solution)/shard_map/ppermute | solution.py:37
  70.6 15.2 %collective-permute-start.12 = (f32[32,4096]{1,0:T(8,128)S(1)}, f32[32,4096]{1,0:T(8,128)S(1)}, u32[]{:S(2)}, u32[]{:S(2)}) collective-permute-start(f32[32,4096]{1,0:T(8,128)S(1)} %get-tuple-element.65), channel_id=1, source_target_pairs={{0,2},{1,3},{2,0},{3,1},{4,6},{5,7},{6,4},{7,5},{8,10},{9,11},{10,... | collective-permute-start | bytes 1572872 | tf_op jit(solution)/shard_map/ppermute | solution.py:41
  88.4 9.8 %collective-permute-start.17 = (f32[96,4096]{1,0:T(8,128)S(1)}, f32[96,4096]{1,0:T(8,128)S(1)}, u32[]{:S(2)}, u32[]{:S(2)}) collective-permute-start(f32[96,4096]{1,0:T(8,128)S(1)} %get-tuple-element.75.refs_0_), channel_id=1, source_target_pairs={{0,1},{1,0},{2,3},{3,2},{4,5},{5,4},{6,7},{7,6},{8,9},{9,8},{10,11... | collective-permute-start | bytes 4718600 | tf_op jit(solution)/shard_map/ppermute | solution.py:45
  88.4 23.8 %all-to-all-start = ((f32[4,168,384]{2,1,0:T(8,128)}), f32[4,168,384]{2,1,0:T(8,128)}, u32[]{:S(2)}, u32[]{:S(2)}) async-start(f32[4,168,384]{2,1,0:T(8,128)} %copy-done.16), calls=%async_computation | async-start | bytes 2064384 | tf_op jit(solution)/shard_map/all_to_all | solution.py:129
  92.8 15.6 %collective-permute-start.14 = (f32[32,4096]{1,0:T(8,128)}, f32[32,4096]{1,0:T(8,128)S(1)}, u32[]{:S(2)}, u32[]{:S(2)}) collective-permute-start(f32[32,4096]{1,0:T(8,128)} %copy-done.25), channel_id=1, source_target_pairs={{0,4},{1,5},{2,6},{3,7},{4,8},{5,9},{6,10},{7,11},{8,12},{9,13},{1... | collective-permute-start | bytes 1572872 | tf_op jit(solution)/shard_map/ppermute | solution.py:33
  93.5 15.8 %collective-permute-start.15 = (f32[32,4096]{1,0:T(8,128)}, f32[32,4096]{1,0:T(8,128)S(1)}, u32[]{:S(2)}, u32[]{:S(2)}) collective-permute-start(f32[32,4096]{1,0:T(8,128)} %copy-done.24), channel_id=1, source_target_pairs={{0,28},{1,29},{2,30},{3,31},{4,0},{5,1},{6,2},{7,3},{8,4},{9,5},{1... | collective-permute-start | bytes 1572872 | tf_op jit(solution)/shard_map/ppermute | solution.py:37
  96.1 15.3 %collective-permute-start.16 = (f32[32,4096]{1,0:T(8,128)}, f32[32,4096]{1,0:T(8,128)S(1)}, u32[]{:S(2)}, u32[]{:S(2)}) collective-permute-start(f32[32,4096]{1,0:T(8,128)} %copy-done.23), channel_id=1, source_target_pairs={{0,2},{1,3},{2,0},{3,1},{4,6},{5,7},{6,4},{7,5},{8,10},{9,11},{10,... | collective-permute-start | bytes 1572872 | tf_op jit(solution)/shard_map/ppermute | solution.py:41
  103.2 4.9 %copy-start.7 = (f32[96,4096]{1,0:T(8,128)}, f32[96,4096]{1,0:T(8,128)S(1)}, u32[]{:S(2)}) copy-start(f32[96,4096]{1,0:T(8,128)S(1)} %collective-permute-done.17.refs_1_.refs_2_) | copy-start | bytes 4718596
  115.4 19.9 %collective-permute-start.18 = (f32[96,4096]{1,0:T(8,128)S(1)}, f32[96,4096]{1,0:T(8,128)}, u32[]{:S(2)}, u32[]{:S(2)}) collective-permute-start(f32[96,4096]{1,0:T(8,128)S(1)} %shard_map.71.refs_1_), channel_id=1, source_target_pairs={{0,1},{1,0},{2,3},{3,2},{4,5},{5,4},{6,7},{7,6},{8,9},{9,8},{10,11... | collective-permute-start | bytes 4718600 | tf_op jit(solution)/shard_map/ppermute | solution.py:45
  115.5 16.1 %all-to-all-start.1 = ((f32[4,160,256]{2,1,0:T(8,128)}), f32[4,160,256]{2,1,0:T(8,128)}, u32[]{:S(2)}, u32[]{:S(2)}) async-start(f32[4,160,256]{2,1,0:T(8,128)} %copy-done.12), calls=%async_computation.1 | async-start | bytes 1310720 | tf_op jit(solution)/shard_map/all_to_all | solution.py:129
  131.7 16.7 %all-to-all-start.2 = ((f32[4,160,128]{2,1,0:T(8,128)}), f32[4,160,128]{2,1,0:T(8,128)S(1)}, u32[]{:S(2)}, u32[]{:S(2)}) async-start(f32[4,160,128]{2,1,0:T(8,128)} %shard_map.70), calls=%async_computation.2 | async-start | bytes 655360 | tf_op jit(solution)/shard_map/all_to_all | solution.py:129
  135.4 2.5 %copy-start.3 = (bf16[640,4096]{1,0:T(8,128)(2,1)S(1)}, bf16[640,4096]{1,0:T(8,128)(2,1)}, u32[]{:S(2)}) copy-start(bf16[640,4096]{1,0:T(8,128)(2,1)} %copy-done.1) | copy-start | bytes 15728644
  141.8 11.0 %copy-start.27 = (s32[32]{0:T(128)S(1)}, s32[32]{0:T(128)}, u32[]{:S(2)}) copy-start(s32[32]{0:T(128)} %param.10) | copy-start | bytes 388
  148.3 14.6 %all-to-all-start.3 = ((f32[4,160,256]{2,1,0:T(8,128)}), f32[4,160,256]{2,1,0:T(8,128)S(1)}, u32[]{:S(2)}, u32[]{:S(2)}) async-start(f32[4,160,256]{2,1,0:T(8,128)} %copy-done.9), calls=%async_computation.3 | async-start | bytes 1310720 | tf_op jit(solution)/shard_map/all_to_all | solution.py:129
  166.0 7.6 %copy-start.28 = (s32[32]{0:T(128)S(1)}, s32[32]{0:T(128)}, u32[]{:S(2)}) copy-start(s32[32]{0:T(128)} %param.11) | copy-start | bytes 388
  169.6 12.4 %all-to-all-start.4 = ((f32[8,168,128]{2,1,0:T(8,128)}), f32[8,168,128]{2,1,0:T(8,128)S(1)}, u32[]{:S(2)}, u32[]{:S(2)}) async-start(f32[8,168,128]{2,1,0:T(8,128)} %shard_map.73), calls=%async_computation.4 | async-start | bytes 1376256 | tf_op jit(solution)/shard_map/all_to_all | solution.py:305
  (21 other events, 25.1 us)
where the time goes:
time: 184 us; the launch traced here: 183 us
  waiting for transfers between devices  63 us (34%)
  starting transfers between devices  50.5 us (27%)
  Pallas kernels  35.3 us (19%)
  local copies, waits for them, and re-layouts  29.6 us (16%)
  matrix products  4.07 us (2%)
    unnamed x58, local copies, waits for them, and re-layouts  26.1 us
    pallas_call x4, Pallas kernels, scores_of(): pl.pallas_call(functools.partial(score_kernel, spans, squares is not None...  23.1 us
    all_to_all x4, waiting for transfers between devices, over_y(): return lax.all_to_all(slices, 'mod', 0, 0, axis_index_groups=Y_GROUPS)  20.3 us
    ppermute x5, waiting for transfers between devices, up(): return lax.ppermute(block, 'blk', Z_UP)  19.2 us
    all_to_all x4, starting transfers between devices, over_y(): return lax.all_to_all(slices, 'mod', 0, 0, axis_index_groups=Y_GROUPS)  17.2 us
    ppermute x5, waiting for transfers between devices, far(): return lax.ppermute(block, 'blk', X_FAR)  14.9 us
    ppermute x5, starting transfers between devices, down(): return lax.ppermute(block, 'blk', Z_DOWN)  12.7 us
    ppermute x5, starting transfers between devices, far(): return lax.ppermute(block, 'blk', X_FAR)  10 us
  transfers between devices with their start and end apart: 24, of which 12 were waited for; matrix products, arithmetic and copies ran while one was open for 1% of the time, Pallas kernels for 16%

commit v1 on v0

--- a/solution.py
+++ b/solution.py
@@ -9,7 +9,7 @@
 
 NZ = 8
 NY = 4
-FEAT_STEP = 1024
+FEAT_STEP = 512
 VMEM_LIMIT = 16 * 1024 * 1024
 
 
@@ -56,25 +56,27 @@
 
 
 def split_kernel(g_ref, hi_ref, lo_ref, sq_ref):
-    rows = g_ref.shape[0]
-    here = pl.ds(pl.multiple_of(pl.program_id(0) * rows, rows), rows)
     g = g_ref[...]
-    hi_ref[here, :], lo_ref[here, :] = split(g)
-    sq_ref[here, :] = jnp.broadcast_to(jnp.sum(g * g, axis=1, keepdims=True), (rows, 128))
+    high, low = split(g)
+    for k in range(hi_ref.shape[0]):
+        part = slice(k * FEAT_STEP, (k + 1) * FEAT_STEP)
+        hi_ref[k], lo_ref[k] = high[:, part], low[:, part]
+    sq_ref[...] = jnp.broadcast_to(jnp.sum(g * g, axis=1, keepdims=True), sq_ref.shape)
 
 
 def split_grads(grads):
     rows, feat = grads.shape
-    whole = pl.BlockSpec(memory_space=pltpu.VMEM)
+    steps = feat // FEAT_STEP
+    piece = pl.BlockSpec((steps, 64, FEAT_STEP), lambda i: (0, i, 0))
     return pl.pallas_call(
         split_kernel,
-        grid=(rows // 128,),
-        in_specs=[pl.BlockSpec((128, feat), lambda i: (i, 0))],
-        out_specs=[whole, whole, whole],
+        grid=(rows // 64,),
+        in_specs=[pl.BlockSpec((64, feat), lambda i: (i, 0))],
+        out_specs=[piece, piece, pl.BlockSpec((64, 128), lambda i: (i, 0))],
         out_shape=[
-            pltpu.VMEM((rows, feat), jnp.bfloat16),
-            pltpu.VMEM((rows, feat), jnp.bfloat16),
-            pltpu.VMEM((rows, 128), jnp.float32),
+            pltpu.HBM((steps, rows, FEAT_STEP), jnp.bfloat16),
+            pltpu.HBM((steps, rows, FEAT_STEP), jnp.bfloat16),
+            jax.ShapeDtypeStruct((rows, 128), jnp.float32),
         ],
         compiler_params=pltpu.CompilerParams(vmem_limit_bytes=VMEM_LIMIT),
     )(pltpu.with_memory_space_constraint(grads, pltpu.HBM))
@@ -85,17 +87,28 @@
         sq_ref, *refs = refs
     pieces = refs[: len(spans)]
     out_ref, acc = refs[len(spans) :]
-    rows, feat = hi_ref.shape
-    for start in range(0, feat, FEAT_STEP):
-        part = slice(start, start + FEAT_STEP)
-        q = jnp.concatenate([p[a:b, part] for p, (a, b) in zip(pieces, spans)], axis=0)
-        qhi, qlo = split(q)
-        ghi, glo = hi_ref[:, part], lo_ref[:, part]
-        value = nt(ghi, qhi) + (nt(ghi, qlo) + nt(glo, qhi))
-        if start == 0:
-            acc[...] = value
-        else:
-            acc[...] += value
+    step = pl.program_id(0)
+    rows = acc.shape[0]
+    q = jnp.concatenate([p[a:b, :] for p, (a, b) in zip(pieces, spans)], axis=0)
+    qhi, qlo = split(q)
+    ghi, glo = hi_ref[0], lo_ref[0]
+    value = nt(ghi, qhi) + (nt(ghi, qlo) + nt(glo, qhi))
+
+    @pl.when(step == 0)
+    def _():
+        acc[...] = value
+
+    @pl.when(step > 0)
+    def _():
+        acc[...] += value
+
+    @pl.when(step == pl.num_programs(0) - 1)
+    def _():
+        emit(squares, sq_ref if squares else None, acc, out_ref)
+
+
+def emit(squares, sq_ref, acc, out_ref):
+    rows = acc.shape[0]
     count = rows // NY
     for k in range(NY):
         here = slice(k * count, (k + 1) * count)
@@ -106,17 +119,20 @@
 
 
 def scores_of(grads, pieces, squares=None):
-    hi, lo = (pltpu.with_memory_space_constraint(g, pltpu.VMEM) for g in grads)
-    rows = hi.shape[0]
+    hi, lo = (pltpu.with_memory_space_constraint(g, pltpu.HBM) for g in grads)
+    steps, rows, wide = hi.shape
     spans = [(first, first + count) for _, first, count in pieces]
     width = sum(count for _, _, count in pieces)
     slice_rows = rows // NY + (0 if squares is None else 8)
     whole = pl.BlockSpec(memory_space=pltpu.VMEM)
     extra = [] if squares is None else [squares]
-    flops = 6 * rows * width * hi.shape[1]
+    flops = 6 * rows * width * steps * wide
     return pl.pallas_call(
         functools.partial(score_kernel, spans, squares is not None),
-        in_specs=[whole] * (2 + len(extra) + len(pieces)),
+        grid=(steps,),
+        in_specs=[pl.BlockSpec((1, rows, wide), lambda i: (i, 0, 0))] * 2
+        + [whole] * len(extra)
+        + [pl.BlockSpec((p[0].shape[0], wide), lambda i: (0, i)) for p in pieces],
         out_specs=whole,
         out_shape=jax.ShapeDtypeStruct((NY, slice_rows, width), jnp.float32),
         scratch_shapes=[pltpu.VMEM((rows, width), jnp.float32)],
@@ -252,13 +268,13 @@
     a1m, a1p = fence(a1m, a1p)
     a2m, a2p, e1p = up(a1m), down(a1p), far(a1p)
     hi, lo, squares = split_grads(grads)
-    a2m, a2p, e0, hi, lo, squares = fence(a2m, a2p, e0, hi, lo, squares)
+    a2m, a2p, e0, e1p, squares = fence(a2m, a2p, e0, e1p, squares)
     a3m, a3p, e1m = up(a2m), down(a2p), far(a1m)
     (near,) = pack([own, a1m, a1p, e0, a2m, a2p], [(k, 0, size) for k in range(6)])
     near_c = other(near)
     ids((0, 0), (-1, 0), (1, 0), (0, 1), (-2, 0), (2, 0))
     part0 = scores_of((hi, lo), [(near, 0, 6 * size), (near_c, 0, 6 * size)], squares)
-    a3m, a3p, e1m, e1p, part0 = fence(a3m, a3p, e1m, e1p, part0)
+    a3m, a3p, e1m, part0 = fence(a3m, a3p, e1m, part0)
     for_up, for_down, for_far, three = pack(
         [a3m, a3p, e1m, e1p],
         [(0, 0, half), (2, 0, half)],
@@ -284,7 +300,7 @@
     got1 = over_y(part1)
     ids((4, 0, 0), (-2, 1, 0), (4, 0, 1), (2, 1, 0))
     part2 = scores_of((hi, lo), [(four, 0, 2 * size), (four_c, 0, 2 * size)])
-    up5, down5, far5, part2, got0 = fence(up5, down5, far5, part2, got0)
+    up5, down5, far5, part2, got1 = fence(up5, down5, far5, part2, got1)
     (five,) = pack([up5, down5, far5], [(k, 0, size) for k in range(3)])
     five_c = other(five)
     got2 = over_y(part2)
@@ -293,7 +309,7 @@
         (hi, lo),
         [(four, 2 * size, size), (five, 0, 3 * size), (four_c, 2 * size, size), (five_c, 0, 3 * size)],
     )
-    part3, got1 = fence(part3, got1)
+    part3, got2 = fence(part3, got2)
     got3 = over_y(part3)
 
     source = jnp.stack(halves).astype(jnp.int32)

time: 184 us -> 170 us (0.924)
  waiting for transfers between devices: 63 us -> 35.2 us
  Pallas kernels: 35.3 us -> 60.5 us
  local copies, waits for them, and re-layouts: 29.6 us -> 11.7 us
  blocking collectives: 0 us -> 11.4 us
  starting transfers between devices: 50.5 us -> 45.5 us
    unnamed x58 -> x30, local copies, waits for them, and re-layouts: 26.1 us -> 8.13 us
    pallas_call x4, Pallas kernels: 23.1 us -> 40.3 us  [scores_of(): pl.pallas_call(functools.partial(score_kernel, spans, squares is not None...]
    ppermute x5, waiting for transfers between devices: 14.9 us -> 3.46 us  [far(): return lax.ppermute(block, 'blk', X_FAR)]
    all_to_all x0 -> x1, blocking collectives: none -> 11.4 us  [over_y(): return lax.all_to_all(slices, 'mod', 0, 0, axis_index_groups=Y_GROUPS)]
    ppermute x5, waiting for transfers between devices: 19.2 us -> 10.1 us  [up(): return lax.ppermute(block, 'blk', Z_UP)]
    all_to_all x4 -> x3, waiting for transfers between devices: 20.3 us -> 12.7 us  [over_y(): return lax.all_to_all(slices, 'mod', 0, 0, axis_index_groups=Y_GROUPS)]
    pallas_call x1, Pallas kernels: 6.84 us -> 12.5 us  [split_grads(): pl.pallas_call(split_kernel, grid=(rows // 64,), in_specs=[pl.BlockSpec((...]
    all_to_all x4 -> x3, starting transfers between devices: 17.2 us -> 12.2 us  [over_y(): return lax.all_to_all(slices, 'mod', 0, 0, axis_index_groups=Y_GROUPS)]
  transfers between devices with their start and end apart: 24 -> 23, of which waited for: 12 -> 9; matrix products, arithmetic and copies ran while one was open for 1% -> 1% of each run, Pallas kernels for 16% -> 31%
where the time goes in v1:
time: 170 us; the launch traced here: 169 us
  Pallas kernels  60.5 us (36%)
  starting transfers between devices  45.5 us (27%)
  waiting for transfers between devices  35.2 us (21%)
  local copies, waits for them, and re-layouts  11.7 us (7%)
  blocking collectives  11.4 us (7%)
  matrix products  4.07 us (2%)
    pallas_call x4, Pallas kernels, scores_of(): pl.pallas_call(functools.partial(score_kernel, spans, squares is not None...  40.3 us
    ppermute x5, starting transfers between devices, down(): return lax.ppermute(block, 'blk', Z_DOWN)  17 us
    all_to_all x3, waiting for transfers between devices, over_y(): return lax.all_to_all(slices, 'mod', 0, 0, axis_index_groups=Y_GROUPS)  12.7 us
    pallas_call x1, Pallas kernels, split_grads(): pl.pallas_call(split_kernel, grid=(rows // 64,), in_specs=[pl.BlockSpec((...  12.5 us
    all_to_all x3, starting transfers between devices, over_y(): return lax.all_to_all(slices, 'mod', 0, 0, axis_index_groups=Y_GROUPS)  12.2 us
    all_to_all x1, blocking collectives, over_y(): return lax.all_to_all(slices, 'mod', 0, 0, axis_index_groups=Y_GROUPS)  11.4 us
    ppermute x5, waiting for transfers between devices, up(): return lax.ppermute(block, 'blk', Z_UP)  10.1 us
    ppermute x5, starting transfers between devices, far(): return lax.ppermute(block, 'blk', X_FAR)  9 us
  transfers between devices with their start and end apart: 23, of which 9 were waited for; matrix products, arithmetic and copies ran while one was open for 1% of the time, Pallas kernels for 31%

profile of v1, /device:TPU:2, one launch (start us, length us, event | category | flops | bytes accessed | tf_op | source)
XLA Modules:
  0.0 169.1 jit_solution(3184871604169633723)
XLA Ops:
  0.0 1.5 reshape_squeeze.3
  1.5 3.1 %fusion.1 = f32[32,64,64]{1,2,0:T(8,128)S(1)} fusion(f32[32,64,64]{2,1,0:T(8,128)S(1)} %reshape_squeeze.3, f32[1,64,64]{2,1,0:T(8,128)S(1)} %copy-done), kind=kOutput, calls=%fused_computation.2 | convolution fusion | flops 100663296 | bytes 1064960 | tf_op jit(solution)/shard_map/rad,cd->rac/dot_general | solution.py:253
  6.3 2.0 %collective-permute-start = (f32[32,4096]{1,0:T(8,128)S(1)}, f32[32,4096]{1,0:T(8,128)S(1)}, u32[]{:S(2)}, u32[]{:S(2)}) collective-permute-start(f32[32,4096]{1,0:T(8,128)S(1)} %reshape.3020.refs_0_), channel_id=1, source_target_pairs={{0,4},{1,5},{2,6},{3,7},{4,8},{5,9},{6,10},{7,11},{8,12},{9,13},{1... | collective-permute-start | bytes 1572872 | tf_op jit(solution)/shard_map/ppermute | solution.py:33
  8.3 4.0 %collective-permute-start.1 = (f32[32,4096]{1,0:T(8,128)S(1)}, f32[32,4096]{1,0:T(8,128)S(1)}, u32[]{:S(2)}, u32[]{:S(2)}) collective-permute-start(f32[32,4096]{1,0:T(8,128)S(1)} %reshape.3020.refs_0_), channel_id=1, source_target_pairs={{0,28},{1,29},{2,30},{3,31},{4,0},{5,1},{6,2},{7,3},{8,4},{9,5},{1... | collective-permute-start | bytes 1572872 | tf_op jit(solution)/shard_map/ppermute | solution.py:37
  12.3 2.1 %collective-permute-start.4 = (f32[32,4096]{1,0:T(8,128)S(1)}, f32[32,4096]{1,0:T(8,128)S(1)}, u32[]{:S(2)}, u32[]{:S(2)}) collective-permute-start(f32[32,4096]{1,0:T(8,128)S(1)} %reshape.3020.refs_0_), channel_id=1, source_target_pairs={{0,2},{1,3},{2,0},{3,1},{4,6},{5,7},{6,4},{7,5},{8,10},{9,11},{10,... | collective-permute-start | bytes 1572872 | tf_op jit(solution)/shard_map/ppermute | solution.py:41
  14.4 9.7 %collective-permute-done.refs_1_ = f32[32,4096]{1,0:T(8,128)S(1)} collective-permute-done((f32[32,4096]{1,0:T(8,128)S(1)}, f32[32,4096]{1,0:T(8,128)S(1)}, u32[]{:S(2)}, u32[]{:S(2)}) %collective-permute-start) | collective-permute-done | bytes 524320 | tf_op jit(solution)/shard_map/ppermute | solution.py:33
  24.1 3.2 %collective-permute-start.3 = (f32[32,4096]{1,0:T(8,128)S(1)}, f32[32,4096]{1,0:T(8,128)S(1)}, u32[]{:S(2)}, u32[]{:S(2)}) collective-permute-start(f32[32,4096]{1,0:T(8,128)S(1)} %collective-permute-done.1.refs_2_), channel_id=1, source_target_pairs={{0,28},{1,29},{2,30},{3,31},{4,0},{5,1},{6,2},{7,3},{8,4},{9,5},{1... | collective-permute-start | bytes 1572872 | tf_op jit(solution)/shard_map/ppermute | solution.py:37
  27.4 2.1 %collective-permute-start.5 = (f32[32,4096]{1,0:T(8,128)S(1)}, f32[32,4096]{1,0:T(8,128)S(1)}, u32[]{:S(2)}, u32[]{:S(2)}) collective-permute-start(f32[32,4096]{1,0:T(8,128)S(1)} %collective-permute-done.1.refs_2_), channel_id=1, source_target_pairs={{0,2},{1,3},{2,0},{3,1},{4,6},{5,7},{6,4},{7,5},{8,10},{9,11},{10,... | collective-permute-start | bytes 1572872 | tf_op jit(solution)/shard_map/ppermute | solution.py:41
  29.5 12.5 %shard_map.64 = (bf16[8,640,512]{2,1,0:T(8,128)(2,1)}, bf16[8,640,512]{2,1,0:T(8,128)(2,1)}, f32[640,128]{1,0:T(8,128)S(1)}) custom-call(f32[640,4096]{1,0:T(8,128)} %bitcast.79), custom_call_target="tpu_custom_call" | custom-call | tf_op jit(solution)/shard_map/pallas_call | solution.py:71
  43.3 1.6 collective-permute-start.8
  45.0 3.2 %collective-permute-start.7 = (f32[32,4096]{1,0:T(8,128)S(1)}, f32[32,4096]{1,0:T(8,128)S(1)}, u32[]{:S(2)}, u32[]{:S(2)}) collective-permute-start(f32[32,4096]{1,0:T(8,128)S(1)} %collective-permute-done.3.refs_5_), channel_id=1, source_target_pairs={{0,28},{1,29},{2,30},{3,31},{4,0},{5,1},{6,2},{7,3},{8,4},{9,5},{1... | collective-permute-start | bytes 1572872 | tf_op jit(solution)/shard_map/ppermute | solution.py:37
  49.0 12.2 %shard_map.66 = f32[4,168,384]{2,1,0:T(8,128)S(1)} custom-call(bf16[8,640,512]{2,1,0:T(8,128)(2,1)} %get-tuple-element.51.hi_ref, bf16[8,640,512]{2,1,0:T(8,128)(2,1)} %get-tuple-element.52.lo_ref, f32[640,128]{1,0:T(8,128)S(1)} %get-tuple-element.53.refs_0_, f32[192,4096]{1,0:T(8,128)S(1)} %shard_map.65.refs_1_, f32[192,4096]{1,0:T(8,128)S(1)} %collective-permute-done.9.refs_2_), custom_call_target="tpu_custom_call" | custom-call | flops 6039797760 | bytes 4194304 | tf_op jit(solution)/shard_map/pallas_call | solution.py:130
  62.7 3.2 %collective-permute-start.12 = (f32[32,4096]{1,0:T(8,128)S(1)}, f32[32,4096]{1,0:T(8,128)S(1)}, u32[]{:S(2)}, u32[]{:S(2)}) collective-permute-start(f32[32,4096]{1,0:T(8,128)S(1)} %get-tuple-element.63), channel_id=1, source_target_pairs={{0,28},{1,29},{2,30},{3,31},{4,0},{5,1},{6,2},{7,3},{8,4},{9,5},{1... | collective-permute-start | bytes 1572872 | tf_op jit(solution)/shard_map/ppermute | solution.py:37
  66.0 1.6 collective-permute-start.13
  67.5 9.4 %shard_map.68 = f32[4,160,256]{2,1,0:T(8,128)S(1)} custom-call(bf16[8,640,512]{2,1,0:T(8,128)(2,1)} %get-tuple-element.51.hi_ref, bf16[8,640,512]{2,1,0:T(8,128)(2,1)} %get-tuple-element.52.lo_ref, f32[128,4096]{1,0:T(8,128)S(1)} %get-tuple-element.59.refs_0_, f32[128,4096]{1,0:T(8,128)S(1)} %collective-permute-done.10.refs_1_), custom_call_target="tpu_custom_call" | custom-call | flops 4026531840 | bytes 4194304 | tf_op jit(solution)/shard_map/pallas_call | solution.py:130
  78.1 3.0 %collective-permute-done.13.refs_2_ = f32[32,4096]{1,0:T(8,128)S(1)} collective-permute-done((f32[32,4096]{1,0:T(8,128)S(1)}, f32[32,4096]{1,0:T(8,128)S(1)}, u32[]{:S(2)}, u32[]{:S(2)}) %collective-permute-start.13) | collective-permute-done | bytes 524320 | tf_op jit(solution)/shard_map/ppermute | solution.py:41
  81.1 1.3 shard_map.69
  82.4 3.2 %collective-permute-start.15 = (f32[32,4096]{1,0:T(8,128)}, f32[32,4096]{1,0:T(8,128)}, u32[]{:S(2)}, u32[]{:S(2)}) collective-permute-start(f32[32,4096]{1,0:T(8,128)} %get-tuple-element.70), channel_id=1, source_target_pairs={{0,28},{1,29},{2,30},{3,31},{4,0},{5,1},{6,2},{7,3},{8,4},{9,5},{1... | collective-permute-start | bytes 1572872 | tf_op jit(solution)/shard_map/ppermute | solution.py:37
  85.6 1.6 collective-permute-start.16
  87.2 4.5 %all-to-all-start.1 = ((f32[4,160,256]{2,1,0:T(8,128)}), f32[4,160,256]{2,1,0:T(8,128)}, u32[]{:S(2)}, u32[]{:S(2)}) async-start(f32[4,160,256]{2,1,0:T(8,128)} %copy-done.6), calls=%async_computation.1 | async-start | bytes 1310720 | tf_op jit(solution)/shard_map/all_to_all | solution.py:145
  91.7 9.0 %shard_map.70 = f32[4,160,128]{2,1,0:T(8,128)S(1)} custom-call(bf16[8,640,512]{2,1,0:T(8,128)(2,1)} %get-tuple-element.51.hi_ref, bf16[8,640,512]{2,1,0:T(8,128)(2,1)} %get-tuple-element.52.lo_ref, f32[96,4096]{1,0:T(8,128)S(1)} %get-tuple-element.72.refs_0_, f32[96,4096]{1,0:T(8,128)S(1)} %collective-permute-done.17.refs_1_.refs_2_), custom_call_target="tpu_custom_call" | custom-call | flops 2013265920 | bytes 4194304 | tf_op jit(solution)/shard_map/pallas_call | solution.py:130
  102.5 1.5 shard_map.71.refs_1_
  104.0 11.4 %all_to_all.25.refs_2_ = f32[4,160,128]{2,1,0:T(8,128)} all-to-all(f32[4,160,128]{2,1,0:T(8,128)S(1)} %shard_map.70), channel_id=1, replica_groups={{0,32,64,96},{128,160,192,224},{1,33,65,97},{129,161,193,225},{2,34,66,..., dimensions={0} | all-to-all | bytes 655360 | tf_op jit(solution)/shard_map/all_to_all | solution.py:145
  115.4 4.2 %all-to-all-start = ((f32[4,168,384]{2,1,0:T(8,128)}), f32[4,168,384]{2,1,0:T(8,128)}, u32[]{:S(2)}, u32[]{:S(2)}) async-start(f32[4,168,384]{2,1,0:T(8,128)} %copy-done.11), calls=%async_computation | async-start | bytes 2064384 | tf_op jit(solution)/shard_map/all_to_all | solution.py:145
  120.1 1.4 copy-done.2
  121.5 9.6 %shard_map.72 = f32[4,160,256]{2,1,0:T(8,128)S(1)} custom-call(bf16[8,640,512]{2,1,0:T(8,128)(2,1)} %get-tuple-element.51.hi_ref, bf16[8,640,512]{2,1,0:T(8,128)(2,1)} %get-tuple-element.52.lo_ref, f32[96,4096]{1,0:T(8,128)S(1)} %get-tuple-element.72.refs_0_, f32[96,4096]{1,0:T(8,128)S(1)} %shard_map.71.refs_1_, f32[96,4096]{1,0:T(8,128)S(1)} %copy-done.2, ...), custom_call_target="tpu_custom_call" | custom-call | flops 4026531840 | bytes 4194304 | tf_op jit(solution)/shard_map/pallas_call | solution.py:130
  132.0 2.8 %all-to-all-done.refs_0_ = f32[4,168,384]{2,1,0:T(8,128)} async-done(((f32[4,168,384]{2,1,0:T(8,128)}), f32[4,168,384]{2,1,0:T(8,128)}, u32[]{:S(2)}, u32[]{:S(2)}) %all-to-all-start) | async-done | bytes 1032224 | tf_op jit(solution)/shard_map/all_to_all | solution.py:145
  134.7 3.5 %all-to-all-start.3 = ((f32[4,160,256]{2,1,0:T(8,128)}), f32[4,160,256]{2,1,0:T(8,128)S(1)}, u32[]{:S(2)}, u32[]{:S(2)}) async-start(f32[4,160,256]{2,1,0:T(8,128)} %copy-done.3), calls=%async_computation.3 | async-start | bytes 1310720 | tf_op jit(solution)/shard_map/all_to_all | solution.py:145
  139.5 8.7 %all-to-all-done.3.refs_3_ = f32[4,160,256]{2,1,0:T(8,128)S(1)} async-done(((f32[4,160,256]{2,1,0:T(8,128)}), f32[4,160,256]{2,1,0:T(8,128)S(1)}, u32[]{:S(2)}, u32[]{:S(2)}) %all-to-all-start.3) | async-done | bytes 655392 | tf_op jit(solution)/shard_map/all_to_all | solution.py:145
  151.2 3.6 %shard_map.73 = f32[8,168,128]{2,1,0:T(8,128)} custom-call(s32[1024,1]{1,0:T(8,128)S(1)} %copy-done.9, f32[4,168,384]{2,1,0:T(8,128)} %all-to-all-done.refs_0_, f32[4,160,256]{2,1,0:T(8,128)} %all-to-all-done.1.refs_1_, f32[4,160,128]{2,1,0:T(8,128)S(1)} %copy-done.10, f32[4,160,256]{2,1,0:T(8,128)S(1)} %copy-done.5), custom_call_target="tpu_custom_call" | custom-call | tf_op jit(solution)/shard_map/pallas_call | solution.py:198
  154.9 4.9 %all-to-all-start.4 = ((f32[8,168,128]{2,1,0:T(8,128)}), f32[8,168,128]{2,1,0:T(8,128)S(1)}, u32[]{:S(2)}, u32[]{:S(2)}) async-start(f32[8,168,128]{2,1,0:T(8,128)} %shard_map.73), calls=%async_computation.4 | async-start | bytes 1376256 | tf_op jit(solution)/shard_map/all_to_all | solution.py:321
  160.0 8.2 %all-to-all-done.4.got_ref = f32[8,168,128]{2,1,0:T(8,128)S(1)} async-done(((f32[8,168,128]{2,1,0:T(8,128)}), f32[8,168,128]{2,1,0:T(8,128)S(1)}, u32[]{:S(2)}, u32[]{:S(2)}) %all-to-all-start.4) | async-done | bytes 688160 | tf_op jit(solution)/shard_map/all_to_all | solution.py:321
  (70 shorter events, 14.8 us)
Async XLA Ops:
  0.0 1.5 copy-start
  0.0 4.6 %copy-start.12 = (f32[1,64,64]{2,1,0:T(8,128)S(1)}, f32[1,64,64]{2,1,0:T(8,128)}, u32[]{:S(2)}) copy-start(f32[1,64,64]{2,1,0:T(8,128)} %param.7) | copy-start | bytes 49156
  6.3 35.7 %copy-start.7 = (f32[32,4096]{1,0:T(8,128)}, f32[32,4096]{1,0:T(8,128)S(1)}, u32[]{:S(2)}) copy-start(f32[32,4096]{1,0:T(8,128)S(1)} %reshape.3020.refs_0_) | copy-start | bytes 1572868
  6.3 17.9 %collective-permute-start = (f32[32,4096]{1,0:T(8,128)S(1)}, f32[32,4096]{1,0:T(8,128)S(1)}, u32[]{:S(2)}, u32[]{:S(2)}) collective-permute-start(f32[32,4096]{1,0:T(8,128)S(1)} %reshape.3020.refs_0_), channel_id=1, source_target_pairs={{0,4},{1,5},{2,6},{3,7},{4,8},{5,9},{6,10},{7,11},{8,12},{9,13},{1... | collective-permute-start | bytes 1572872 | tf_op jit(solution)/shard_map/ppermute | solution.py:33
  8.3 15.9 %collective-permute-start.1 = (f32[32,4096]{1,0:T(8,128)S(1)}, f32[32,4096]{1,0:T(8,128)S(1)}, u32[]{:S(2)}, u32[]{:S(2)}) collective-permute-start(f32[32,4096]{1,0:T(8,128)S(1)} %reshape.3020.refs_0_), channel_id=1, source_target_pairs={{0,28},{1,29},{2,30},{3,31},{4,0},{5,1},{6,2},{7,3},{8,4},{9,5},{1... | collective-permute-start | bytes 1572872 | tf_op jit(solution)/shard_map/ppermute | solution.py:37
  12.3 29.7 %collective-permute-start.4 = (f32[32,4096]{1,0:T(8,128)S(1)}, f32[32,4096]{1,0:T(8,128)S(1)}, u32[]{:S(2)}, u32[]{:S(2)}) collective-permute-start(f32[32,4096]{1,0:T(8,128)S(1)} %reshape.3020.refs_0_), channel_id=1, source_target_pairs={{0,2},{1,3},{2,0},{3,1},{4,6},{5,7},{6,4},{7,5},{8,10},{9,11},{10,... | collective-permute-start | bytes 1572872 | tf_op jit(solution)/shard_map/ppermute | solution.py:41
  24.1 17.8 %collective-permute-start.2 = (f32[32,4096]{1,0:T(8,128)S(1)}, f32[32,4096]{1,0:T(8,128)S(1)}, u32[]{:S(2)}, u32[]{:S(2)}) collective-permute-start(f32[32,4096]{1,0:T(8,128)S(1)} %collective-permute-done.refs_1_), channel_id=1, source_target_pairs={{0,4},{1,5},{2,6},{3,7},{4,8},{5,9},{6,10},{7,11},{8,12},{9,13},{1... | collective-permute-start | bytes 1572872 | tf_op jit(solution)/shard_map/ppermute | solution.py:33
  24.1 17.8 %collective-permute-start.3 = (f32[32,4096]{1,0:T(8,128)S(1)}, f32[32,4096]{1,0:T(8,128)S(1)}, u32[]{:S(2)}, u32[]{:S(2)}) collective-permute-start(f32[32,4096]{1,0:T(8,128)S(1)} %collective-permute-done.1.refs_2_), channel_id=1, source_target_pairs={{0,28},{1,29},{2,30},{3,31},{4,0},{5,1},{6,2},{7,3},{8,4},{9,5},{1... | collective-permute-start | bytes 1572872 | tf_op jit(solution)/shard_map/ppermute | solution.py:37
  27.4 14.6 %collective-permute-start.5 = (f32[32,4096]{1,0:T(8,128)S(1)}, f32[32,4096]{1,0:T(8,128)S(1)}, u32[]{:S(2)}, u32[]{:S(2)}) collective-permute-start(f32[32,4096]{1,0:T(8,128)S(1)} %collective-permute-done.1.refs_2_), channel_id=1, source_target_pairs={{0,2},{1,3},{2,0},{3,1},{4,6},{5,7},{6,4},{7,5},{8,10},{9,11},{10,... | collective-permute-start | bytes 1572872 | tf_op jit(solution)/shard_map/ppermute | solution.py:41
  43.2 5.7 %collective-permute-start.9 = (f32[192,4096]{1,0:T(8,128)S(1)}, f32[192,4096]{1,0:T(8,128)S(1)}, u32[]{:S(2)}, u32[]{:S(2)}) collective-permute-start(f32[192,4096]{1,0:T(8,128)S(1)} %shard_map.65.refs_1_), channel_id=1, source_target_pairs={{0,1},{1,0},{2,3},{3,2},{4,5},{5,4},{6,7},{7,6},{8,9},{9,8},{10,11... | collective-permute-start | bytes 9437192 | tf_op jit(solution)/shard_map/ppermute | solution.py:45
  43.3 18.9 %collective-permute-start.8 = (f32[32,4096]{1,0:T(8,128)S(1)}, f32[32,4096]{1,0:T(8,128)S(1)}, u32[]{:S(2)}, u32[]{:S(2)}) collective-permute-start(f32[32,4096]{1,0:T(8,128)S(1)} %collective-permute-done.refs_1_), channel_id=1, source_target_pairs={{0,2},{1,3},{2,0},{3,1},{4,6},{5,7},{6,4},{7,5},{8,10},{9,11},{10,... | collective-permute-start | bytes 1572872 | tf_op jit(solution)/shard_map/ppermute | solution.py:41
  45.0 17.2 %collective-permute-start.6 = (f32[32,4096]{1,0:T(8,128)S(1)}, f32[32,4096]{1,0:T(8,128)S(1)}, u32[]{:S(2)}, u32[]{:S(2)}) collective-permute-start(f32[32,4096]{1,0:T(8,128)S(1)} %collective-permute-done.2.refs_4_), channel_id=1, source_target_pairs={{0,4},{1,5},{2,6},{3,7},{4,8},{5,9},{6,10},{7,11},{8,12},{9,13},{1... | collective-permute-start | bytes 1572872 | tf_op jit(solution)/shard_map/ppermute | solution.py:33
  45.0 17.2 %collective-permute-start.7 = (f32[32,4096]{1,0:T(8,128)S(1)}, f32[32,4096]{1,0:T(8,128)S(1)}, u32[]{:S(2)}, u32[]{:S(2)}) collective-permute-start(f32[32,4096]{1,0:T(8,128)S(1)} %collective-permute-done.3.refs_5_), channel_id=1, source_target_pairs={{0,28},{1,29},{2,30},{3,31},{4,0},{5,1},{6,2},{7,3},{8,4},{9,5},{1... | collective-permute-start | bytes 1572872 | tf_op jit(solution)/shard_map/ppermute | solution.py:37
  62.5 5.0 %collective-permute-start.10 = (f32[128,4096]{1,0:T(8,128)S(1)}, f32[128,4096]{1,0:T(8,128)S(1)}, u32[]{:S(2)}, u32[]{:S(2)}) collective-permute-start(f32[128,4096]{1,0:T(8,128)S(1)} %get-tuple-element.59.refs_0_), channel_id=1, source_target_pairs={{0,1},{1,0},{2,3},{3,2},{4,5},{5,4},{6,7},{7,6},{8,9},{9,8},{10,11... | collective-permute-start | bytes 6291464 | tf_op jit(solution)/shard_map/ppermute | solution.py:45
  62.7 15.4 %collective-permute-start.11 = (f32[32,4096]{1,0:T(8,128)S(1)}, f32[32,4096]{1,0:T(8,128)S(1)}, u32[]{:S(2)}, u32[]{:S(2)}) collective-permute-start(f32[32,4096]{1,0:T(8,128)S(1)} %get-tuple-element.62), channel_id=1, source_target_pairs={{0,4},{1,5},{2,6},{3,7},{4,8},{5,9},{6,10},{7,11},{8,12},{9,13},{1... | collective-permute-start | bytes 1572872 | tf_op jit(solution)/shard_map/ppermute | solution.py:33
  62.7 15.4 %collective-permute-start.12 = (f32[32,4096]{1,0:T(8,128)S(1)}, f32[32,4096]{1,0:T(8,128)S(1)}, u32[]{:S(2)}, u32[]{:S(2)}) collective-permute-start(f32[32,4096]{1,0:T(8,128)S(1)} %get-tuple-element.63), channel_id=1, source_target_pairs={{0,28},{1,29},{2,30},{3,31},{4,0},{5,1},{6,2},{7,3},{8,4},{9,5},{1... | collective-permute-start | bytes 1572872 | tf_op jit(solution)/shard_map/ppermute | solution.py:37
  66.0 15.1 %collective-permute-start.13 = (f32[32,4096]{1,0:T(8,128)S(1)}, f32[32,4096]{1,0:T(8,128)S(1)}, u32[]{:S(2)}, u32[]{:S(2)}) collective-permute-start(f32[32,4096]{1,0:T(8,128)S(1)} %get-tuple-element.64), channel_id=1, source_target_pairs={{0,2},{1,3},{2,0},{3,1},{4,6},{5,7},{6,4},{7,5},{8,10},{9,11},{10,... | collective-permute-start | bytes 1572872 | tf_op jit(solution)/shard_map/ppermute | solution.py:41
  82.4 4.8 %collective-permute-start.17 = (f32[96,4096]{1,0:T(8,128)S(1)}, f32[96,4096]{1,0:T(8,128)S(1)}, u32[]{:S(2)}, u32[]{:S(2)}) collective-permute-start(f32[96,4096]{1,0:T(8,128)S(1)} %get-tuple-element.72.refs_0_), channel_id=1, source_target_pairs={{0,1},{1,0},{2,3},{3,2},{4,5},{5,4},{6,7},{7,6},{8,9},{9,8},{10,11... | collective-permute-start | bytes 4718600 | tf_op jit(solution)/shard_map/ppermute | solution.py:45
  82.4 18.3 %collective-permute-start.14 = (f32[32,4096]{1,0:T(8,128)}, f32[32,4096]{1,0:T(8,128)}, u32[]{:S(2)}, u32[]{:S(2)}) collective-permute-start(f32[32,4096]{1,0:T(8,128)} %get-tuple-element.69), channel_id=1, source_target_pairs={{0,4},{1,5},{2,6},{3,7},{4,8},{5,9},{6,10},{7,11},{8,12},{9,13},{1... | collective-permute-start | bytes 1572872 | tf_op jit(solution)/shard_map/ppermute | solution.py:33
  82.4 18.3 %collective-permute-start.15 = (f32[32,4096]{1,0:T(8,128)}, f32[32,4096]{1,0:T(8,128)}, u32[]{:S(2)}, u32[]{:S(2)}) collective-permute-start(f32[32,4096]{1,0:T(8,128)} %get-tuple-element.70), channel_id=1, source_target_pairs={{0,28},{1,29},{2,30},{3,31},{4,0},{5,1},{6,2},{7,3},{8,4},{9,5},{1... | collective-permute-start | bytes 1572872 | tf_op jit(solution)/shard_map/ppermute | solution.py:37
  85.6 15.6 %collective-permute-start.16 = (f32[32,4096]{1,0:T(8,128)}, f32[32,4096]{1,0:T(8,128)}, u32[]{:S(2)}, u32[]{:S(2)}) collective-permute-start(f32[32,4096]{1,0:T(8,128)} %get-tuple-element.71), channel_id=1, source_target_pairs={{0,2},{1,3},{2,0},{3,1},{4,6},{5,7},{6,4},{7,5},{8,10},{9,11},{10,... | collective-permute-start | bytes 1572872 | tf_op jit(solution)/shard_map/ppermute | solution.py:41
  87.2 13.5 %copy-start.1 = (f32[96,4096]{1,0:T(8,128)}, f32[96,4096]{1,0:T(8,128)S(1)}, u32[]{:S(2)}) copy-start(f32[96,4096]{1,0:T(8,128)S(1)} %collective-permute-done.17.refs_1_.refs_2_) | copy-start | bytes 4718596
  87.2 15.3 %all-to-all-start.1 = ((f32[4,160,256]{2,1,0:T(8,128)}), f32[4,160,256]{2,1,0:T(8,128)}, u32[]{:S(2)}, u32[]{:S(2)}) async-start(f32[4,160,256]{2,1,0:T(8,128)} %copy-done.6), calls=%async_computation.1 | async-start | bytes 1310720 | tf_op jit(solution)/shard_map/all_to_all | solution.py:145
  103.9 16.1 %collective-permute-start.18 = (f32[96,4096]{1,0:T(8,128)S(1)}, f32[96,4096]{1,0:T(8,128)}, u32[]{:S(2)}, u32[]{:S(2)}) collective-permute-start(f32[96,4096]{1,0:T(8,128)S(1)} %shard_map.71.refs_1_), channel_id=1, source_target_pairs={{0,1},{1,0},{2,3},{3,2},{4,5},{5,4},{6,7},{7,6},{8,9},{9,8},{10,11... | collective-permute-start | bytes 4718600 | tf_op jit(solution)/shard_map/ppermute | solution.py:45
  115.4 19.3 %all-to-all-start = ((f32[4,168,384]{2,1,0:T(8,128)}), f32[4,168,384]{2,1,0:T(8,128)}, u32[]{:S(2)}, u32[]{:S(2)}) async-start(f32[4,168,384]{2,1,0:T(8,128)} %copy-done.11), calls=%async_computation | async-start | bytes 2064384 | tf_op jit(solution)/shard_map/all_to_all | solution.py:145
  120.1 1.4 copy-start.2
  121.5 16.7 %copy-start.13 = (s32[32]{0:T(128)S(1)}, s32[32]{0:T(128)}, u32[]{:S(2)}) copy-start(s32[32]{0:T(128)} %param.10) | copy-start | bytes 388
  131.9 17.2 %copy-start.10 = (f32[4,160,128]{2,1,0:T(8,128)S(1)}, f32[4,160,128]{2,1,0:T(8,128)}, u32[]{:S(2)}) copy-start(f32[4,160,128]{2,1,0:T(8,128)} %all_to_all.25.refs_2_) | copy-start | bytes 983044
  134.7 13.5 %all-to-all-start.3 = ((f32[4,160,256]{2,1,0:T(8,128)}), f32[4,160,256]{2,1,0:T(8,128)S(1)}, u32[]{:S(2)}, u32[]{:S(2)}) async-start(f32[4,160,256]{2,1,0:T(8,128)} %copy-done.3), calls=%async_computation.3 | async-start | bytes 1310720 | tf_op jit(solution)/shard_map/all_to_all | solution.py:145
  149.1 1.1 copy-start.5
  151.2 8.5 %copy-start.14 = (s32[32]{0:T(128)S(1)}, s32[32]{0:T(128)}, u32[]{:S(2)}) copy-start(s32[32]{0:T(128)} %param.11) | copy-start | bytes 388
  154.9 13.3 %all-to-all-start.4 = ((f32[8,168,128]{2,1,0:T(8,128)}), f32[8,168,128]{2,1,0:T(8,128)S(1)}, u32[]{:S(2)}, u32[]{:S(2)}) async-start(f32[8,168,128]{2,1,0:T(8,128)} %shard_map.73), calls=%async_computation.4 | async-start | bytes 1376256 | tf_op jit(solution)/shard_map/all_to_all | solution.py:321
  (6 other events, 5.6 us)

commit v2 on v1

--- a/solution.py
+++ b/solution.py
@@ -9,7 +9,7 @@
 
 NZ = 8
 NY = 4
-FEAT_STEP = 512
+FEAT_STEP = 1024
 VMEM_LIMIT = 16 * 1024 * 1024
 
 
@@ -82,9 +82,12 @@
     )(pltpu.with_memory_space_constraint(grads, pltpu.HBM))
 
 
-def score_kernel(spans, squares, hi_ref, lo_ref, *refs):
+def score_kernel(spans, squares, prior, hi_ref, lo_ref, *refs):
+    sq_ref = old_ref = None
     if squares:
         sq_ref, *refs = refs
+    if prior:
+        old_ref, *refs = refs
     pieces = refs[: len(spans)]
     out_ref, acc = refs[len(spans) :]
     step = pl.program_id(0)
@@ -104,37 +107,43 @@
 
     @pl.when(step == pl.num_programs(0) - 1)
     def _():
-        emit(squares, sq_ref if squares else None, acc, out_ref)
-
-
-def emit(squares, sq_ref, acc, out_ref):
-    rows = acc.shape[0]
-    count = rows // NY
+        emit(sq_ref, old_ref, acc, out_ref)
+
+
+def emit(sq_ref, old_ref, acc, out_ref):
+    count = acc.shape[0] // NY
+    at = out_ref.shape[2] - acc.shape[1]
     for k in range(NY):
         here = slice(k * count, (k + 1) * count)
-        out_ref[k, 0:count, :] = acc[here, :]
-        if squares:
+        out_ref[k, 0:count, at:] = acc[here, :]
+        if old_ref is not None:
+            out_ref[k, :, 0:at] = old_ref[k]
+            out_ref[k, count:, at:] = jnp.zeros((out_ref.shape[1] - count, acc.shape[1]), jnp.float32)
+        if sq_ref is not None:
             out_ref[k, count:, :] = jnp.zeros((8, out_ref.shape[2]), jnp.float32)
             out_ref[k, count:, 0:count] = jnp.transpose(sq_ref[here, 0:8])
 
 
-def scores_of(grads, pieces, squares=None):
+def scores_of(grads, pieces, squares=None, prior=None):
     hi, lo = (pltpu.with_memory_space_constraint(g, pltpu.HBM) for g in grads)
     steps, rows, wide = hi.shape
     spans = [(first, first + count) for _, first, count in pieces]
     width = sum(count for _, _, count in pieces)
     slice_rows = rows // NY + (0 if squares is None else 8)
+    if prior is not None:
+        slice_rows = prior.shape[1]
     whole = pl.BlockSpec(memory_space=pltpu.VMEM)
-    extra = [] if squares is None else [squares]
+    extra = [v for v in (squares, prior) if v is not None]
+    full = width + (0 if prior is None else prior.shape[2])
     flops = 6 * rows * width * steps * wide
     return pl.pallas_call(
-        functools.partial(score_kernel, spans, squares is not None),
+        functools.partial(score_kernel, spans, squares is not None, prior is not None),
         grid=(steps,),
         in_specs=[pl.BlockSpec((1, rows, wide), lambda i: (i, 0, 0))] * 2
         + [whole] * len(extra)
         + [pl.BlockSpec((p[0].shape[0], wide), lambda i: (0, i)) for p in pieces],
         out_specs=whole,
-        out_shape=jax.ShapeDtypeStruct((NY, slice_rows, width), jnp.float32),
+        out_shape=jax.ShapeDtypeStruct((NY, slice_rows, full), jnp.float32),
         scratch_shapes=[pltpu.VMEM((rows, width), jnp.float32)],
         compiler_params=pltpu.CompilerParams(vmem_limit_bytes=VMEM_LIMIT),
         cost_estimate=pl.CostEstimate(flops=flops, bytes_accessed=4 * 1024 * 1024, transcendentals=0),
@@ -168,8 +177,8 @@
     )(*blocks)
 
 
-def place_kernel(dest_ref, *refs):
-    *parts, out_ref = refs
+def place_kernel(nparts, dest_ref, *refs):
+    parts, (*old, out_ref) = refs[:nparts], refs[nparts:]
     sums = [p[0] + p[1] + (p[2] + p[3]) for p in parts]
     count = parts[-1].shape[1]
     total = jnp.concatenate([v[:count] for v in sums], axis=1)
@@ -178,30 +187,35 @@
     mid = rest.astype(jnp.bfloat16)
     low = (rest - mid.astype(jnp.float32)).astype(jnp.bfloat16)
     stacked = jnp.concatenate([high, mid, low], axis=0)
-    squares = sums[0][count:, :]
-    row = lax.broadcasted_iota(jnp.int32, (8, 128), 0)
-    tail = jnp.where(row == 0, squares[:, 0:128], squares[:, 128:256])
-    nq = dest_ref.shape[0]
-    lane = lax.broadcasted_iota(jnp.int32, (nq, 256), 1)
-    for first in range(0, nq, 256):
-        pick = jnp.where(dest_ref[...] == lane + first, 1.0, 0.0).astype(jnp.bfloat16)
-        moved = jnp.dot(stacked, pick, preferred_element_type=jnp.float32)
+    if old:
+        tail = old[0][0, count:, :]
+    else:
+        squares = sums[0][count:, :]
+        row = lax.broadcasted_iota(jnp.int32, (8, 128), 0)
+        tail = jnp.where(row == 0, squares[:, 0:128], squares[:, 128:256])
+    slot = lax.broadcasted_iota(jnp.int32, (256, total.shape[1]), 0)
+    for first in range(0, 128 * out_ref.shape[0], 256):
+        pick = jnp.where(dest_ref[...] == slot + first, 1.0, 0.0).astype(jnp.bfloat16)
+        moved = nt(stacked, pick)
         moved = moved[:count] + (moved[count : 2 * count] + moved[2 * count :])
         for k in range(2):
-            out_ref[first // 128 + k, 0:count, :] = moved[:, k * 128 : (k + 1) * 128]
-            out_ref[first // 128 + k, count:, :] = tail
-
-
-def place(dest, parts):
+            at = first // 128 + k
+            value = moved[:, k * 128 : (k + 1) * 128]
+            out_ref[at, 0:count, :] = value + old[0][at, 0:count, :] if old else value
+            out_ref[at, count:, :] = tail
+
+
+def place(groups, dest, parts, rows, old=()):
     whole = pl.BlockSpec(memory_space=pltpu.VMEM)
-    nq = dest.shape[0]
-    return pl.pallas_call(
-        place_kernel,
-        in_specs=[whole] * (1 + len(parts)),
+    return pl.pallas_call(
+        functools.partial(place_kernel, len(parts)),
+        grid=(1,),
+        in_specs=[whole] * (1 + len(parts) + len(old)),
         out_specs=whole,
-        out_shape=jax.ShapeDtypeStruct((nq // 128, parts[0].shape[1], 128), jnp.float32),
-        compiler_params=pltpu.CompilerParams(vmem_limit_bytes=VMEM_LIMIT),
-    )(dest[:, None], *parts)
+        out_shape=jax.ShapeDtypeStruct((groups, rows, 128), jnp.float32),
+        compiler_params=pltpu.CompilerParams(vmem_limit_bytes=VMEM_LIMIT),
+        cost_estimate=pl.CostEstimate(flops=10**9, bytes_accessed=4 * 1024 * 1024, transcendentals=0),
+    )(dest[None, :], *parts, *old)
 
 
 def finish_kernel(window, terms, base_ref, first_ref, got_ref, out_ref):
@@ -283,8 +297,7 @@
         [(k, 0, size) for k in range(4)],
     )
     up4, down4, far4 = up(for_up), down(for_down), far(for_far)
-    three_c, part0 = fence(other(three), part0)
-    got0 = over_y(part0)
+    three_c = other(three)
     ids((-3, 0), (3, 0), (-1, 1), (1, 1))
     part1 = scores_of((hi, lo), [(three, 0, 4 * size), (three_c, 0, 4 * size)])
     up4, down4, far4, part1 = fence(up4, down4, far4, part1)
@@ -299,17 +312,17 @@
     four_c, part1 = fence(other(four), part1)
     got1 = over_y(part1)
     ids((4, 0, 0), (-2, 1, 0), (4, 0, 1), (2, 1, 0))
-    part2 = scores_of((hi, lo), [(four, 0, 2 * size), (four_c, 0, 2 * size)])
-    up5, down5, far5, part2, got1 = fence(up5, down5, far5, part2, got1)
+    part02 = scores_of((hi, lo), [(four, 0, 2 * size), (four_c, 0, 2 * size)], prior=part0)
+    up5, down5, far5, part02, got1 = fence(up5, down5, far5, part02, got1)
     (five,) = pack([up5, down5, far5], [(k, 0, size) for k in range(3)])
     five_c = other(five)
-    got2 = over_y(part2)
+    got02 = over_y(part02)
     ids((3, 1, 1), (-3, 1, 1), (-2, 1, 1), (-3, 1, 0), (2, 1, 1), (3, 1, 0), (4, 1, 0), (4, 1, 1))
     part3 = scores_of(
         (hi, lo),
         [(four, 2 * size, size), (five, 0, 3 * size), (four_c, 2 * size, size), (five_c, 0, 3 * size)],
     )
-    part3, got2 = fence(part3, got2)
+    part3, got02 = fence(part3, got02)
     got3 = over_y(part3)
 
     source = jnp.stack(halves).astype(jnp.int32)
@@ -317,7 +330,12 @@
     target = jnp.sum(jnp.where((source // 2)[:, None] == blocks[None, :], owners[None, :], 0), axis=1)
     dest = ((target * 2 + source % 2) * half)[:, None] + jnp.arange(half, dtype=jnp.int32)[None, :]
     dest = dest.reshape(-1)
-    placed = place(dest, [got0, got1, got2, got3])
+    ends = (part0.shape[2], part0.shape[2] + part1.shape[2], part02.shape[2] + part1.shape[2])
+    early = ends[2]
+    first_dest = jnp.concatenate([dest[: ends[0]], dest[ends[1] : early], dest[ends[0] : ends[1]]])
+    groups, rows = dest.shape[0] // 128, got02.shape[1]
+    placed = place(groups, first_dest, [got02, got1], rows)
+    placed = place(groups, dest[early:], [got3], rows, [placed])
     got = lax.all_to_all(placed, "mod", 0, 0)
     out_block = m * (nblk // nmods) + jnp.arange(placed.shape[2], dtype=jnp.int32) // qblock
     first = jnp.sum(jnp.where(out_block[:, None] == blocks[None, :], range_start[None, :], 0), axis=1)

time: 170 us -> 162 us (0.953)
  blocking collectives: 11.4 us -> 0 us
  waiting for transfers between devices: 35.2 us -> 43.3 us
  Pallas kernels: 60.5 us -> 56.9 us
  local copies, waits for them, and re-layouts: 11.7 us -> 9.71 us
    all_to_all x1 -> x0, blocking collectives: 11.4 us -> none  [over_y(): return lax.all_to_all(slices, 'mod', 0, 0, axis_index_groups=Y_GROUPS)]
    pallas_call x4, Pallas kernels: 40.3 us -> 34.1 us  [scores_of(): pl.pallas_call(functools.partial(score_kernel, spans, squares is not None...]
    all_to_all x3, waiting for transfers between devices: 12.7 us -> 18.4 us  [over_y(): return lax.all_to_all(slices, 'mod', 0, 0, axis_index_groups=Y_GROUPS)]
    pallas_call x1 -> x2, Pallas kernels: 3.63 us -> 4.91 us  [place(): pl.pallas_call(functools.partial(place_kernel, len(parts)), grid=(1,), in...]
    unnamed x30 -> x26, local copies, waits for them, and re-layouts: 8.13 us -> 6.97 us
  transfers between devices with their start and end apart: 23 -> 23, of which waited for: 9 -> 8; matrix products, arithmetic and copies ran while one was open for 1% -> 1% of each run, Pallas kernels for 31% -> 30%
where the time goes in v2:
time: 162 us
  Pallas kernels  56.9 us (35%)
  starting transfers between devices  46.8 us (29%)
  waiting for transfers between devices  43.3 us (27%)
  local copies, waits for them, and re-layouts  9.71 us (6%)
  matrix products  4.07 us (3%)
    pallas_call x4, Pallas kernels, scores_of(): pl.pallas_call(functools.partial(score_kernel, spans, squares is not None...  34.1 us
    all_to_all x3, waiting for transfers between devices, over_y(): return lax.all_to_all(slices, 'mod', 0, 0, axis_index_groups=Y_GROUPS)  18.4 us
    ppermute x5, starting transfers between devices, down(): return lax.ppermute(block, 'blk', Z_DOWN)  16.1 us
    all_to_all x3, starting transfers between devices, over_y(): return lax.all_to_all(slices, 'mod', 0, 0, axis_index_groups=Y_GROUPS)  13.1 us
    pallas_call x1, Pallas kernels, split_grads(): pl.pallas_call(split_kernel, grid=(rows // 64,), in_specs=[pl.BlockSpec((...  12.5 us
    ppermute x5, waiting for transfers between devices, up(): return lax.ppermute(block, 'blk', Z_UP)  11.8 us
    ppermute x5, starting transfers between devices, far(): return lax.ppermute(block, 'blk', X_FAR)  9.46 us
    all_to_all x1, waiting for transfers between devices, shards(): got = lax.all_to_all(placed, 'mod', 0, 0)  9.28 us
  transfers between devices with their start and end apart: 23, of which 8 were waited for; matrix products, arithmetic and copies ran while one was open for 1% of the time, Pallas kernels for 30%

profile of v2, /device:TPU:2, one launch (start us, length us, event | category | flops | bytes accessed | tf_op | source)
XLA Modules:
  0.0 161.5 jit_solution(9766263201018073086)
XLA Ops:
  0.0 1.5 reshape_squeeze.3
  1.5 3.1 %fusion.1 = f32[32,64,64]{1,2,0:T(8,128)S(1)} fusion(f32[32,64,64]{2,1,0:T(8,128)S(1)} %reshape_squeeze.3, f32[1,64,64]{2,1,0:T(8,128)S(1)} %copy-done), kind=kOutput, calls=%fused_computation.2 | convolution fusion | flops 100663296 | bytes 1064960 | tf_op jit(solution)/shard_map/rad,cd->rac/dot_general | solution.py:267
  6.3 2.0 %collective-permute-start = (f32[32,4096]{1,0:T(8,128)S(1)}, f32[32,4096]{1,0:T(8,128)S(1)}, u32[]{:S(2)}, u32[]{:S(2)}) collective-permute-start(f32[32,4096]{1,0:T(8,128)S(1)} %reshape.3004.refs_0_), channel_id=1, source_target_pairs={{0,4},{1,5},{2,6},{3,7},{4,8},{5,9},{6,10},{7,11},{8,12},{9,13},{1... | collective-permute-start | bytes 1572872 | tf_op jit(solution)/shard_map/ppermute | solution.py:33
  8.3 4.0 %collective-permute-start.1 = (f32[32,4096]{1,0:T(8,128)S(1)}, f32[32,4096]{1,0:T(8,128)S(1)}, u32[]{:S(2)}, u32[]{:S(2)}) collective-permute-start(f32[32,4096]{1,0:T(8,128)S(1)} %reshape.3004.refs_0_), channel_id=1, source_target_pairs={{0,28},{1,29},{2,30},{3,31},{4,0},{5,1},{6,2},{7,3},{8,4},{9,5},{1... | collective-permute-start | bytes 1572872 | tf_op jit(solution)/shard_map/ppermute | solution.py:37
  12.3 2.1 %collective-permute-start.4 = (f32[32,4096]{1,0:T(8,128)S(1)}, f32[32,4096]{1,0:T(8,128)S(1)}, u32[]{:S(2)}, u32[]{:S(2)}) collective-permute-start(f32[32,4096]{1,0:T(8,128)S(1)} %reshape.3004.refs_0_), channel_id=1, source_target_pairs={{0,2},{1,3},{2,0},{3,1},{4,6},{5,7},{6,4},{7,5},{8,10},{9,11},{10,... | collective-permute-start | bytes 1572872 | tf_op jit(solution)/shard_map/ppermute | solution.py:41
  14.4 9.7 %collective-permute-done.refs_1_ = f32[32,4096]{1,0:T(8,128)S(1)} collective-permute-done((f32[32,4096]{1,0:T(8,128)S(1)}, f32[32,4096]{1,0:T(8,128)S(1)}, u32[]{:S(2)}, u32[]{:S(2)}) %collective-permute-start) | collective-permute-done | bytes 524320 | tf_op jit(solution)/shard_map/ppermute | solution.py:33
  24.1 3.2 %collective-permute-start.3 = (f32[32,4096]{1,0:T(8,128)S(1)}, f32[32,4096]{1,0:T(8,128)S(1)}, u32[]{:S(2)}, u32[]{:S(2)}) collective-permute-start(f32[32,4096]{1,0:T(8,128)S(1)} %collective-permute-done.1.refs_2_), channel_id=1, source_target_pairs={{0,28},{1,29},{2,30},{3,31},{4,0},{5,1},{6,2},{7,3},{8,4},{9,5},{1... | collective-permute-start | bytes 1572872 | tf_op jit(solution)/shard_map/ppermute | solution.py:37
  27.4 2.1 %collective-permute-start.5 = (f32[32,4096]{1,0:T(8,128)S(1)}, f32[32,4096]{1,0:T(8,128)S(1)}, u32[]{:S(2)}, u32[]{:S(2)}) collective-permute-start(f32[32,4096]{1,0:T(8,128)S(1)} %collective-permute-done.1.refs_2_), channel_id=1, source_target_pairs={{0,2},{1,3},{2,0},{3,1},{4,6},{5,7},{6,4},{7,5},{8,10},{9,11},{10,... | collective-permute-start | bytes 1572872 | tf_op jit(solution)/shard_map/ppermute | solution.py:41
  29.5 12.5 %shard_map.64 = (bf16[4,640,1024]{2,1,0:T(8,128)(2,1)}, bf16[4,640,1024]{2,1,0:T(8,128)(2,1)}, f32[640,128]{1,0:T(8,128)S(1)}) custom-call(f32[640,4096]{1,0:T(8,128)} %bitcast.79), custom_call_target="tpu_custom_call" | custom-call | tf_op jit(solution)/shard_map/pallas_call | solution.py:71
  43.4 1.6 collective-permute-start.8
  45.0 3.2 %collective-permute-start.7 = (f32[32,4096]{1,0:T(8,128)S(1)}, f32[32,4096]{1,0:T(8,128)S(1)}, u32[]{:S(2)}, u32[]{:S(2)}) collective-permute-start(f32[32,4096]{1,0:T(8,128)S(1)} %collective-permute-done.3.refs_5_), channel_id=1, source_target_pairs={{0,28},{1,29},{2,30},{3,31},{4,0},{5,1},{6,2},{7,3},{8,4},{9,5},{1... | collective-permute-start | bytes 1572872 | tf_op jit(solution)/shard_map/ppermute | solution.py:37
  49.0 11.3 %shard_map.66.refs_0_ = f32[4,168,384]{2,1,0:T(8,128)S(1)} custom-call(bf16[4,640,1024]{2,1,0:T(8,128)(2,1)} %get-tuple-element.43.hi_ref, bf16[4,640,1024]{2,1,0:T(8,128)(2,1)} %get-tuple-element.44.lo_ref, f32[640,128]{1,0:T(8,128)S(1)} %get-tuple-element.51.refs_0_, f32[192,4096]{1,0:T(8,128)S(1)} %shard_map.65.refs_1_, ...), custom_call_target="tpu_custom_call" | custom-call | flops 6039797760 | bytes 4194304 | tf_op jit(solution)/shard_map/pallas_call | solution.py:139
  61.7 2.4 %collective-permute-start.11 = (f32[32,4096]{1,0:T(8,128)S(1)}, f32[32,4096]{1,0:T(8,128)S(1)}, u32[]{:S(2)}, u32[]{:S(2)}) collective-permute-start(f32[32,4096]{1,0:T(8,128)S(1)} %get-tuple-element.58), channel_id=1, source_target_pairs={{0,28},{1,29},{2,30},{3,31},{4,0},{5,1},{6,2},{7,3},{8,4},{9,5},{1... | collective-permute-start | bytes 1572872 | tf_op jit(solution)/shard_map/ppermute | solution.py:37
  64.1 1.8 %collective-permute-start.12 = (f32[32,4096]{1,0:T(8,128)S(1)}, f32[32,4096]{1,0:T(8,128)S(1)}, u32[]{:S(2)}, u32[]{:S(2)}) collective-permute-start(f32[32,4096]{1,0:T(8,128)S(1)} %get-tuple-element.59), channel_id=1, source_target_pairs={{0,2},{1,3},{2,0},{3,1},{4,6},{5,7},{6,4},{7,5},{8,10},{9,11},{10,... | collective-permute-start | bytes 1572872 | tf_op jit(solution)/shard_map/ppermute | solution.py:41
  65.8 7.5 %shard_map.68 = f32[4,160,256]{2,1,0:T(8,128)S(1)} custom-call(bf16[4,640,1024]{2,1,0:T(8,128)(2,1)} %get-tuple-element.43.hi_ref, bf16[4,640,1024]{2,1,0:T(8,128)(2,1)} %get-tuple-element.44.lo_ref, f32[128,4096]{1,0:T(8,128)S(1)} %get-tuple-element.60.refs_0_, f32[128,4096]{1,0:T(8,128)S(1)} %collective-permute-done.13.refs_1_), custom_call_target="tpu_custom_call" | custom-call | flops 4026531840 | bytes 4194304 | tf_op jit(solution)/shard_map/pallas_call | solution.py:139
  74.2 2.0 %collective-permute-done.10.refs_0_ = f32[32,4096]{1,0:T(8,128)S(1)} collective-permute-done((f32[32,4096]{1,0:T(8,128)S(1)}, f32[32,4096]{1,0:T(8,128)S(1)}, u32[]{:S(2)}, u32[]{:S(2)}) %collective-permute-start.10) | collective-permute-done | bytes 524320 | tf_op jit(solution)/shard_map/ppermute | solution.py:33
  76.2 3.0 %collective-permute-done.12.refs_2_ = f32[32,4096]{1,0:T(8,128)S(1)} collective-permute-done((f32[32,4096]{1,0:T(8,128)S(1)}, f32[32,4096]{1,0:T(8,128)S(1)}, u32[]{:S(2)}, u32[]{:S(2)}) %collective-permute-start.12) | collective-permute-done | bytes 524320 | tf_op jit(solution)/shard_map/ppermute | solution.py:41
  79.2 1.3 shard_map.69
  80.5 3.2 %collective-permute-start.15 = (f32[32,4096]{1,0:T(8,128)}, f32[32,4096]{1,0:T(8,128)}, u32[]{:S(2)}, u32[]{:S(2)}) collective-permute-start(f32[32,4096]{1,0:T(8,128)} %get-tuple-element.66), channel_id=1, source_target_pairs={{0,28},{1,29},{2,30},{3,31},{4,0},{5,1},{6,2},{7,3},{8,4},{9,5},{1... | collective-permute-start | bytes 1572872 | tf_op jit(solution)/shard_map/ppermute | solution.py:37
  83.8 1.8 %collective-permute-start.16 = (f32[32,4096]{1,0:T(8,128)}, f32[32,4096]{1,0:T(8,128)}, u32[]{:S(2)}, u32[]{:S(2)}) collective-permute-start(f32[32,4096]{1,0:T(8,128)} %get-tuple-element.67), channel_id=1, source_target_pairs={{0,2},{1,3},{2,0},{3,1},{4,6},{5,7},{6,4},{7,5},{8,10},{9,11},{10,... | collective-permute-start | bytes 1572872 | tf_op jit(solution)/shard_map/ppermute | solution.py:41
  85.6 4.5 %all-to-all-start = ((f32[4,160,256]{2,1,0:T(8,128)}), f32[4,160,256]{2,1,0:T(8,128)}, u32[]{:S(2)}, u32[]{:S(2)}) async-start(f32[4,160,256]{2,1,0:T(8,128)} %copy-done.3), calls=%async_computation | async-start | bytes 1310720 | tf_op jit(solution)/shard_map/all_to_all | solution.py:154
  91.3 7.4 %shard_map.70 = f32[4,168,512]{2,1,0:T(8,128)S(1)} custom-call(bf16[4,640,1024]{2,1,0:T(8,128)(2,1)} %get-tuple-element.43.hi_ref, bf16[4,640,1024]{2,1,0:T(8,128)(2,1)} %get-tuple-element.44.lo_ref, f32[4,168,384]{2,1,0:T(8,128)S(1)} %copy-done.7, f32[96,4096]{1,0:T(8,128)S(1)} %get-tuple-element.64.refs_1_.refs_0_, ...), custom_call_target="tpu_custom_call" | custom-call | flops 2013265920 | bytes 4194304 | tf_op jit(solution)/shard_map/pallas_call | solution.py:139
  100.9 2.6 %shard_map.71.refs_1_ = f32[96,4096]{1,0:T(8,128)} custom-call(f32[32,4096]{1,0:T(8,128)} %collective-permute-done.14.refs_0_, f32[32,4096]{1,0:T(8,128)} %collective-permute-done.15.refs_1_, f32[32,4096]{1,0:T(8,128)} %collective-permute-done.16.refs_2_), custom_call_target="tpu_custom_call" | custom-call | tf_op jit(solution)/shard_map/pallas_call | solution.py:168
  103.5 4.5 %all-to-all-start.1 = ((f32[4,168,512]{2,1,0:T(8,128)}), f32[4,168,512]{2,1,0:T(8,128)}, u32[]{:S(2)}, u32[]{:S(2)}) async-start(f32[4,168,512]{2,1,0:T(8,128)} %copy-done.1), calls=%async_computation.1 | async-start | bytes 2752512 | tf_op jit(solution)/shard_map/all_to_all | solution.py:154
  108.5 8.0 %shard_map.72 = f32[4,160,256]{2,1,0:T(8,128)S(1)} custom-call(bf16[4,640,1024]{2,1,0:T(8,128)(2,1)} %get-tuple-element.43.hi_ref, bf16[4,640,1024]{2,1,0:T(8,128)(2,1)} %get-tuple-element.44.lo_ref, f32[96,4096]{1,0:T(8,128)S(1)} %get-tuple-element.64.refs_1_.refs_0_, f32[96,4096]{1,0:T(8,128)} %shard_map.71.refs_1_, ...), custom_call_target="tpu_custom_call" | custom-call | flops 4026531840 | bytes 4194304 | tf_op jit(solution)/shard_map/pallas_call | solution.py:139
  117.4 10.1 %all-to-all-done.1.refs_0_ = f32[4,168,512]{2,1,0:T(8,128)} async-done(((f32[4,168,512]{2,1,0:T(8,128)}), f32[4,168,512]{2,1,0:T(8,128)}, u32[]{:S(2)}, u32[]{:S(2)}) %all-to-all-start.1) | async-done | bytes 1376288 | tf_op jit(solution)/shard_map/all_to_all | solution.py:154
  127.5 4.2 %all-to-all-start.2 = ((f32[4,160,256]{2,1,0:T(8,128)}), f32[4,160,256]{2,1,0:T(8,128)}, u32[]{:S(2)}, u32[]{:S(2)}) async-start(f32[4,160,256]{2,1,0:T(8,128)} %copy-done.2), calls=%async_computation.2 | async-start | bytes 1310720 | tf_op jit(solution)/shard_map/all_to_all | solution.py:154
  132.1 2.5 %shard_map.73.refs_1_ = f32[8,168,128]{2,1,0:T(8,128)S(1)} custom-call(s32[1,768]{1,0:T(1,128)S(1)} %broadcast_in_dim.47.dest_ref, f32[4,168,512]{2,1,0:T(8,128)} %all-to-all-done.1.refs_0_, f32[4,160,256]{2,1,0:T(8,128)} %all-to-all-done.refs_1_), custom_call_target="tpu_custom_call" | custom-call | flops 1000000000 | bytes 4194304 | tf_op jit(solution)/shard_map/pallas_call | solution.py:210
  135.5 7.2 %all-to-all-done.2.refs_0_ = f32[4,160,256]{2,1,0:T(8,128)} async-done(((f32[4,160,256]{2,1,0:T(8,128)}), f32[4,160,256]{2,1,0:T(8,128)}, u32[]{:S(2)}, u32[]{:S(2)}) %all-to-all-start.2) | async-done | bytes 655392 | tf_op jit(solution)/shard_map/all_to_all | solution.py:154
  143.7 2.4 %shard_map.74 = f32[8,168,128]{2,1,0:T(8,128)} custom-call(s32[1,256]{1,0:T(1,128)S(1)} %broadcast_in_dim.46.dest_ref, f32[4,160,256]{2,1,0:T(8,128)} %all-to-all-done.2.refs_0_, f32[8,168,128]{2,1,0:T(8,128)S(1)} %copy-done.9), custom_call_target="tpu_custom_call" | custom-call | flops 1000000000 | bytes 4194304 | tf_op jit(solution)/shard_map/pallas_call | solution.py:210
  146.2 4.9 %all-to-all-start.3 = ((f32[8,168,128]{2,1,0:T(8,128)}), f32[8,168,128]{2,1,0:T(8,128)S(1)}, u32[]{:S(2)}, u32[]{:S(2)}) async-start(f32[8,168,128]{2,1,0:T(8,128)} %shard_map.74), calls=%async_computation.3 | async-start | bytes 1376256 | tf_op jit(solution)/shard_map/all_to_all | solution.py:339
  151.3 9.3 %all-to-all-done.3.got_ref = f32[8,168,128]{2,1,0:T(8,128)S(1)} async-done(((f32[8,168,128]{2,1,0:T(8,128)}), f32[8,168,128]{2,1,0:T(8,128)S(1)}, u32[]{:S(2)}, u32[]{:S(2)}) %all-to-all-start.3) | async-done | bytes 688160 | tf_op jit(solution)/shard_map/all_to_all | solution.py:339
  (74 shorter events, 14.1 us)
Async XLA Ops:
  0.0 1.5 copy-start
  0.0 4.6 %copy-start.10 = (f32[1,64,64]{2,1,0:T(8,128)S(1)}, f32[1,64,64]{2,1,0:T(8,128)}, u32[]{:S(2)}) copy-start(f32[1,64,64]{2,1,0:T(8,128)} %param.7) | copy-start | bytes 49156
  6.3 35.7 %copy-start.4 = (f32[32,4096]{1,0:T(8,128)}, f32[32,4096]{1,0:T(8,128)S(1)}, u32[]{:S(2)}) copy-start(f32[32,4096]{1,0:T(8,128)S(1)} %reshape.3004.refs_0_) | copy-start | bytes 1572868
  6.3 17.9 %collective-permute-start = (f32[32,4096]{1,0:T(8,128)S(1)}, f32[32,4096]{1,0:T(8,128)S(1)}, u32[]{:S(2)}, u32[]{:S(2)}) collective-permute-start(f32[32,4096]{1,0:T(8,128)S(1)} %reshape.3004.refs_0_), channel_id=1, source_target_pairs={{0,4},{1,5},{2,6},{3,7},{4,8},{5,9},{6,10},{7,11},{8,12},{9,13},{1... | collective-permute-start | bytes 1572872 | tf_op jit(solution)/shard_map/ppermute | solution.py:33
  8.3 15.9 %collective-permute-start.1 = (f32[32,4096]{1,0:T(8,128)S(1)}, f32[32,4096]{1,0:T(8,128)S(1)}, u32[]{:S(2)}, u32[]{:S(2)}) collective-permute-start(f32[32,4096]{1,0:T(8,128)S(1)} %reshape.3004.refs_0_), channel_id=1, source_target_pairs={{0,28},{1,29},{2,30},{3,31},{4,0},{5,1},{6,2},{7,3},{8,4},{9,5},{1... | collective-permute-start | bytes 1572872 | tf_op jit(solution)/shard_map/ppermute | solution.py:37
  12.3 29.7 %collective-permute-start.4 = (f32[32,4096]{1,0:T(8,128)S(1)}, f32[32,4096]{1,0:T(8,128)S(1)}, u32[]{:S(2)}, u32[]{:S(2)}) collective-permute-start(f32[32,4096]{1,0:T(8,128)S(1)} %reshape.3004.refs_0_), channel_id=1, source_target_pairs={{0,2},{1,3},{2,0},{3,1},{4,6},{5,7},{6,4},{7,5},{8,10},{9,11},{10,... | collective-permute-start | bytes 1572872 | tf_op jit(solution)/shard_map/ppermute | solution.py:41
  24.1 17.9 %collective-permute-start.2 = (f32[32,4096]{1,0:T(8,128)S(1)}, f32[32,4096]{1,0:T(8,128)S(1)}, u32[]{:S(2)}, u32[]{:S(2)}) collective-permute-start(f32[32,4096]{1,0:T(8,128)S(1)} %collective-permute-done.refs_1_), channel_id=1, source_target_pairs={{0,4},{1,5},{2,6},{3,7},{4,8},{5,9},{6,10},{7,11},{8,12},{9,13},{1... | collective-permute-start | bytes 1572872 | tf_op jit(solution)/shard_map/ppermute | solution.py:33
  24.1 17.9 %collective-permute-start.3 = (f32[32,4096]{1,0:T(8,128)S(1)}, f32[32,4096]{1,0:T(8,128)S(1)}, u32[]{:S(2)}, u32[]{:S(2)}) collective-permute-start(f32[32,4096]{1,0:T(8,128)S(1)} %collective-permute-done.1.refs_2_), channel_id=1, source_target_pairs={{0,28},{1,29},{2,30},{3,31},{4,0},{5,1},{6,2},{7,3},{8,4},{9,5},{1... | collective-permute-start | bytes 1572872 | tf_op jit(solution)/shard_map/ppermute | solution.py:37
  27.4 14.6 %collective-permute-start.5 = (f32[32,4096]{1,0:T(8,128)S(1)}, f32[32,4096]{1,0:T(8,128)S(1)}, u32[]{:S(2)}, u32[]{:S(2)}) collective-permute-start(f32[32,4096]{1,0:T(8,128)S(1)} %collective-permute-done.1.refs_2_), channel_id=1, source_target_pairs={{0,2},{1,3},{2,0},{3,1},{4,6},{5,7},{6,4},{7,5},{8,10},{9,11},{10,... | collective-permute-start | bytes 1572872 | tf_op jit(solution)/shard_map/ppermute | solution.py:41
  43.3 5.7 %collective-permute-start.9 = (f32[192,4096]{1,0:T(8,128)S(1)}, f32[192,4096]{1,0:T(8,128)S(1)}, u32[]{:S(2)}, u32[]{:S(2)}) collective-permute-start(f32[192,4096]{1,0:T(8,128)S(1)} %shard_map.65.refs_1_), channel_id=1, source_target_pairs={{0,1},{1,0},{2,3},{3,2},{4,5},{5,4},{6,7},{7,6},{8,9},{9,8},{10,11... | collective-permute-start | bytes 9437192 | tf_op jit(solution)/shard_map/ppermute | solution.py:45
  43.4 17.0 %collective-permute-start.8 = (f32[32,4096]{1,0:T(8,128)S(1)}, f32[32,4096]{1,0:T(8,128)S(1)}, u32[]{:S(2)}, u32[]{:S(2)}) collective-permute-start(f32[32,4096]{1,0:T(8,128)S(1)} %collective-permute-done.refs_1_), channel_id=1, source_target_pairs={{0,2},{1,3},{2,0},{3,1},{4,6},{5,7},{6,4},{7,5},{8,10},{9,11},{10,... | collective-permute-start | bytes 1572872 | tf_op jit(solution)/shard_map/ppermute | solution.py:41
  45.0 15.3 %collective-permute-start.6 = (f32[32,4096]{1,0:T(8,128)S(1)}, f32[32,4096]{1,0:T(8,128)S(1)}, u32[]{:S(2)}, u32[]{:S(2)}) collective-permute-start(f32[32,4096]{1,0:T(8,128)S(1)} %collective-permute-done.2.refs_4_), channel_id=1, source_target_pairs={{0,4},{1,5},{2,6},{3,7},{4,8},{5,9},{6,10},{7,11},{8,12},{9,13},{1... | collective-permute-start | bytes 1572872 | tf_op jit(solution)/shard_map/ppermute | solution.py:33
  45.0 15.4 %collective-permute-start.7 = (f32[32,4096]{1,0:T(8,128)S(1)}, f32[32,4096]{1,0:T(8,128)S(1)}, u32[]{:S(2)}, u32[]{:S(2)}) collective-permute-start(f32[32,4096]{1,0:T(8,128)S(1)} %collective-permute-done.3.refs_5_), channel_id=1, source_target_pairs={{0,28},{1,29},{2,30},{3,31},{4,0},{5,1},{6,2},{7,3},{8,4},{9,5},{1... | collective-permute-start | bytes 1572872 | tf_op jit(solution)/shard_map/ppermute | solution.py:37
  60.3 13.0 %copy-start.6 = (f32[4,168,384]{2,1,0:T(8,128)}, f32[4,168,384]{2,1,0:T(8,128)S(1)}, u32[]{:S(2)}) copy-start(f32[4,168,384]{2,1,0:T(8,128)S(1)} %shard_map.66.refs_0_) | copy-start | bytes 3096580
  60.6 5.2 %collective-permute-start.13 = (f32[128,4096]{1,0:T(8,128)S(1)}, f32[128,4096]{1,0:T(8,128)S(1)}, u32[]{:S(2)}, u32[]{:S(2)}) collective-permute-start(f32[128,4096]{1,0:T(8,128)S(1)} %get-tuple-element.60.refs_0_), channel_id=1, source_target_pairs={{0,1},{1,0},{2,3},{3,2},{4,5},{5,4},{6,7},{7,6},{8,9},{9,8},{10,11... | collective-permute-start | bytes 6291464 | tf_op jit(solution)/shard_map/ppermute | solution.py:45
  60.8 15.4 %collective-permute-start.10 = (f32[32,4096]{1,0:T(8,128)S(1)}, f32[32,4096]{1,0:T(8,128)S(1)}, u32[]{:S(2)}, u32[]{:S(2)}) collective-permute-start(f32[32,4096]{1,0:T(8,128)S(1)} %get-tuple-element.57), channel_id=1, source_target_pairs={{0,4},{1,5},{2,6},{3,7},{4,8},{5,9},{6,10},{7,11},{8,12},{9,13},{1... | collective-permute-start | bytes 1572872 | tf_op jit(solution)/shard_map/ppermute | solution.py:33
  61.7 14.5 %collective-permute-start.11 = (f32[32,4096]{1,0:T(8,128)S(1)}, f32[32,4096]{1,0:T(8,128)S(1)}, u32[]{:S(2)}, u32[]{:S(2)}) collective-permute-start(f32[32,4096]{1,0:T(8,128)S(1)} %get-tuple-element.58), channel_id=1, source_target_pairs={{0,28},{1,29},{2,30},{3,31},{4,0},{5,1},{6,2},{7,3},{8,4},{9,5},{1... | collective-permute-start | bytes 1572872 | tf_op jit(solution)/shard_map/ppermute | solution.py:37
  64.1 15.1 %collective-permute-start.12 = (f32[32,4096]{1,0:T(8,128)S(1)}, f32[32,4096]{1,0:T(8,128)S(1)}, u32[]{:S(2)}, u32[]{:S(2)}) collective-permute-start(f32[32,4096]{1,0:T(8,128)S(1)} %get-tuple-element.59), channel_id=1, source_target_pairs={{0,2},{1,3},{2,0},{3,1},{4,6},{5,7},{6,4},{7,5},{8,10},{9,11},{10,... | collective-permute-start | bytes 1572872 | tf_op jit(solution)/shard_map/ppermute | solution.py:41
  80.5 5.1 %collective-permute-start.17 = (f32[96,4096]{1,0:T(8,128)S(1)}, f32[96,4096]{1,0:T(8,128)S(1)}, u32[]{:S(2)}, u32[]{:S(2)}) collective-permute-start(f32[96,4096]{1,0:T(8,128)S(1)} %get-tuple-element.64.refs_1_.refs_0_), channel_id=1, source_target_pairs={{0,1},{1,0},{2,3},{3,2},{4,5},{5,4},{6,7},{7,6},{8,9},{9,8},{10,11... | collective-permute-start | bytes 4718600 | tf_op jit(solution)/shard_map/ppermute | solution.py:45
  80.5 19.2 %collective-permute-start.14 = (f32[32,4096]{1,0:T(8,128)}, f32[32,4096]{1,0:T(8,128)}, u32[]{:S(2)}, u32[]{:S(2)}) collective-permute-start(f32[32,4096]{1,0:T(8,128)} %get-tuple-element.65), channel_id=1, source_target_pairs={{0,4},{1,5},{2,6},{3,7},{4,8},{5,9},{6,10},{7,11},{8,12},{9,13},{1... | collective-permute-start | bytes 1572872 | tf_op jit(solution)/shard_map/ppermute | solution.py:33
  80.5 19.2 %collective-permute-start.15 = (f32[32,4096]{1,0:T(8,128)}, f32[32,4096]{1,0:T(8,128)}, u32[]{:S(2)}, u32[]{:S(2)}) collective-permute-start(f32[32,4096]{1,0:T(8,128)} %get-tuple-element.66), channel_id=1, source_target_pairs={{0,28},{1,29},{2,30},{3,31},{4,0},{5,1},{6,2},{7,3},{8,4},{9,5},{1... | collective-permute-start | bytes 1572872 | tf_op jit(solution)/shard_map/ppermute | solution.py:37
  83.8 16.0 %collective-permute-start.16 = (f32[32,4096]{1,0:T(8,128)}, f32[32,4096]{1,0:T(8,128)}, u32[]{:S(2)}, u32[]{:S(2)}) collective-permute-start(f32[32,4096]{1,0:T(8,128)} %get-tuple-element.67), channel_id=1, source_target_pairs={{0,2},{1,3},{2,0},{3,1},{4,6},{5,7},{6,4},{7,5},{8,10},{9,11},{10,... | collective-permute-start | bytes 1572872 | tf_op jit(solution)/shard_map/ppermute | solution.py:41
  85.6 15.3 %all-to-all-start = ((f32[4,160,256]{2,1,0:T(8,128)}), f32[4,160,256]{2,1,0:T(8,128)}, u32[]{:S(2)}, u32[]{:S(2)}) async-start(f32[4,160,256]{2,1,0:T(8,128)} %copy-done.3), calls=%async_computation | async-start | bytes 1310720 | tf_op jit(solution)/shard_map/all_to_all | solution.py:154
  90.1 1.2 copy-start.7
  98.7 1.1 copy-start.1
  103.5 4.9 %copy-start.11 = (s32[32]{0:T(128)S(1)}, s32[32]{0:T(128)}, u32[]{:S(2)}) copy-start(s32[32]{0:T(128)} %param.10) | copy-start | bytes 388
  103.5 5.0 %collective-permute-start.18 = (f32[96,4096]{1,0:T(8,128)}, f32[96,4096]{1,0:T(8,128)}, u32[]{:S(2)}, u32[]{:S(2)}) collective-permute-start(f32[96,4096]{1,0:T(8,128)} %shard_map.71.refs_1_), channel_id=1, source_target_pairs={{0,1},{1,0},{2,3},{3,2},{4,5},{5,4},{6,7},{7,6},{8,9},{9,8},{10,11... | collective-permute-start | bytes 4718600 | tf_op jit(solution)/shard_map/ppermute | solution.py:45
  103.5 24.0 %all-to-all-start.1 = ((f32[4,168,512]{2,1,0:T(8,128)}), f32[4,168,512]{2,1,0:T(8,128)}, u32[]{:S(2)}, u32[]{:S(2)}) async-start(f32[4,168,512]{2,1,0:T(8,128)} %copy-done.1), calls=%async_computation.1 | async-start | bytes 2752512 | tf_op jit(solution)/shard_map/all_to_all | solution.py:154
  127.5 15.1 %all-to-all-start.2 = ((f32[4,160,256]{2,1,0:T(8,128)}), f32[4,160,256]{2,1,0:T(8,128)}, u32[]{:S(2)}, u32[]{:S(2)}) async-start(f32[4,160,256]{2,1,0:T(8,128)} %copy-done.2), calls=%async_computation.2 | async-start | bytes 1310720 | tf_op jit(solution)/shard_map/all_to_all | solution.py:154
  142.6 1.1 copy-start.9
  143.7 7.3 %copy-start.12 = (s32[32]{0:T(128)S(1)}, s32[32]{0:T(128)}, u32[]{:S(2)}) copy-start(s32[32]{0:T(128)} %param.11) | copy-start | bytes 388
  146.2 14.4 %all-to-all-start.3 = ((f32[8,168,128]{2,1,0:T(8,128)}), f32[8,168,128]{2,1,0:T(8,128)S(1)}, u32[]{:S(2)}, u32[]{:S(2)}) async-start(f32[8,168,128]{2,1,0:T(8,128)} %shard_map.74), calls=%async_computation.3 | async-start | bytes 1376256 | tf_op jit(solution)/shard_map/all_to_all | solution.py:339
  (4 other events, 3.6 us)

commit v3 on v2

--- a/solution.py
+++ b/solution.py
@@ -82,12 +82,10 @@
     )(pltpu.with_memory_space_constraint(grads, pltpu.HBM))
 
 
-def score_kernel(spans, squares, prior, hi_ref, lo_ref, *refs):
-    sq_ref = old_ref = None
+def score_kernel(spans, squares, hi_ref, lo_ref, *refs):
+    sq_ref = None
     if squares:
         sq_ref, *refs = refs
-    if prior:
-        old_ref, *refs = refs
     pieces = refs[: len(spans)]
     out_ref, acc = refs[len(spans) :]
     step = pl.program_id(0)
@@ -107,43 +105,36 @@
 
     @pl.when(step == pl.num_programs(0) - 1)
     def _():
-        emit(sq_ref, old_ref, acc, out_ref)
-
-
-def emit(sq_ref, old_ref, acc, out_ref):
+        emit(sq_ref, acc, out_ref)
+
+
+def emit(sq_ref, acc, out_ref):
     count = acc.shape[0] // NY
-    at = out_ref.shape[2] - acc.shape[1]
     for k in range(NY):
         here = slice(k * count, (k + 1) * count)
-        out_ref[k, 0:count, at:] = acc[here, :]
-        if old_ref is not None:
-            out_ref[k, :, 0:at] = old_ref[k]
-            out_ref[k, count:, at:] = jnp.zeros((out_ref.shape[1] - count, acc.shape[1]), jnp.float32)
+        out_ref[k, 0:count, :] = acc[here, :]
         if sq_ref is not None:
             out_ref[k, count:, :] = jnp.zeros((8, out_ref.shape[2]), jnp.float32)
             out_ref[k, count:, 0:count] = jnp.transpose(sq_ref[here, 0:8])
 
 
-def scores_of(grads, pieces, squares=None, prior=None):
+def scores_of(grads, pieces, squares=None):
     hi, lo = (pltpu.with_memory_space_constraint(g, pltpu.HBM) for g in grads)
     steps, rows, wide = hi.shape
     spans = [(first, first + count) for _, first, count in pieces]
     width = sum(count for _, _, count in pieces)
     slice_rows = rows // NY + (0 if squares is None else 8)
-    if prior is not None:
-        slice_rows = prior.shape[1]
     whole = pl.BlockSpec(memory_space=pltpu.VMEM)
-    extra = [v for v in (squares, prior) if v is not None]
-    full = width + (0 if prior is None else prior.shape[2])
+    extra = [] if squares is None else [squares]
     flops = 6 * rows * width * steps * wide
     return pl.pallas_call(
-        functools.partial(score_kernel, spans, squares is not None, prior is not None),
+        functools.partial(score_kernel, spans, squares is not None),
         grid=(steps,),
         in_specs=[pl.BlockSpec((1, rows, wide), lambda i: (i, 0, 0))] * 2
         + [whole] * len(extra)
         + [pl.BlockSpec((p[0].shape[0], wide), lambda i: (0, i)) for p in pieces],
         out_specs=whole,
-        out_shape=jax.ShapeDtypeStruct((NY, slice_rows, full), jnp.float32),
+        out_shape=jax.ShapeDtypeStruct((NY, slice_rows, width), jnp.float32),
         scratch_shapes=[pltpu.VMEM((rows, width), jnp.float32)],
         compiler_params=pltpu.CompilerParams(vmem_limit_bytes=VMEM_LIMIT),
         cost_estimate=pl.CostEstimate(flops=flops, bytes_accessed=4 * 1024 * 1024, transcendentals=0),
@@ -249,7 +240,6 @@
 
 
 def shards(train_grads, left_factor, right_factor, queries, owners, range_start):
-    highest = lax.Precision.HIGHEST
     nmods = lax.axis_size("mod")
     nblk = lax.axis_size("blk")
     rows_dev = train_grads.shape[1]
@@ -264,8 +254,8 @@
     z, h, c = b // 4, (b // 2) % 2, b % 2
 
     mats = queries[0].reshape(qblock, side, side)
-    mats = jnp.einsum("rad,cd->rac", mats, right_factor[0], precision=highest)
-    mats = jnp.einsum("ba,rac->rbc", left_factor[0], mats, precision=highest)
+    mats = jnp.einsum("rad,cd->rac", mats, right_factor[0], precision=lax.Precision.HIGH)
+    mats = jnp.einsum("ba,rac->rbc", left_factor[0], mats, precision=lax.Precision.HIGH)
     own = mats.reshape(qblock, feat)
 
     own, grads = fence(own, grads)
@@ -284,45 +274,46 @@
     hi, lo, squares = split_grads(grads)
     a2m, a2p, e0, e1p, squares = fence(a2m, a2p, e0, e1p, squares)
     a3m, a3p, e1m = up(a2m), down(a2p), far(a1m)
-    (near,) = pack([own, a1m, a1p, e0, a2m, a2p], [(k, 0, size) for k in range(6)])
+    (near,) = pack([own, a1m, a1p, e0], [(k, 0, size) for k in range(4)])
     near_c = other(near)
-    ids((0, 0), (-1, 0), (1, 0), (0, 1), (-2, 0), (2, 0))
-    part0 = scores_of((hi, lo), [(near, 0, 6 * size), (near_c, 0, 6 * size)], squares)
+    ids((0, 0), (-1, 0), (1, 0), (0, 1))
+    part0 = scores_of((hi, lo), [(near, 0, 4 * size), (near_c, 0, 4 * size)], squares)
     a3m, a3p, e1m, part0 = fence(a3m, a3p, e1m, part0)
     for_up, for_down, for_far, three = pack(
-        [a3m, a3p, e1m, e1p],
+        [a3m, a3p, e1m, e1p, a2m, a2p],
         [(0, 0, half), (2, 0, half)],
         [(1, half, half), (3, 0, half)],
         [(1, half, half), (0, half, half)],
-        [(k, 0, size) for k in range(4)],
+        [(4, 0, size), (5, 0, size), (2, 0, size), (3, 0, size)],
     )
     up4, down4, far4 = up(for_up), down(for_down), far(for_far)
-    three_c = other(three)
-    ids((-3, 0), (3, 0), (-1, 1), (1, 1))
+    three_c, part0 = fence(other(three), part0)
+    got0 = over_y(part0)
+    ids((-2, 0), (2, 0), (-1, 1), (1, 1))
     part1 = scores_of((hi, lo), [(three, 0, 4 * size), (three_c, 0, 4 * size)])
-    up4, down4, far4, part1 = fence(up4, down4, far4, part1)
+    up4, down4, far4, part1, got0 = fence(up4, down4, far4, part1, got0)
     for_up, for_down, for_far, four = pack(
-        [up4, down4, far4, e1m, e1p],
+        [up4, down4, far4, e1m, e1p, a3m, a3p],
         [(3, half, half), (0, half, half)],
         [(4, half, half), (1, half, half)],
         [(0, 0, half), (1, 0, half)],
-        [(k, 0, size) for k in range(3)],
+        [(k, 0, size) for k in (5, 6, 0, 1, 2)],
     )
     up5, down5, far5 = up(for_up), down(for_down), far(for_far)
     four_c, part1 = fence(other(four), part1)
     got1 = over_y(part1)
-    ids((4, 0, 0), (-2, 1, 0), (4, 0, 1), (2, 1, 0))
-    part02 = scores_of((hi, lo), [(four, 0, 2 * size), (four_c, 0, 2 * size)], prior=part0)
-    up5, down5, far5, part02, got1 = fence(up5, down5, far5, part02, got1)
+    ids((-3, 0), (3, 0), (4, 0, 0), (-2, 1, 0), (4, 0, 1), (2, 1, 0))
+    part2 = scores_of((hi, lo), [(four, 0, 4 * size), (four_c, 0, 4 * size)])
+    up5, down5, far5, part2, got1 = fence(up5, down5, far5, part2, got1)
     (five,) = pack([up5, down5, far5], [(k, 0, size) for k in range(3)])
     five_c = other(five)
-    got02 = over_y(part02)
+    got2 = over_y(part2)
     ids((3, 1, 1), (-3, 1, 1), (-2, 1, 1), (-3, 1, 0), (2, 1, 1), (3, 1, 0), (4, 1, 0), (4, 1, 1))
     part3 = scores_of(
         (hi, lo),
-        [(four, 2 * size, size), (five, 0, 3 * size), (four_c, 2 * size, size), (five_c, 0, 3 * size)],
-    )
-    part3, got02 = fence(part3, got02)
+        [(four, 4 * size, size), (five, 0, 3 * size), (four_c, 4 * size, size), (five_c, 0, 3 * size)],
+    )
+    part3, got2 = fence(part3, got2)
     got3 = over_y(part3)
 
     source = jnp.stack(halves).astype(jnp.int32)
@@ -330,11 +321,9 @@
     target = jnp.sum(jnp.where((source // 2)[:, None] == blocks[None, :], owners[None, :], 0), axis=1)
     dest = ((target * 2 + source % 2) * half)[:, None] + jnp.arange(half, dtype=jnp.int32)[None, :]
     dest = dest.reshape(-1)
-    ends = (part0.shape[2], part0.shape[2] + part1.shape[2], part02.shape[2] + part1.shape[2])
-    early = ends[2]
-    first_dest = jnp.concatenate([dest[: ends[0]], dest[ends[1] : early], dest[ends[0] : ends[1]]])
-    groups, rows = dest.shape[0] // 128, got02.shape[1]
-    placed = place(groups, first_dest, [got02, got1], rows)
+    early = got0.shape[2] + got1.shape[2] + got2.shape[2]
+    groups, rows = dest.shape[0] // 128, got0.shape[1]
+    placed = place(groups, dest[:early], [got0, got1, got2], rows)
     placed = place(groups, dest[early:], [got3], rows, [placed])
     got = lax.all_to_all(placed, "mod", 0, 0)
     out_block = m * (nblk // nmods) + jnp.arange(placed.shape[2], dtype=jnp.int32) // qblock

time: 162 us -> 161 us (level)
  waiting for transfers between devices: 43.3 us -> 35.5 us
  local copies, waits for them, and re-layouts: 9.71 us -> 14.6 us
  starting transfers between devices: 46.8 us -> 49.1 us
  matrix products: 4.07 us -> 2.19 us
    all_to_all x3 -> x4, waiting for transfers between devices: 18.4 us -> 12.3 us  [over_y(): return lax.all_to_all(slices, 'mod', 0, 0, axis_index_groups=Y_GROUPS)]
    unnamed x26 -> x30, local copies, waits for them, and re-layouts: 6.97 us -> 12 us
    all_to_all x3 -> x4, starting transfers between devices: 13.1 us -> 15.7 us  [over_y(): return lax.all_to_all(slices, 'mod', 0, 0, axis_index_groups=Y_GROUPS)]
    pallas_call x4, Pallas kernels: 4.38 us -> 6.76 us  [pack(): pl.pallas_call(functools.partial(pack_kernel, plans), in_specs=[whole] *...]
    dot_general x2, matrix products: 4.07 us -> 2.19 us  [the longest x1 1.62 us: shards(): jnp.einsum('rad,cd->rac', mats, right_factor[0], precision=lax.Precision....]
  transfers between devices with their start and end apart: 23 -> 24, of which waited for: 8 -> 9; matrix products, arithmetic and copies ran while one was open for 1% -> 0% of each run, Pallas kernels for 30% -> 31%
where the time goes in v3:
time: 161 us; the launch traced here: 160 us
  Pallas kernels  57.8 us (36%)
  starting transfers between devices  49.1 us (30%)
  waiting for transfers between devices  35.5 us (22%)
  local copies, waits for them, and re-layouts  14.6 us (9%)
  matrix products  2.19 us (1%)
    pallas_call x4, Pallas kernels, scores_of(): pl.pallas_call(functools.partial(score_kernel, spans, squares is not None...  34 us
    all_to_all x4, starting transfers between devices, over_y(): return lax.all_to_all(slices, 'mod', 0, 0, axis_index_groups=Y_GROUPS)  15.7 us
    ppermute x5, starting transfers between devices, down(): return lax.ppermute(block, 'blk', Z_DOWN)  15.6 us
    pallas_call x1, Pallas kernels, split_grads(): pl.pallas_call(split_kernel, grid=(rows // 64,), in_specs=[pl.BlockSpec((...  12.5 us
    all_to_all x4, waiting for transfers between devices, over_y(): return lax.all_to_all(slices, 'mod', 0, 0, axis_index_groups=Y_GROUPS)  12.3 us
    unnamed x30, local copies, waits for them, and re-layouts  12 us
    ppermute x5, waiting for transfers between devices, up(): return lax.ppermute(block, 'blk', Z_UP)  10.7 us
    all_to_all x1, waiting for transfers between devices, shards(): got = lax.all_to_all(placed, 'mod', 0, 0)  9.74 us
  transfers between devices with their start and end apart: 24, of which 9 were waited for; matrix products, arithmetic and copies ran while one was open for 0% of the time, Pallas kernels for 31%

profile of v3, /device:TPU:2, one launch (start us, length us, event | category | flops | bytes accessed | tf_op | source)
XLA Modules:
  0.0 159.6 jit_solution(16119454493433460440)
XLA Ops:
  1.5 1.6 %fusion.1 = f32[32,64,64]{1,2,0:T(8,128)S(1)} fusion(f32[32,64,64]{2,1,0:T(8,128)S(1)} %reshape_squeeze.3, f32[1,64,64]{2,1,0:T(8,128)S(1)} %copy-done), kind=kOutput, calls=%fused_computation.2 | convolution fusion | flops 50331648 | bytes 1064960 | tf_op jit(solution)/shard_map/rad,cd->rac/dot_general | solution.py:257
  4.4 2.0 %collective-permute-start = (f32[32,4096]{1,0:T(8,128)S(1)}, f32[32,4096]{1,0:T(8,128)S(1)}, u32[]{:S(2)}, u32[]{:S(2)}) collective-permute-start(f32[32,4096]{1,0:T(8,128)S(1)} %reshape.3003.refs_0_), channel_id=1, source_target_pairs={{0,4},{1,5},{2,6},{3,7},{4,8},{5,9},{6,10},{7,11},{8,12},{9,13},{1... | collective-permute-start | bytes 1572872 | tf_op jit(solution)/shard_map/ppermute | solution.py:33
  6.4 4.0 %collective-permute-start.1 = (f32[32,4096]{1,0:T(8,128)S(1)}, f32[32,4096]{1,0:T(8,128)S(1)}, u32[]{:S(2)}, u32[]{:S(2)}) collective-permute-start(f32[32,4096]{1,0:T(8,128)S(1)} %reshape.3003.refs_0_), channel_id=1, source_target_pairs={{0,28},{1,29},{2,30},{3,31},{4,0},{5,1},{6,2},{7,3},{8,4},{9,5},{1... | collective-permute-start | bytes 1572872 | tf_op jit(solution)/shard_map/ppermute | solution.py:37
  10.4 2.1 %collective-permute-start.4 = (f32[32,4096]{1,0:T(8,128)S(1)}, f32[32,4096]{1,0:T(8,128)S(1)}, u32[]{:S(2)}, u32[]{:S(2)}) collective-permute-start(f32[32,4096]{1,0:T(8,128)S(1)} %reshape.3003.refs_0_), channel_id=1, source_target_pairs={{0,2},{1,3},{2,0},{3,1},{4,6},{5,7},{6,4},{7,5},{8,10},{9,11},{10,... | collective-permute-start | bytes 1572872 | tf_op jit(solution)/shard_map/ppermute | solution.py:41
  12.5 9.7 %collective-permute-done.refs_1_ = f32[32,4096]{1,0:T(8,128)S(1)} collective-permute-done((f32[32,4096]{1,0:T(8,128)S(1)}, f32[32,4096]{1,0:T(8,128)S(1)}, u32[]{:S(2)}, u32[]{:S(2)}) %collective-permute-start) | collective-permute-done | bytes 524320 | tf_op jit(solution)/shard_map/ppermute | solution.py:33
  22.2 3.2 %collective-permute-start.3 = (f32[32,4096]{1,0:T(8,128)S(1)}, f32[32,4096]{1,0:T(8,128)S(1)}, u32[]{:S(2)}, u32[]{:S(2)}) collective-permute-start(f32[32,4096]{1,0:T(8,128)S(1)} %collective-permute-done.1.refs_2_), channel_id=1, source_target_pairs={{0,28},{1,29},{2,30},{3,31},{4,0},{5,1},{6,2},{7,3},{8,4},{9,5},{1... | collective-permute-start | bytes 1572872 | tf_op jit(solution)/shard_map/ppermute | solution.py:37
  25.5 2.1 %collective-permute-start.5 = (f32[32,4096]{1,0:T(8,128)S(1)}, f32[32,4096]{1,0:T(8,128)S(1)}, u32[]{:S(2)}, u32[]{:S(2)}) collective-permute-start(f32[32,4096]{1,0:T(8,128)S(1)} %collective-permute-done.1.refs_2_), channel_id=1, source_target_pairs={{0,2},{1,3},{2,0},{3,1},{4,6},{5,7},{6,4},{7,5},{8,10},{9,11},{10,... | collective-permute-start | bytes 1572872 | tf_op jit(solution)/shard_map/ppermute | solution.py:41
  27.6 12.5 %shard_map.64 = (bf16[4,640,1024]{2,1,0:T(8,128)(2,1)}, bf16[4,640,1024]{2,1,0:T(8,128)(2,1)}, f32[640,128]{1,0:T(8,128)S(1)}) custom-call(f32[640,4096]{1,0:T(8,128)} %bitcast.79), custom_call_target="tpu_custom_call" | custom-call | tf_op jit(solution)/shard_map/pallas_call | solution.py:71
  40.4 1.6 %collective-permute-start.8 = (f32[32,4096]{1,0:T(8,128)S(1)}, f32[32,4096]{1,0:T(8,128)S(1)}, u32[]{:S(2)}, u32[]{:S(2)}) collective-permute-start(f32[32,4096]{1,0:T(8,128)S(1)} %collective-permute-done.refs_1_), channel_id=1, source_target_pairs={{0,2},{1,3},{2,0},{3,1},{4,6},{5,7},{6,4},{7,5},{8,10},{9,11},{10,... | collective-permute-start | bytes 1572872 | tf_op jit(solution)/shard_map/ppermute | solution.py:41
  42.0 3.2 %collective-permute-start.7 = (f32[32,4096]{1,0:T(8,128)S(1)}, f32[32,4096]{1,0:T(8,128)S(1)}, u32[]{:S(2)}, u32[]{:S(2)}) collective-permute-start(f32[32,4096]{1,0:T(8,128)S(1)} %collective-permute-done.3.refs_5_), channel_id=1, source_target_pairs={{0,28},{1,29},{2,30},{3,31},{4,0},{5,1},{6,2},{7,3},{8,4},{9,5},{1... | collective-permute-start | bytes 1572872 | tf_op jit(solution)/shard_map/ppermute | solution.py:37
  45.2 8.4 %shard_map.66 = f32[4,168,256]{2,1,0:T(8,128)} custom-call(bf16[4,640,1024]{2,1,0:T(8,128)(2,1)} %get-tuple-element.46.hi_ref, bf16[4,640,1024]{2,1,0:T(8,128)(2,1)} %get-tuple-element.47.lo_ref, f32[640,128]{1,0:T(8,128)S(1)} %get-tuple-element.54.refs_0_, f32[128,4096]{1,0:T(8,128)S(1)} %shard_map.65.refs_1_, f32[128,4096]{1,0:T(8,128)S(1)} %collective-permute-done.9.refs_2_), custom_call_target="tpu_custom_call" | custom-call | flops 4026531840 | bytes 4194304 | tf_op jit(solution)/shard_map/pallas_call | solution.py:130
  53.7 2.5 %collective-permute-done.8.refs_2_.refs_3_ = f32[32,4096]{1,0:T(8,128)S(1)} collective-permute-done((f32[32,4096]{1,0:T(8,128)S(1)}, f32[32,4096]{1,0:T(8,128)S(1)}, u32[]{:S(2)}, u32[]{:S(2)}) %collective-permute-start.8) | collective-permute-done | bytes 524320 | tf_op jit(solution)/shard_map/ppermute | solution.py:41
  60.5 2.2 %collective-permute-start.11 = (f32[32,4096]{1,0:T(8,128)}, f32[32,4096]{1,0:T(8,128)}, u32[]{:S(2)}, u32[]{:S(2)}) collective-permute-start(f32[32,4096]{1,0:T(8,128)} %get-tuple-element.61), channel_id=1, source_target_pairs={{0,28},{1,29},{2,30},{3,31},{4,0},{5,1},{6,2},{7,3},{8,4},{9,5},{1... | collective-permute-start | bytes 1572872 | tf_op jit(solution)/shard_map/ppermute | solution.py:37
  62.7 2.0 %collective-permute-start.12 = (f32[32,4096]{1,0:T(8,128)}, f32[32,4096]{1,0:T(8,128)}, u32[]{:S(2)}, u32[]{:S(2)}) collective-permute-start(f32[32,4096]{1,0:T(8,128)} %get-tuple-element.62), channel_id=1, source_target_pairs={{0,2},{1,3},{2,0},{3,1},{4,6},{5,7},{6,4},{7,5},{8,10},{9,11},{10,... | collective-permute-start | bytes 1572872 | tf_op jit(solution)/shard_map/ppermute | solution.py:41
  66.1 4.5 %all-to-all-start = ((f32[4,168,256]{2,1,0:T(8,128)}), f32[4,168,256]{2,1,0:T(8,128)}, u32[]{:S(2)}, u32[]{:S(2)}) async-start(f32[4,168,256]{2,1,0:T(8,128)} %shard_map.66), calls=%async_computation | async-start | bytes 1376256 | tf_op jit(solution)/shard_map/all_to_all | solution.py:145
  70.5 1.6 copy-done.11
  72.1 8.4 %shard_map.68 = f32[4,160,256]{2,1,0:T(8,128)} custom-call(bf16[4,640,1024]{2,1,0:T(8,128)(2,1)} %get-tuple-element.46.hi_ref, bf16[4,640,1024]{2,1,0:T(8,128)(2,1)} %get-tuple-element.47.lo_ref, f32[128,4096]{1,0:T(8,128)S(1)} %get-tuple-element.63.refs_0_, f32[128,4096]{1,0:T(8,128)S(1)} %copy-done.11), custom_call_target="tpu_custom_call" | custom-call | flops 4026531840 | bytes 4194304 | tf_op jit(solution)/shard_map/pallas_call | solution.py:130
  84.8 2.6 %shard_map.69 = (f32[32,4096]{1,0:T(8,128)}, f32[32,4096]{1,0:T(8,128)}, f32[32,4096]{1,0:T(8,128)}, f32[160,4096]{1,0:T(8,128)S(1)}) custom-call(f32[32,4096]{1,0:T(8,128)} %collective-permute-done.10.refs_0_, f32[32,4096]{1,0:T(8,128)} %collective-permute-done.11.refs_1_, f32[32,4096]{1,0:T(8,128)} %collective-permute-done.12.refs_2_, ...), custom_call_target="tpu_custom_call" | custom-call | tf_op jit(solution)/shard_map/pallas_call | solution.py:159
  87.8 2.8 %collective-permute-start.15 = (f32[32,4096]{1,0:T(8,128)}, f32[32,4096]{1,0:T(8,128)}, u32[]{:S(2)}, u32[]{:S(2)}) collective-permute-start(f32[32,4096]{1,0:T(8,128)} %get-tuple-element.72), channel_id=1, source_target_pairs={{0,28},{1,29},{2,30},{3,31},{4,0},{5,1},{6,2},{7,3},{8,4},{9,5},{1... | collective-permute-start | bytes 1572872 | tf_op jit(solution)/shard_map/ppermute | solution.py:37
  92.3 1.6 copy-done.1
  93.9 3.6 %all-to-all-start.1 = ((f32[4,160,256]{2,1,0:T(8,128)}), f32[4,160,256]{2,1,0:T(8,128)S(1)}, u32[]{:S(2)}, u32[]{:S(2)}) async-start(f32[4,160,256]{2,1,0:T(8,128)} %shard_map.68), calls=%async_computation.1 | async-start | bytes 1310720 | tf_op jit(solution)/shard_map/all_to_all | solution.py:145
  97.5 1.7 %copy-done.2 = f32[160,4096]{1,0:T(8,128)S(1)} copy-done((f32[160,4096]{1,0:T(8,128)S(1)}, f32[160,4096]{1,0:T(8,128)}, u32[]{:S(2)}) %copy-start.2) | copy-done | bytes 2621464
  99.2 8.4 %shard_map.70 = f32[4,160,256]{2,1,0:T(8,128)} custom-call(bf16[4,640,1024]{2,1,0:T(8,128)(2,1)} %get-tuple-element.46.hi_ref, bf16[4,640,1024]{2,1,0:T(8,128)(2,1)} %get-tuple-element.47.lo_ref, f32[160,4096]{1,0:T(8,128)S(1)} %get-tuple-element.70.refs_0_, f32[160,4096]{1,0:T(8,128)S(1)} %copy-done.2), custom_call_target="tpu_custom_call" | custom-call | flops 4026531840 | bytes 4194304 | tf_op jit(solution)/shard_map/pallas_call | solution.py:130
  108.8 2.6 %shard_map.71.refs_1_ = f32[96,4096]{1,0:T(8,128)} custom-call(f32[32,4096]{1,0:T(8,128)} %collective-permute-done.14.refs_0_, f32[32,4096]{1,0:T(8,128)} %collective-permute-done.15.refs_1_, f32[32,4096]{1,0:T(8,128)} %collective-permute-done.16.refs_2_), custom_call_target="tpu_custom_call" | custom-call | tf_op jit(solution)/shard_map/pallas_call | solution.py:159
  111.6 4.2 %all-to-all-start.2 = ((f32[4,160,256]{2,1,0:T(8,128)}), f32[4,160,256]{2,1,0:T(8,128)}, u32[]{:S(2)}, u32[]{:S(2)}) async-start(f32[4,160,256]{2,1,0:T(8,128)} %shard_map.70), calls=%async_computation.2 | async-start | bytes 1310720 | tf_op jit(solution)/shard_map/all_to_all | solution.py:145
  115.9 1.7 %copy-done.3 = f32[160,4096]{1,0:T(8,128)S(1)} copy-done((f32[160,4096]{1,0:T(8,128)S(1)}, f32[160,4096]{1,0:T(8,128)}, u32[]{:S(2)}) %copy-start.3) | copy-done | bytes 2621464
  117.6 8.8 %shard_map.72 = f32[4,160,256]{2,1,0:T(8,128)} custom-call(bf16[4,640,1024]{2,1,0:T(8,128)(2,1)} %get-tuple-element.46.hi_ref, bf16[4,640,1024]{2,1,0:T(8,128)(2,1)} %get-tuple-element.47.lo_ref, f32[160,4096]{1,0:T(8,128)S(1)} %get-tuple-element.70.refs_0_, f32[96,4096]{1,0:T(8,128)} %shard_map.71.refs_1_, f32[160,4096]{1,0:T(8,128)S(1)} %copy-done.3, ...), custom_call_target="tpu_custom_call" | custom-call | flops 4026531840 | bytes 4194304 | tf_op jit(solution)/shard_map/pallas_call | solution.py:130
  127.7 3.5 %all-to-all-start.3 = ((f32[4,160,256]{2,1,0:T(8,128)}), f32[4,160,256]{2,1,0:T(8,128)S(1)}, u32[]{:S(2)}, u32[]{:S(2)}) async-start(f32[4,160,256]{2,1,0:T(8,128)} %shard_map.72), calls=%async_computation.3 | async-start | bytes 1310720 | tf_op jit(solution)/shard_map/all_to_all | solution.py:145
  131.4 2.3 %shard_map.73.refs_1_ = f32[8,168,128]{2,1,0:T(8,128)S(1)} custom-call(s32[1,768]{1,0:T(1,128)S(1)} %broadcast_in_dim.47.dest_ref, f32[4,168,256]{2,1,0:T(8,128)} %all-to-all-done.refs_0_, f32[4,160,256]{2,1,0:T(8,128)S(1)} %all-to-all-done.1.refs_1_, f32[4,160,256]{2,1,0:T(8,128)} %all-to-all-done.2.refs_2_), custom_call_target="tpu_custom_call" | custom-call | flops 1000000000 | bytes 4194304 | tf_op jit(solution)/shard_map/pallas_call | solution.py:201
  133.7 8.7 %all-to-all-done.3.refs_0_ = f32[4,160,256]{2,1,0:T(8,128)S(1)} async-done(((f32[4,160,256]{2,1,0:T(8,128)}), f32[4,160,256]{2,1,0:T(8,128)S(1)}, u32[]{:S(2)}, u32[]{:S(2)}) %all-to-all-start.3) | async-done | bytes 655392 | tf_op jit(solution)/shard_map/all_to_all | solution.py:145
  143.7 4.9 %all-to-all-start.4 = ((f32[8,168,128]{2,1,0:T(8,128)}), f32[8,168,128]{2,1,0:T(8,128)S(1)}, u32[]{:S(2)}, u32[]{:S(2)}) async-start(f32[8,168,128]{2,1,0:T(8,128)} %shard_map.74), calls=%async_computation.4 | async-start | bytes 1376256 | tf_op jit(solution)/shard_map/all_to_all | solution.py:328
  148.9 9.7 %all-to-all-done.4.got_ref = f32[8,168,128]{2,1,0:T(8,128)S(1)} async-done(((f32[8,168,128]{2,1,0:T(8,128)}), f32[8,168,128]{2,1,0:T(8,128)S(1)}, u32[]{:S(2)}, u32[]{:S(2)}) %all-to-all-start.4) | async-done | bytes 688160 | tf_op jit(solution)/shard_map/all_to_all | solution.py:328
  (75 shorter events, 20.4 us)
Async XLA Ops:
  0.0 3.1 %copy-start.12 = (f32[1,64,64]{2,1,0:T(8,128)S(1)}, f32[1,64,64]{2,1,0:T(8,128)}, u32[]{:S(2)}) copy-start(f32[1,64,64]{2,1,0:T(8,128)} %param.7) | copy-start | bytes 49156
  4.4 17.9 %collective-permute-start = (f32[32,4096]{1,0:T(8,128)S(1)}, f32[32,4096]{1,0:T(8,128)S(1)}, u32[]{:S(2)}, u32[]{:S(2)}) collective-permute-start(f32[32,4096]{1,0:T(8,128)S(1)} %reshape.3003.refs_0_), channel_id=1, source_target_pairs={{0,4},{1,5},{2,6},{3,7},{4,8},{5,9},{6,10},{7,11},{8,12},{9,13},{1... | collective-permute-start | bytes 1572872 | tf_op jit(solution)/shard_map/ppermute | solution.py:33
  6.4 15.9 %collective-permute-start.1 = (f32[32,4096]{1,0:T(8,128)S(1)}, f32[32,4096]{1,0:T(8,128)S(1)}, u32[]{:S(2)}, u32[]{:S(2)}) collective-permute-start(f32[32,4096]{1,0:T(8,128)S(1)} %reshape.3003.refs_0_), channel_id=1, source_target_pairs={{0,28},{1,29},{2,30},{3,31},{4,0},{5,1},{6,2},{7,3},{8,4},{9,5},{1... | collective-permute-start | bytes 1572872 | tf_op jit(solution)/shard_map/ppermute | solution.py:37
  10.4 29.7 %collective-permute-start.4 = (f32[32,4096]{1,0:T(8,128)S(1)}, f32[32,4096]{1,0:T(8,128)S(1)}, u32[]{:S(2)}, u32[]{:S(2)}) collective-permute-start(f32[32,4096]{1,0:T(8,128)S(1)} %reshape.3003.refs_0_), channel_id=1, source_target_pairs={{0,2},{1,3},{2,0},{3,1},{4,6},{5,7},{6,4},{7,5},{8,10},{9,11},{10,... | collective-permute-start | bytes 1572872 | tf_op jit(solution)/shard_map/ppermute | solution.py:41
  22.2 17.9 %collective-permute-start.2 = (f32[32,4096]{1,0:T(8,128)S(1)}, f32[32,4096]{1,0:T(8,128)S(1)}, u32[]{:S(2)}, u32[]{:S(2)}) collective-permute-start(f32[32,4096]{1,0:T(8,128)S(1)} %collective-permute-done.refs_1_), channel_id=1, source_target_pairs={{0,4},{1,5},{2,6},{3,7},{4,8},{5,9},{6,10},{7,11},{8,12},{9,13},{1... | collective-permute-start | bytes 1572872 | tf_op jit(solution)/shard_map/ppermute | solution.py:33
  22.2 17.9 %collective-permute-start.3 = (f32[32,4096]{1,0:T(8,128)S(1)}, f32[32,4096]{1,0:T(8,128)S(1)}, u32[]{:S(2)}, u32[]{:S(2)}) collective-permute-start(f32[32,4096]{1,0:T(8,128)S(1)} %collective-permute-done.1.refs_2_), channel_id=1, source_target_pairs={{0,28},{1,29},{2,30},{3,31},{4,0},{5,1},{6,2},{7,3},{8,4},{9,5},{1... | collective-permute-start | bytes 1572872 | tf_op jit(solution)/shard_map/ppermute | solution.py:37
  25.5 14.6 %collective-permute-start.5 = (f32[32,4096]{1,0:T(8,128)S(1)}, f32[32,4096]{1,0:T(8,128)S(1)}, u32[]{:S(2)}, u32[]{:S(2)}) collective-permute-start(f32[32,4096]{1,0:T(8,128)S(1)} %collective-permute-done.1.refs_2_), channel_id=1, source_target_pairs={{0,2},{1,3},{2,0},{3,1},{4,6},{5,7},{6,4},{7,5},{8,10},{9,11},{10,... | collective-permute-start | bytes 1572872 | tf_op jit(solution)/shard_map/ppermute | solution.py:41
  40.3 5.0 %collective-permute-start.9 = (f32[128,4096]{1,0:T(8,128)S(1)}, f32[128,4096]{1,0:T(8,128)S(1)}, u32[]{:S(2)}, u32[]{:S(2)}) collective-permute-start(f32[128,4096]{1,0:T(8,128)S(1)} %shard_map.65.refs_1_), channel_id=1, source_target_pairs={{0,1},{1,0},{2,3},{3,2},{4,5},{5,4},{6,7},{7,6},{8,9},{9,8},{10,11... | collective-permute-start | bytes 6291464 | tf_op jit(solution)/shard_map/ppermute | solution.py:45
  40.4 15.8 %collective-permute-start.8 = (f32[32,4096]{1,0:T(8,128)S(1)}, f32[32,4096]{1,0:T(8,128)S(1)}, u32[]{:S(2)}, u32[]{:S(2)}) collective-permute-start(f32[32,4096]{1,0:T(8,128)S(1)} %collective-permute-done.refs_1_), channel_id=1, source_target_pairs={{0,2},{1,3},{2,0},{3,1},{4,6},{5,7},{6,4},{7,5},{8,10},{9,11},{10,... | collective-permute-start | bytes 1572872 | tf_op jit(solution)/shard_map/ppermute | solution.py:41
  42.0 15.2 %collective-permute-start.6 = (f32[32,4096]{1,0:T(8,128)S(1)}, f32[32,4096]{1,0:T(8,128)S(1)}, u32[]{:S(2)}, u32[]{:S(2)}) collective-permute-start(f32[32,4096]{1,0:T(8,128)S(1)} %collective-permute-done.2.refs_4_), channel_id=1, source_target_pairs={{0,4},{1,5},{2,6},{3,7},{4,8},{5,9},{6,10},{7,11},{8,12},{9,13},{1... | collective-permute-start | bytes 1572872 | tf_op jit(solution)/shard_map/ppermute | solution.py:33
  42.0 15.2 %collective-permute-start.7 = (f32[32,4096]{1,0:T(8,128)S(1)}, f32[32,4096]{1,0:T(8,128)S(1)}, u32[]{:S(2)}, u32[]{:S(2)}) collective-permute-start(f32[32,4096]{1,0:T(8,128)S(1)} %collective-permute-done.3.refs_5_), channel_id=1, source_target_pairs={{0,28},{1,29},{2,30},{3,31},{4,0},{5,1},{6,2},{7,3},{8,4},{9,5},{1... | collective-permute-start | bytes 1572872 | tf_op jit(solution)/shard_map/ppermute | solution.py:37
  57.2 8.9 %copy-start.8 = (f32[32,4096]{1,0:T(8,128)}, f32[32,4096]{1,0:T(8,128)S(1)}, u32[]{:S(2)}) copy-start(f32[32,4096]{1,0:T(8,128)S(1)} %collective-permute-done.7.refs_1_.refs_6_) | copy-start | bytes 1572868
  59.4 5.2 %collective-permute-start.13 = (f32[128,4096]{1,0:T(8,128)S(1)}, f32[128,4096]{1,0:T(8,128)S(1)}, u32[]{:S(2)}, u32[]{:S(2)}) collective-permute-start(f32[128,4096]{1,0:T(8,128)S(1)} %get-tuple-element.63.refs_0_), channel_id=1, source_target_pairs={{0,1},{1,0},{2,3},{3,2},{4,5},{5,4},{6,7},{7,6},{8,9},{9,8},{10,11... | collective-permute-start | bytes 6291464 | tf_op jit(solution)/shard_map/ppermute | solution.py:45
  59.4 21.0 %collective-permute-start.10 = (f32[32,4096]{1,0:T(8,128)}, f32[32,4096]{1,0:T(8,128)}, u32[]{:S(2)}, u32[]{:S(2)}) collective-permute-start(f32[32,4096]{1,0:T(8,128)} %get-tuple-element.60), channel_id=1, source_target_pairs={{0,4},{1,5},{2,6},{3,7},{4,8},{5,9},{6,10},{7,11},{8,12},{9,13},{1... | collective-permute-start | bytes 1572872 | tf_op jit(solution)/shard_map/ppermute | solution.py:33
  60.5 20.0 %collective-permute-start.11 = (f32[32,4096]{1,0:T(8,128)}, f32[32,4096]{1,0:T(8,128)}, u32[]{:S(2)}, u32[]{:S(2)}) collective-permute-start(f32[32,4096]{1,0:T(8,128)} %get-tuple-element.61), channel_id=1, source_target_pairs={{0,28},{1,29},{2,30},{3,31},{4,0},{5,1},{6,2},{7,3},{8,4},{9,5},{1... | collective-permute-start | bytes 1572872 | tf_op jit(solution)/shard_map/ppermute | solution.py:37
  62.7 17.8 %collective-permute-start.12 = (f32[32,4096]{1,0:T(8,128)}, f32[32,4096]{1,0:T(8,128)}, u32[]{:S(2)}, u32[]{:S(2)}) collective-permute-start(f32[32,4096]{1,0:T(8,128)} %get-tuple-element.62), channel_id=1, source_target_pairs={{0,2},{1,3},{2,0},{3,1},{4,6},{5,7},{6,4},{7,5},{8,10},{9,11},{10,... | collective-permute-start | bytes 1572872 | tf_op jit(solution)/shard_map/ppermute | solution.py:41
  66.1 15.6 %all-to-all-start = ((f32[4,168,256]{2,1,0:T(8,128)}), f32[4,168,256]{2,1,0:T(8,128)}, u32[]{:S(2)}, u32[]{:S(2)}) async-start(f32[4,168,256]{2,1,0:T(8,128)} %shard_map.66), calls=%async_computation | async-start | bytes 1376256 | tf_op jit(solution)/shard_map/all_to_all | solution.py:145
  70.5 1.6 copy-start.11
  87.4 4.9 %collective-permute-start.17 = (f32[160,4096]{1,0:T(8,128)S(1)}, f32[160,4096]{1,0:T(8,128)S(1)}, u32[]{:S(2)}, u32[]{:S(2)}) collective-permute-start(f32[160,4096]{1,0:T(8,128)S(1)} %get-tuple-element.70.refs_0_), channel_id=1, source_target_pairs={{0,1},{1,0},{2,3},{3,2},{4,5},{5,4},{6,7},{7,6},{8,9},{9,8},{10,11... | collective-permute-start | bytes 7864328 | tf_op jit(solution)/shard_map/ppermute | solution.py:45
  87.4 20.2 %collective-permute-start.14 = (f32[32,4096]{1,0:T(8,128)}, f32[32,4096]{1,0:T(8,128)}, u32[]{:S(2)}, u32[]{:S(2)}) collective-permute-start(f32[32,4096]{1,0:T(8,128)} %get-tuple-element.71), channel_id=1, source_target_pairs={{0,4},{1,5},{2,6},{3,7},{4,8},{5,9},{6,10},{7,11},{8,12},{9,13},{1... | collective-permute-start | bytes 1572872 | tf_op jit(solution)/shard_map/ppermute | solution.py:33
  87.8 19.8 %collective-permute-start.15 = (f32[32,4096]{1,0:T(8,128)}, f32[32,4096]{1,0:T(8,128)}, u32[]{:S(2)}, u32[]{:S(2)}) collective-permute-start(f32[32,4096]{1,0:T(8,128)} %get-tuple-element.72), channel_id=1, source_target_pairs={{0,28},{1,29},{2,30},{3,31},{4,0},{5,1},{6,2},{7,3},{8,4},{9,5},{1... | collective-permute-start | bytes 1572872 | tf_op jit(solution)/shard_map/ppermute | solution.py:37
  90.6 17.0 %collective-permute-start.16 = (f32[32,4096]{1,0:T(8,128)}, f32[32,4096]{1,0:T(8,128)}, u32[]{:S(2)}, u32[]{:S(2)}) collective-permute-start(f32[32,4096]{1,0:T(8,128)} %get-tuple-element.73), channel_id=1, source_target_pairs={{0,2},{1,3},{2,0},{3,1},{4,6},{5,7},{6,4},{7,5},{8,10},{9,11},{10,... | collective-permute-start | bytes 1572872 | tf_op jit(solution)/shard_map/ppermute | solution.py:41
  92.3 1.6 copy-start.1
  93.9 14.9 %all-to-all-start.1 = ((f32[4,160,256]{2,1,0:T(8,128)}), f32[4,160,256]{2,1,0:T(8,128)S(1)}, u32[]{:S(2)}, u32[]{:S(2)}) async-start(f32[4,160,256]{2,1,0:T(8,128)} %shard_map.68), calls=%async_computation.1 | async-start | bytes 1310720 | tf_op jit(solution)/shard_map/all_to_all | solution.py:145
  97.5 1.7 %copy-start.2 = (f32[160,4096]{1,0:T(8,128)S(1)}, f32[160,4096]{1,0:T(8,128)}, u32[]{:S(2)}) copy-start(f32[160,4096]{1,0:T(8,128)} %copy-done.1) | copy-start | bytes 7864324
  107.6 8.2 %copy-start.13 = (s32[32]{0:T(128)S(1)}, s32[32]{0:T(128)}, u32[]{:S(2)}) copy-start(s32[32]{0:T(128)} %param.10) | copy-start | bytes 388
  111.4 4.4 %collective-permute-start.18 = (f32[96,4096]{1,0:T(8,128)}, f32[96,4096]{1,0:T(8,128)}, u32[]{:S(2)}, u32[]{:S(2)}) collective-permute-start(f32[96,4096]{1,0:T(8,128)} %shard_map.71.refs_1_), channel_id=1, source_target_pairs={{0,1},{1,0},{2,3},{3,2},{4,5},{5,4},{6,7},{7,6},{8,9},{9,8},{10,11... | collective-permute-start | bytes 4718600 | tf_op jit(solution)/shard_map/ppermute | solution.py:45
  111.6 16.1 %all-to-all-start.2 = ((f32[4,160,256]{2,1,0:T(8,128)}), f32[4,160,256]{2,1,0:T(8,128)}, u32[]{:S(2)}, u32[]{:S(2)}) async-start(f32[4,160,256]{2,1,0:T(8,128)} %shard_map.70), calls=%async_computation.2 | async-start | bytes 1310720 | tf_op jit(solution)/shard_map/all_to_all | solution.py:145
  115.9 1.7 %copy-start.3 = (f32[160,4096]{1,0:T(8,128)S(1)}, f32[160,4096]{1,0:T(8,128)}, u32[]{:S(2)}) copy-start(f32[160,4096]{1,0:T(8,128)} %copy-done.1) | copy-start | bytes 7864324
  127.7 14.8 %all-to-all-start.3 = ((f32[4,160,256]{2,1,0:T(8,128)}), f32[4,160,256]{2,1,0:T(8,128)S(1)}, u32[]{:S(2)}, u32[]{:S(2)}) async-start(f32[4,160,256]{2,1,0:T(8,128)} %shard_map.72), calls=%async_computation.3 | async-start | bytes 1310720 | tf_op jit(solution)/shard_map/all_to_all | solution.py:145
  133.7 15.0 %copy-start.14 = (s32[32]{0:T(128)S(1)}, s32[32]{0:T(128)}, u32[]{:S(2)}) copy-start(s32[32]{0:T(128)} %param.11) | copy-start | bytes 388
  143.7 14.9 %all-to-all-start.4 = ((f32[8,168,128]{2,1,0:T(8,128)}), f32[8,168,128]{2,1,0:T(8,128)S(1)}, u32[]{:S(2)}, u32[]{:S(2)}) async-start(f32[8,168,128]{2,1,0:T(8,128)} %shard_map.74), calls=%async_computation.4 | async-start | bytes 1376256 | tf_op jit(solution)/shard_map/all_to_all | solution.py:328
  (7 other events, 8.2 us)

commit v4 on v3

--- a/solution.py
+++ b/solution.py
@@ -254,8 +254,8 @@
     z, h, c = b // 4, (b // 2) % 2, b % 2
 
     mats = queries[0].reshape(qblock, side, side)
-    mats = jnp.einsum("rad,cd->rac", mats, right_factor[0], precision=lax.Precision.HIGH)
-    mats = jnp.einsum("ba,rac->rbc", left_factor[0], mats, precision=lax.Precision.HIGH)
+    mats = jnp.einsum("rad,cd->rac", mats, right_factor[0], precision=lax.Precision.HIGHEST)
+    mats = jnp.einsum("ba,rac->rbc", left_factor[0], mats, precision=lax.Precision.HIGHEST)
     own = mats.reshape(qblock, feat)
 
     own, grads = fence(own, grads)
@@ -287,7 +287,8 @@
         [(4, 0, size), (5, 0, size), (2, 0, size), (3, 0, size)],
     )
     up4, down4, far4 = up(for_up), down(for_down), far(for_far)
-    three_c, part0 = fence(other(three), part0)
+    three_c = other(three)
+    part0 = fence(three_c[:8, :128], part0)[1]
     got0 = over_y(part0)
     ids((-2, 0), (2, 0), (-1, 1), (1, 1))
     part1 = scores_of((hi, lo), [(three, 0, 4 * size), (three_c, 0, 4 * size)])
@@ -300,7 +301,8 @@
         [(k, 0, size) for k in (5, 6, 0, 1, 2)],
     )
     up5, down5, far5 = up(for_up), down(for_down), far(for_far)
-    four_c, part1 = fence(other(four), part1)
+    four_c = other(four)
+    part1 = fence(four_c[:8, :128], part1)[1]
     got1 = over_y(part1)
     ids((-3, 0), (3, 0), (4, 0, 0), (-2, 1, 0), (4, 0, 1), (2, 1, 0))
     part2 = scores_of((hi, lo), [(four, 0, 4 * size), (four_c, 0, 4 * size)])

time: 161 us -> 158 us (0.981)
  local copies, waits for them, and re-layouts: 14.6 us -> 6.51 us
  waiting for transfers between devices: 35.5 us -> 38.5 us
  matrix products: 2.19 us -> 4.07 us
    unnamed x30 -> x20, local copies, waits for them, and re-layouts: 12 us -> 3.94 us
    all_to_all x4, waiting for transfers between devices: 12.3 us -> 15.8 us  [over_y(): return lax.all_to_all(slices, 'mod', 0, 0, axis_index_groups=Y_GROUPS)]
  transfers between devices with their start and end apart: 24 -> 24, of which waited for: 9 -> 8; matrix products, arithmetic and copies ran while one was open for 0% -> 0% of each run, Pallas kernels for 31% -> 32%
where the time goes in v4:
time: 158 us; the launch traced here: 157 us
  Pallas kernels  58.7 us (37%)
  starting transfers between devices  49 us (31%)
  waiting for transfers between devices  38.5 us (24%)
  local copies, waits for them, and re-layouts  6.51 us (4%)
  matrix products  4.07 us (3%)
    pallas_call x4, Pallas kernels, scores_of(): pl.pallas_call(functools.partial(score_kernel, spans, squares is not None...  35 us
    ppermute x5, starting transfers between devices, down(): return lax.ppermute(block, 'blk', Z_DOWN)  15.8 us
    all_to_all x4, waiting for transfers between devices, over_y(): return lax.all_to_all(slices, 'mod', 0, 0, axis_index_groups=Y_GROUPS)  15.8 us
    all_to_all x4, starting transfers between devices, over_y(): return lax.all_to_all(slices, 'mod', 0, 0, axis_index_groups=Y_GROUPS)  15.6 us
    pallas_call x1, Pallas kernels, split_grads(): pl.pallas_call(split_kernel, grid=(rows // 64,), in_specs=[pl.BlockSpec((...  12.5 us
    ppermute x5, waiting for transfers between devices, up(): return lax.ppermute(block, 'blk', Z_UP)  10.6 us
    all_to_all x1, waiting for transfers between devices, shards(): got = lax.all_to_all(placed, 'mod', 0, 0)  9.47 us
    ppermute x5, starting transfers between devices, far(): return lax.ppermute(block, 'blk', X_FAR)  9.37 us
  transfers between devices with their start and end apart: 24, of which 8 were waited for; matrix products, arithmetic and copies ran while one was open for 0% of the time, Pallas kernels for 32%

profile of v4, /device:TPU:2, one launch (start us, length us, event | category | flops | bytes accessed | tf_op | source)
XLA Modules:
  0.0 157.3 jit_solution(3458396646351503387)
XLA Ops:
  1.5 3.1 %fusion.1 = f32[32,64,64]{1,2,0:T(8,128)S(1)} fusion(f32[32,64,64]{2,1,0:T(8,128)S(1)} %reshape_squeeze.3, f32[1,64,64]{2,1,0:T(8,128)S(1)} %copy-done), kind=kOutput, calls=%fused_computation.2 | convolution fusion | flops 100663296 | bytes 1064960 | tf_op jit(solution)/shard_map/rad,cd->rac/dot_general | solution.py:257
  6.3 2.0 %collective-permute-start = (f32[32,4096]{1,0:T(8,128)S(1)}, f32[32,4096]{1,0:T(8,128)S(1)}, u32[]{:S(2)}, u32[]{:S(2)}) collective-permute-start(f32[32,4096]{1,0:T(8,128)S(1)} %reshape.3003.refs_0_), channel_id=1, source_target_pairs={{0,4},{1,5},{2,6},{3,7},{4,8},{5,9},{6,10},{7,11},{8,12},{9,13},{1... | collective-permute-start | bytes 1572872 | tf_op jit(solution)/shard_map/ppermute | solution.py:33
  8.3 4.0 %collective-permute-start.1 = (f32[32,4096]{1,0:T(8,128)S(1)}, f32[32,4096]{1,0:T(8,128)S(1)}, u32[]{:S(2)}, u32[]{:S(2)}) collective-permute-start(f32[32,4096]{1,0:T(8,128)S(1)} %reshape.3003.refs_0_), channel_id=1, source_target_pairs={{0,28},{1,29},{2,30},{3,31},{4,0},{5,1},{6,2},{7,3},{8,4},{9,5},{1... | collective-permute-start | bytes 1572872 | tf_op jit(solution)/shard_map/ppermute | solution.py:37
  12.3 2.1 %collective-permute-start.4 = (f32[32,4096]{1,0:T(8,128)S(1)}, f32[32,4096]{1,0:T(8,128)S(1)}, u32[]{:S(2)}, u32[]{:S(2)}) collective-permute-start(f32[32,4096]{1,0:T(8,128)S(1)} %reshape.3003.refs_0_), channel_id=1, source_target_pairs={{0,2},{1,3},{2,0},{3,1},{4,6},{5,7},{6,4},{7,5},{8,10},{9,11},{10,... | collective-permute-start | bytes 1572872 | tf_op jit(solution)/shard_map/ppermute | solution.py:41
  14.4 9.7 %collective-permute-done.refs_1_ = f32[32,4096]{1,0:T(8,128)S(1)} collective-permute-done((f32[32,4096]{1,0:T(8,128)S(1)}, f32[32,4096]{1,0:T(8,128)S(1)}, u32[]{:S(2)}, u32[]{:S(2)}) %collective-permute-start) | collective-permute-done | bytes 524320 | tf_op jit(solution)/shard_map/ppermute | solution.py:33
  24.1 3.2 %collective-permute-start.3 = (f32[32,4096]{1,0:T(8,128)S(1)}, f32[32,4096]{1,0:T(8,128)S(1)}, u32[]{:S(2)}, u32[]{:S(2)}) collective-permute-start(f32[32,4096]{1,0:T(8,128)S(1)} %collective-permute-done.1.refs_2_), channel_id=1, source_target_pairs={{0,28},{1,29},{2,30},{3,31},{4,0},{5,1},{6,2},{7,3},{8,4},{9,5},{1... | collective-permute-start | bytes 1572872 | tf_op jit(solution)/shard_map/ppermute | solution.py:37
  27.4 2.1 %collective-permute-start.5 = (f32[32,4096]{1,0:T(8,128)S(1)}, f32[32,4096]{1,0:T(8,128)S(1)}, u32[]{:S(2)}, u32[]{:S(2)}) collective-permute-start(f32[32,4096]{1,0:T(8,128)S(1)} %collective-permute-done.1.refs_2_), channel_id=1, source_target_pairs={{0,2},{1,3},{2,0},{3,1},{4,6},{5,7},{6,4},{7,5},{8,10},{9,11},{10,... | collective-permute-start | bytes 1572872 | tf_op jit(solution)/shard_map/ppermute | solution.py:41
  29.5 12.5 %shard_map.64 = (bf16[4,640,1024]{2,1,0:T(8,128)(2,1)}, bf16[4,640,1024]{2,1,0:T(8,128)(2,1)}, f32[640,128]{1,0:T(8,128)S(1)}) custom-call(f32[640,4096]{1,0:T(8,128)} %bitcast.79), custom_call_target="tpu_custom_call" | custom-call | tf_op jit(solution)/shard_map/pallas_call | solution.py:71
  42.3 1.6 %collective-permute-start.8 = (f32[32,4096]{1,0:T(8,128)S(1)}, f32[32,4096]{1,0:T(8,128)S(1)}, u32[]{:S(2)}, u32[]{:S(2)}) collective-permute-start(f32[32,4096]{1,0:T(8,128)S(1)} %collective-permute-done.refs_1_), channel_id=1, source_target_pairs={{0,2},{1,3},{2,0},{3,1},{4,6},{5,7},{6,4},{7,5},{8,10},{9,11},{10,... | collective-permute-start | bytes 1572872 | tf_op jit(solution)/shard_map/ppermute | solution.py:41
  43.9 3.2 %collective-permute-start.7 = (f32[32,4096]{1,0:T(8,128)S(1)}, f32[32,4096]{1,0:T(8,128)S(1)}, u32[]{:S(2)}, u32[]{:S(2)}) collective-permute-start(f32[32,4096]{1,0:T(8,128)S(1)} %collective-permute-done.3.refs_5_), channel_id=1, source_target_pairs={{0,28},{1,29},{2,30},{3,31},{4,0},{5,1},{6,2},{7,3},{8,4},{9,5},{1... | collective-permute-start | bytes 1572872 | tf_op jit(solution)/shard_map/ppermute | solution.py:37
  47.1 8.4 %shard_map.66 = f32[4,168,256]{2,1,0:T(8,128)} custom-call(bf16[4,640,1024]{2,1,0:T(8,128)(2,1)} %get-tuple-element.42.hi_ref, bf16[4,640,1024]{2,1,0:T(8,128)(2,1)} %get-tuple-element.43.lo_ref, f32[640,128]{1,0:T(8,128)S(1)} %get-tuple-element.50.refs_0_, f32[128,4096]{1,0:T(8,128)S(1)} %shard_map.65.refs_1_, f32[128,4096]{1,0:T(8,128)S(1)} %collective-permute-done.9.refs_2_), custom_call_target="tpu_custom_call" | custom-call | flops 4026531840 | bytes 4194304 | tf_op jit(solution)/shard_map/pallas_call | solution.py:130
  55.5 2.6 %collective-permute-done.8.refs_2_.refs_3_ = f32[32,4096]{1,0:T(8,128)S(1)} collective-permute-done((f32[32,4096]{1,0:T(8,128)S(1)}, f32[32,4096]{1,0:T(8,128)S(1)}, u32[]{:S(2)}, u32[]{:S(2)}) %collective-permute-start.8) | collective-permute-done | bytes 524320 | tf_op jit(solution)/shard_map/ppermute | solution.py:41
  62.4 2.1 %collective-permute-start.11 = (f32[32,4096]{1,0:T(8,128)}, f32[32,4096]{1,0:T(8,128)}, u32[]{:S(2)}, u32[]{:S(2)}) collective-permute-start(f32[32,4096]{1,0:T(8,128)} %get-tuple-element.57), channel_id=1, source_target_pairs={{0,28},{1,29},{2,30},{3,31},{4,0},{5,1},{6,2},{7,3},{8,4},{9,5},{1... | collective-permute-start | bytes 1572872 | tf_op jit(solution)/shard_map/ppermute | solution.py:37
  64.5 2.0 %collective-permute-start.12 = (f32[32,4096]{1,0:T(8,128)}, f32[32,4096]{1,0:T(8,128)}, u32[]{:S(2)}, u32[]{:S(2)}) collective-permute-start(f32[32,4096]{1,0:T(8,128)} %get-tuple-element.58), channel_id=1, source_target_pairs={{0,2},{1,3},{2,0},{3,1},{4,6},{5,7},{6,4},{7,5},{8,10},{9,11},{10,... | collective-permute-start | bytes 1572872 | tf_op jit(solution)/shard_map/ppermute | solution.py:41
  66.5 4.5 %all-to-all-start = ((f32[4,168,256]{2,1,0:T(8,128)}), f32[4,168,256]{2,1,0:T(8,128)}, u32[]{:S(2)}, u32[]{:S(2)}) async-start(f32[4,168,256]{2,1,0:T(8,128)} %shard_map.66), calls=%async_computation | async-start | bytes 1376256 | tf_op jit(solution)/shard_map/all_to_all | solution.py:145
  71.0 8.6 %shard_map.68 = f32[4,160,256]{2,1,0:T(8,128)} custom-call(bf16[4,640,1024]{2,1,0:T(8,128)(2,1)} %get-tuple-element.42.hi_ref, bf16[4,640,1024]{2,1,0:T(8,128)(2,1)} %get-tuple-element.43.lo_ref, f32[128,4096]{1,0:T(8,128)S(1)} %get-tuple-element.59.refs_0_, f32[128,4096]{1,0:T(8,128)} %collective-permute-done.13.refs_1_), custom_call_target="tpu_custom_call" | custom-call | flops 4026531840 | bytes 4194304 | tf_op jit(solution)/shard_map/pallas_call | solution.py:130
  79.6 2.6 %all-to-all-done.refs_0_ = f32[4,168,256]{2,1,0:T(8,128)} async-done(((f32[4,168,256]{2,1,0:T(8,128)}), f32[4,168,256]{2,1,0:T(8,128)}, u32[]{:S(2)}, u32[]{:S(2)}) %all-to-all-start) | async-done | bytes 688160 | tf_op jit(solution)/shard_map/all_to_all | solution.py:145
  85.3 2.6 %shard_map.69 = (f32[32,4096]{1,0:T(8,128)}, f32[32,4096]{1,0:T(8,128)}, f32[32,4096]{1,0:T(8,128)}, f32[160,4096]{1,0:T(8,128)S(1)}) custom-call(f32[32,4096]{1,0:T(8,128)} %collective-permute-done.10.refs_0_, f32[32,4096]{1,0:T(8,128)} %collective-permute-done.11.refs_1_, f32[32,4096]{1,0:T(8,128)} %collective-permute-done.12.refs_2_, ...), custom_call_target="tpu_custom_call" | custom-call | tf_op jit(solution)/shard_map/pallas_call | solution.py:159
  87.9 3.2 %collective-permute-start.15 = (f32[32,4096]{1,0:T(8,128)}, f32[32,4096]{1,0:T(8,128)}, u32[]{:S(2)}, u32[]{:S(2)}) collective-permute-start(f32[32,4096]{1,0:T(8,128)} %get-tuple-element.66), channel_id=1, source_target_pairs={{0,28},{1,29},{2,30},{3,31},{4,0},{5,1},{6,2},{7,3},{8,4},{9,5},{1... | collective-permute-start | bytes 1572872 | tf_op jit(solution)/shard_map/ppermute | solution.py:37
  91.1 1.5 collective-permute-start.16
  92.6 3.5 %all-to-all-start.1 = ((f32[4,160,256]{2,1,0:T(8,128)}), f32[4,160,256]{2,1,0:T(8,128)S(1)}, u32[]{:S(2)}, u32[]{:S(2)}) async-start(f32[4,160,256]{2,1,0:T(8,128)} %shard_map.68), calls=%async_computation.1 | async-start | bytes 1310720 | tf_op jit(solution)/shard_map/all_to_all | solution.py:145
  96.1 8.7 %shard_map.70 = f32[4,160,256]{2,1,0:T(8,128)} custom-call(bf16[4,640,1024]{2,1,0:T(8,128)(2,1)} %get-tuple-element.42.hi_ref, bf16[4,640,1024]{2,1,0:T(8,128)(2,1)} %get-tuple-element.43.lo_ref, f32[160,4096]{1,0:T(8,128)S(1)} %get-tuple-element.64.refs_0_, f32[160,4096]{1,0:T(8,128)} %collective-permute-done.17.refs_1_.refs_2_), custom_call_target="tpu_custom_call" | custom-call | flops 4026531840 | bytes 4194304 | tf_op jit(solution)/shard_map/pallas_call | solution.py:130
  104.8 2.2 %all-to-all-done.1.refs_1_ = f32[4,160,256]{2,1,0:T(8,128)S(1)} async-done(((f32[4,160,256]{2,1,0:T(8,128)}), f32[4,160,256]{2,1,0:T(8,128)S(1)}, u32[]{:S(2)}, u32[]{:S(2)}) %all-to-all-start.1) | async-done | bytes 655392 | tf_op jit(solution)/shard_map/all_to_all | solution.py:145
  107.1 2.6 %shard_map.71.refs_1_ = f32[96,4096]{1,0:T(8,128)} custom-call(f32[32,4096]{1,0:T(8,128)} %collective-permute-done.14.refs_0_, f32[32,4096]{1,0:T(8,128)} %collective-permute-done.15.refs_1_, f32[32,4096]{1,0:T(8,128)} %collective-permute-done.16.refs_2_), custom_call_target="tpu_custom_call" | custom-call | tf_op jit(solution)/shard_map/pallas_call | solution.py:159
  109.8 4.2 %all-to-all-start.2 = ((f32[4,160,256]{2,1,0:T(8,128)}), f32[4,160,256]{2,1,0:T(8,128)}, u32[]{:S(2)}, u32[]{:S(2)}) async-start(f32[4,160,256]{2,1,0:T(8,128)} %shard_map.70), calls=%async_computation.2 | async-start | bytes 1310720 | tf_op jit(solution)/shard_map/all_to_all | solution.py:145
  114.2 9.2 %shard_map.72 = f32[4,160,256]{2,1,0:T(8,128)} custom-call(bf16[4,640,1024]{2,1,0:T(8,128)(2,1)} %get-tuple-element.42.hi_ref, bf16[4,640,1024]{2,1,0:T(8,128)(2,1)} %get-tuple-element.43.lo_ref, f32[160,4096]{1,0:T(8,128)S(1)} %get-tuple-element.64.refs_0_, f32[96,4096]{1,0:T(8,128)} %shard_map.71.refs_1_, ...), custom_call_target="tpu_custom_call" | custom-call | flops 4026531840 | bytes 4194304 | tf_op jit(solution)/shard_map/pallas_call | solution.py:130
  123.3 2.6 %all-to-all-done.2.refs_2_ = f32[4,160,256]{2,1,0:T(8,128)} async-done(((f32[4,160,256]{2,1,0:T(8,128)}), f32[4,160,256]{2,1,0:T(8,128)}, u32[]{:S(2)}, u32[]{:S(2)}) %all-to-all-start.2) | async-done | bytes 655392 | tf_op jit(solution)/shard_map/all_to_all | solution.py:145
  125.9 3.5 %all-to-all-start.3 = ((f32[4,160,256]{2,1,0:T(8,128)}), f32[4,160,256]{2,1,0:T(8,128)S(1)}, u32[]{:S(2)}, u32[]{:S(2)}) async-start(f32[4,160,256]{2,1,0:T(8,128)} %shard_map.72), calls=%async_computation.3 | async-start | bytes 1310720 | tf_op jit(solution)/shard_map/all_to_all | solution.py:145
  129.7 2.3 %shard_map.73.refs_1_ = f32[8,168,128]{2,1,0:T(8,128)S(1)} custom-call(s32[1,768]{1,0:T(1,128)S(1)} %broadcast_in_dim.47.dest_ref, f32[4,168,256]{2,1,0:T(8,128)} %all-to-all-done.refs_0_, f32[4,160,256]{2,1,0:T(8,128)S(1)} %all-to-all-done.1.refs_1_, f32[4,160,256]{2,1,0:T(8,128)} %all-to-all-done.2.refs_2_), custom_call_target="tpu_custom_call" | custom-call | flops 1000000000 | bytes 4194304 | tf_op jit(solution)/shard_map/pallas_call | solution.py:201
  132.0 8.5 %all-to-all-done.3.refs_0_ = f32[4,160,256]{2,1,0:T(8,128)S(1)} async-done(((f32[4,160,256]{2,1,0:T(8,128)}), f32[4,160,256]{2,1,0:T(8,128)S(1)}, u32[]{:S(2)}, u32[]{:S(2)}) %all-to-all-start.3) | async-done | bytes 655392 | tf_op jit(solution)/shard_map/all_to_all | solution.py:145
  141.8 4.9 %all-to-all-start.4 = ((f32[8,168,128]{2,1,0:T(8,128)}), f32[8,168,128]{2,1,0:T(8,128)S(1)}, u32[]{:S(2)}, u32[]{:S(2)}) async-start(f32[8,168,128]{2,1,0:T(8,128)} %shard_map.74), calls=%async_computation.4 | async-start | bytes 1376256 | tf_op jit(solution)/shard_map/all_to_all | solution.py:330
  146.9 9.5 %all-to-all-done.4.got_ref = f32[8,168,128]{2,1,0:T(8,128)S(1)} async-done(((f32[8,168,128]{2,1,0:T(8,128)}), f32[8,168,128]{2,1,0:T(8,128)S(1)}, u32[]{:S(2)}, u32[]{:S(2)}) %all-to-all-start.4) | async-done | bytes 688160 | tf_op jit(solution)/shard_map/all_to_all | solution.py:330
  (65 shorter events, 13.8 us)
Async XLA Ops:
  0.0 1.5 copy-start
  0.0 4.6 %copy-start.7 = (f32[1,64,64]{2,1,0:T(8,128)S(1)}, f32[1,64,64]{2,1,0:T(8,128)}, u32[]{:S(2)}) copy-start(f32[1,64,64]{2,1,0:T(8,128)} %param.7) | copy-start | bytes 49156
  6.3 17.9 %collective-permute-start = (f32[32,4096]{1,0:T(8,128)S(1)}, f32[32,4096]{1,0:T(8,128)S(1)}, u32[]{:S(2)}, u32[]{:S(2)}) collective-permute-start(f32[32,4096]{1,0:T(8,128)S(1)} %reshape.3003.refs_0_), channel_id=1, source_target_pairs={{0,4},{1,5},{2,6},{3,7},{4,8},{5,9},{6,10},{7,11},{8,12},{9,13},{1... | collective-permute-start | bytes 1572872 | tf_op jit(solution)/shard_map/ppermute | solution.py:33
  8.3 15.9 %collective-permute-start.1 = (f32[32,4096]{1,0:T(8,128)S(1)}, f32[32,4096]{1,0:T(8,128)S(1)}, u32[]{:S(2)}, u32[]{:S(2)}) collective-permute-start(f32[32,4096]{1,0:T(8,128)S(1)} %reshape.3003.refs_0_), channel_id=1, source_target_pairs={{0,28},{1,29},{2,30},{3,31},{4,0},{5,1},{6,2},{7,3},{8,4},{9,5},{1... | collective-permute-start | bytes 1572872 | tf_op jit(solution)/shard_map/ppermute | solution.py:37
  12.3 29.7 %collective-permute-start.4 = (f32[32,4096]{1,0:T(8,128)S(1)}, f32[32,4096]{1,0:T(8,128)S(1)}, u32[]{:S(2)}, u32[]{:S(2)}) collective-permute-start(f32[32,4096]{1,0:T(8,128)S(1)} %reshape.3003.refs_0_), channel_id=1, source_target_pairs={{0,2},{1,3},{2,0},{3,1},{4,6},{5,7},{6,4},{7,5},{8,10},{9,11},{10,... | collective-permute-start | bytes 1572872 | tf_op jit(solution)/shard_map/ppermute | solution.py:41
  24.1 17.9 %collective-permute-start.2 = (f32[32,4096]{1,0:T(8,128)S(1)}, f32[32,4096]{1,0:T(8,128)S(1)}, u32[]{:S(2)}, u32[]{:S(2)}) collective-permute-start(f32[32,4096]{1,0:T(8,128)S(1)} %collective-permute-done.refs_1_), channel_id=1, source_target_pairs={{0,4},{1,5},{2,6},{3,7},{4,8},{5,9},{6,10},{7,11},{8,12},{9,13},{1... | collective-permute-start | bytes 1572872 | tf_op jit(solution)/shard_map/ppermute | solution.py:33
  24.1 17.9 %collective-permute-start.3 = (f32[32,4096]{1,0:T(8,128)S(1)}, f32[32,4096]{1,0:T(8,128)S(1)}, u32[]{:S(2)}, u32[]{:S(2)}) collective-permute-start(f32[32,4096]{1,0:T(8,128)S(1)} %collective-permute-done.1.refs_2_), channel_id=1, source_target_pairs={{0,28},{1,29},{2,30},{3,31},{4,0},{5,1},{6,2},{7,3},{8,4},{9,5},{1... | collective-permute-start | bytes 1572872 | tf_op jit(solution)/shard_map/ppermute | solution.py:37
  27.4 14.7 %collective-permute-start.5 = (f32[32,4096]{1,0:T(8,128)S(1)}, f32[32,4096]{1,0:T(8,128)S(1)}, u32[]{:S(2)}, u32[]{:S(2)}) collective-permute-start(f32[32,4096]{1,0:T(8,128)S(1)} %collective-permute-done.1.refs_2_), channel_id=1, source_target_pairs={{0,2},{1,3},{2,0},{3,1},{4,6},{5,7},{6,4},{7,5},{8,10},{9,11},{10,... | collective-permute-start | bytes 1572872 | tf_op jit(solution)/shard_map/ppermute | solution.py:41
  42.2 4.9 %collective-permute-start.9 = (f32[128,4096]{1,0:T(8,128)S(1)}, f32[128,4096]{1,0:T(8,128)S(1)}, u32[]{:S(2)}, u32[]{:S(2)}) collective-permute-start(f32[128,4096]{1,0:T(8,128)S(1)} %shard_map.65.refs_1_), channel_id=1, source_target_pairs={{0,1},{1,0},{2,3},{3,2},{4,5},{5,4},{6,7},{7,6},{8,9},{9,8},{10,11... | collective-permute-start | bytes 6291464 | tf_op jit(solution)/shard_map/ppermute | solution.py:45
  42.3 15.8 %collective-permute-start.8 = (f32[32,4096]{1,0:T(8,128)S(1)}, f32[32,4096]{1,0:T(8,128)S(1)}, u32[]{:S(2)}, u32[]{:S(2)}) collective-permute-start(f32[32,4096]{1,0:T(8,128)S(1)} %collective-permute-done.refs_1_), channel_id=1, source_target_pairs={{0,2},{1,3},{2,0},{3,1},{4,6},{5,7},{6,4},{7,5},{8,10},{9,11},{10,... | collective-permute-start | bytes 1572872 | tf_op jit(solution)/shard_map/ppermute | solution.py:41
  43.9 15.2 %collective-permute-start.6 = (f32[32,4096]{1,0:T(8,128)S(1)}, f32[32,4096]{1,0:T(8,128)S(1)}, u32[]{:S(2)}, u32[]{:S(2)}) collective-permute-start(f32[32,4096]{1,0:T(8,128)S(1)} %collective-permute-done.2.refs_4_), channel_id=1, source_target_pairs={{0,4},{1,5},{2,6},{3,7},{4,8},{5,9},{6,10},{7,11},{8,12},{9,13},{1... | collective-permute-start | bytes 1572872 | tf_op jit(solution)/shard_map/ppermute | solution.py:33
  43.9 15.2 %collective-permute-start.7 = (f32[32,4096]{1,0:T(8,128)S(1)}, f32[32,4096]{1,0:T(8,128)S(1)}, u32[]{:S(2)}, u32[]{:S(2)}) collective-permute-start(f32[32,4096]{1,0:T(8,128)S(1)} %collective-permute-done.3.refs_5_), channel_id=1, source_target_pairs={{0,28},{1,29},{2,30},{3,31},{4,0},{5,1},{6,2},{7,3},{8,4},{9,5},{1... | collective-permute-start | bytes 1572872 | tf_op jit(solution)/shard_map/ppermute | solution.py:37
  59.1 1.4 copy-start.3
  59.1 7.5 %copy-start.5 = (f32[32,4096]{1,0:T(8,128)}, f32[32,4096]{1,0:T(8,128)S(1)}, u32[]{:S(2)}) copy-start(f32[32,4096]{1,0:T(8,128)S(1)} %collective-permute-done.7.refs_1_.refs_6_) | copy-start | bytes 1572868
  61.3 9.7 %collective-permute-start.13 = (f32[128,4096]{1,0:T(8,128)S(1)}, f32[128,4096]{1,0:T(8,128)}, u32[]{:S(2)}, u32[]{:S(2)}) collective-permute-start(f32[128,4096]{1,0:T(8,128)S(1)} %get-tuple-element.59.refs_0_), channel_id=1, source_target_pairs={{0,1},{1,0},{2,3},{3,2},{4,5},{5,4},{6,7},{7,6},{8,9},{9,8},{10,11... | collective-permute-start | bytes 6291464 | tf_op jit(solution)/shard_map/ppermute | solution.py:45
  61.3 20.9 %collective-permute-start.10 = (f32[32,4096]{1,0:T(8,128)}, f32[32,4096]{1,0:T(8,128)}, u32[]{:S(2)}, u32[]{:S(2)}) collective-permute-start(f32[32,4096]{1,0:T(8,128)} %get-tuple-element.56), channel_id=1, source_target_pairs={{0,4},{1,5},{2,6},{3,7},{4,8},{5,9},{6,10},{7,11},{8,12},{9,13},{1... | collective-permute-start | bytes 1572872 | tf_op jit(solution)/shard_map/ppermute | solution.py:33
  62.4 19.8 %collective-permute-start.11 = (f32[32,4096]{1,0:T(8,128)}, f32[32,4096]{1,0:T(8,128)}, u32[]{:S(2)}, u32[]{:S(2)}) collective-permute-start(f32[32,4096]{1,0:T(8,128)} %get-tuple-element.57), channel_id=1, source_target_pairs={{0,28},{1,29},{2,30},{3,31},{4,0},{5,1},{6,2},{7,3},{8,4},{9,5},{1... | collective-permute-start | bytes 1572872 | tf_op jit(solution)/shard_map/ppermute | solution.py:37
  64.5 17.7 %collective-permute-start.12 = (f32[32,4096]{1,0:T(8,128)}, f32[32,4096]{1,0:T(8,128)}, u32[]{:S(2)}, u32[]{:S(2)}) collective-permute-start(f32[32,4096]{1,0:T(8,128)} %get-tuple-element.58), channel_id=1, source_target_pairs={{0,2},{1,3},{2,0},{3,1},{4,6},{5,7},{6,4},{7,5},{8,10},{9,11},{10,... | collective-permute-start | bytes 1572872 | tf_op jit(solution)/shard_map/ppermute | solution.py:41
  66.5 15.6 %all-to-all-start = ((f32[4,168,256]{2,1,0:T(8,128)}), f32[4,168,256]{2,1,0:T(8,128)}, u32[]{:S(2)}, u32[]{:S(2)}) async-start(f32[4,168,256]{2,1,0:T(8,128)} %shard_map.66), calls=%async_computation | async-start | bytes 1376256 | tf_op jit(solution)/shard_map/all_to_all | solution.py:145
  82.2 1.0 copy-start.2
  83.2 1.0 copy-start.4
  87.9 8.2 %collective-permute-start.17 = (f32[160,4096]{1,0:T(8,128)S(1)}, f32[160,4096]{1,0:T(8,128)}, u32[]{:S(2)}, u32[]{:S(2)}) collective-permute-start(f32[160,4096]{1,0:T(8,128)S(1)} %get-tuple-element.64.refs_0_), channel_id=1, source_target_pairs={{0,1},{1,0},{2,3},{3,2},{4,5},{5,4},{6,7},{7,6},{8,9},{9,8},{10,11... | collective-permute-start | bytes 7864328 | tf_op jit(solution)/shard_map/ppermute | solution.py:45
  87.9 19.2 %collective-permute-start.14 = (f32[32,4096]{1,0:T(8,128)}, f32[32,4096]{1,0:T(8,128)}, u32[]{:S(2)}, u32[]{:S(2)}) collective-permute-start(f32[32,4096]{1,0:T(8,128)} %get-tuple-element.65), channel_id=1, source_target_pairs={{0,4},{1,5},{2,6},{3,7},{4,8},{5,9},{6,10},{7,11},{8,12},{9,13},{1... | collective-permute-start | bytes 1572872 | tf_op jit(solution)/shard_map/ppermute | solution.py:33
  87.9 19.2 %collective-permute-start.15 = (f32[32,4096]{1,0:T(8,128)}, f32[32,4096]{1,0:T(8,128)}, u32[]{:S(2)}, u32[]{:S(2)}) collective-permute-start(f32[32,4096]{1,0:T(8,128)} %get-tuple-element.66), channel_id=1, source_target_pairs={{0,28},{1,29},{2,30},{3,31},{4,0},{5,1},{6,2},{7,3},{8,4},{9,5},{1... | collective-permute-start | bytes 1572872 | tf_op jit(solution)/shard_map/ppermute | solution.py:37
  91.1 16.0 %collective-permute-start.16 = (f32[32,4096]{1,0:T(8,128)}, f32[32,4096]{1,0:T(8,128)}, u32[]{:S(2)}, u32[]{:S(2)}) collective-permute-start(f32[32,4096]{1,0:T(8,128)} %get-tuple-element.67), channel_id=1, source_target_pairs={{0,2},{1,3},{2,0},{3,1},{4,6},{5,7},{6,4},{7,5},{8,10},{9,11},{10,... | collective-permute-start | bytes 1572872 | tf_op jit(solution)/shard_map/ppermute | solution.py:41
  92.6 14.4 %all-to-all-start.1 = ((f32[4,160,256]{2,1,0:T(8,128)}), f32[4,160,256]{2,1,0:T(8,128)S(1)}, u32[]{:S(2)}, u32[]{:S(2)}) async-start(f32[4,160,256]{2,1,0:T(8,128)} %shard_map.68), calls=%async_computation.1 | async-start | bytes 1310720 | tf_op jit(solution)/shard_map/all_to_all | solution.py:145
  104.8 9.2 %copy-start.8 = (s32[32]{0:T(128)S(1)}, s32[32]{0:T(128)}, u32[]{:S(2)}) copy-start(s32[32]{0:T(128)} %param.10) | copy-start | bytes 388
  109.7 4.5 %collective-permute-start.18 = (f32[96,4096]{1,0:T(8,128)}, f32[96,4096]{1,0:T(8,128)}, u32[]{:S(2)}, u32[]{:S(2)}) collective-permute-start(f32[96,4096]{1,0:T(8,128)} %shard_map.71.refs_1_), channel_id=1, source_target_pairs={{0,1},{1,0},{2,3},{3,2},{4,5},{5,4},{6,7},{7,6},{8,9},{9,8},{10,11... | collective-permute-start | bytes 4718600 | tf_op jit(solution)/shard_map/ppermute | solution.py:45
  109.8 16.1 %all-to-all-start.2 = ((f32[4,160,256]{2,1,0:T(8,128)}), f32[4,160,256]{2,1,0:T(8,128)}, u32[]{:S(2)}, u32[]{:S(2)}) async-start(f32[4,160,256]{2,1,0:T(8,128)} %shard_map.70), calls=%async_computation.2 | async-start | bytes 1310720 | tf_op jit(solution)/shard_map/all_to_all | solution.py:145
  125.9 14.5 %all-to-all-start.3 = ((f32[4,160,256]{2,1,0:T(8,128)}), f32[4,160,256]{2,1,0:T(8,128)S(1)}, u32[]{:S(2)}, u32[]{:S(2)}) async-start(f32[4,160,256]{2,1,0:T(8,128)} %shard_map.72), calls=%async_computation.3 | async-start | bytes 1310720 | tf_op jit(solution)/shard_map/all_to_all | solution.py:145
  132.0 14.7 %copy-start.9 = (s32[32]{0:T(128)S(1)}, s32[32]{0:T(128)}, u32[]{:S(2)}) copy-start(s32[32]{0:T(128)} %param.11) | copy-start | bytes 388
  141.8 14.6 %all-to-all-start.4 = ((f32[8,168,128]{2,1,0:T(8,128)}), f32[8,168,128]{2,1,0:T(8,128)S(1)}, u32[]{:S(2)}, u32[]{:S(2)}) async-start(f32[8,168,128]{2,1,0:T(8,128)} %shard_map.74), calls=%async_computation.4 | async-start | bytes 1376256 | tf_op jit(solution)/shard_map/all_to_all | solution.py:330
  (2 other events, 1.8 us)
